TPU v7x, 32 devices: a whole 2x2x4 slice. The times are simulated.
32 devices in a mesh: seq: 8 (over z, y), mp: 4 (over x, core).
Axes of the slice: x: 2, y: 2, z: 4, core: 2. Of those that a mesh axis runs over, the one named last changes fastest.
Arguments:
- tokens: bfloat16 [3072, 4096], P('seq', 'mp'), may hold values from -6 to 6
- norm_gain: float32 [2, 4096], replicated, may hold values from 0.25 to 1.75
- in_weight: bfloat16 [2, 3, 4096, 4096], P(None, None, 'seq', 'mp'), may hold values from -0.09375 to 0.09375
- feat_filter: float32 [2, 3, 3, 4096], P(None, None, None, 'mp'), may hold values from -3 to 3
- short_filter: float32 [256, 7], P('mp'), may hold values from -3 to 3
- medium_filter: float32 [256, 128], P('mp'), may hold values from -0.4 to 0.4
- out_weight: bfloat16 [4096, 4096], P('seq', 'mp'), may hold values from -0.09375 to 0.09375
Outputs:
- stream: bfloat16 [3072, 4096], P('seq', 'mp')
- mixed: bfloat16 [3072, 4096], P('seq', 'mp')
All inputs are finite; a program needn't handle non-finite values.
Results may differ from a plain program's by a relative error of at most 0.015.
Values may be sent and summed in bfloat16 or wider, within the bound.
No kernel may reach another device: no remote copies, remote signals or barrier semaphores. Data moves between devices by JAX's collectives and lax.ppermute only.
A program may use at most 128 MiB of HBM per device.

v0:
```python
import jax
import jax.numpy as jnp
from jax import lax
from jax.sharding import PartitionSpec as P


def shifted(x, axis, by):
    peers = lax.axis_size(axis)
    pairs = [(i, i + by) for i in range(peers) if 0 <= i + by < peers]
    return lax.ppermute(x, axis, pairs)


def causal_taps(extended, taps, count):
    reach = taps.shape[0] - 1
    offset = extended.shape[0] - count - reach
    values = extended.astype(jnp.float32)
    total = jnp.zeros((count, extended.shape[1]), jnp.float32)
    for index in range(reach + 1):
        begin = offset + reach - index
        total = total + taps[index] * values[begin : begin + count]
    return total


def toeplitz_conv(kv_ext, filt, count):
    width = filt.shape[1]
    channels = kv_ext.shape[1]
    groups_here = filt.shape[0]
    per_group = channels // groups_here
    padded = jnp.concatenate([jnp.zeros((1, channels), kv_ext.dtype), kv_ext], axis=0)
    blocks = padded.astype(jnp.float32).reshape(count // width + 1, width, groups_here, per_group)
    lag = jnp.arange(width)[:, None] - jnp.arange(width)[None, :]
    current = jnp.where(lag >= 0, filt[:, jnp.clip(lag, 0, width - 1)], 0.0)
    earlier = jnp.where(lag < 0, filt[:, jnp.clip(lag + width, 0, width - 1)], 0.0)
    out = jnp.einsum("gik,bkgc->bigc", current, blocks[1:], precision=lax.Precision.HIGHEST)
    out = out + jnp.einsum("gik,bkgc->bigc", earlier, blocks[:-1], precision=lax.Precision.HIGHEST)
    return out.reshape(count, channels)


def normalized(stream_loc, gain):
    full = lax.all_gather(stream_loc, "mp", axis=1, tiled=True)
    values = full.astype(jnp.float32)
    mean_sq = jnp.mean(values * values, axis=-1, keepdims=True)
    return (values * lax.rsqrt(mean_sq + 1e-06) * gain).astype(jnp.bfloat16)


def project(normed, weights):
    return jnp.einsum(
        "rd,cdf->crf",
        normed,
        lax.all_gather(weights, "seq", axis=1, tiled=True),
        preferred_element_type=jnp.float32,
    ).astype(jnp.bfloat16)


def gated_mix(proj, feat_taps, inner_fn, span):
    rows = proj.shape[1]
    reach = feat_taps.shape[1] - 1
    rim = shifted(proj[:, rows - reach :, :], "seq", 1)
    extended = jnp.concatenate([rim, proj], axis=1)
    query = causal_taps(extended[0], feat_taps[0], rows)
    key_part = causal_taps(extended[1], feat_taps[1], rows)
    value_part = causal_taps(extended[2], feat_taps[2], rows)
    kv_prod = (key_part * value_part).astype(jnp.bfloat16)
    earlier = shifted(kv_prod[rows - span :], "seq", 1)
    kv_ext = jnp.concatenate([earlier, kv_prod], axis=0)
    inner = inner_fn(kv_ext, rows)
    return (query * inner).astype(jnp.bfloat16)


def local(tokens, norm_gain, in_weight, feat_filter, short_filter, medium_filter, out_weight):
    per_group = tokens.shape[1] // short_filter.shape[0]
    short_taps = jnp.repeat(short_filter.T, per_group, axis=1)

    def short_inner(kv_ext, count):
        return causal_taps(kv_ext, short_taps, count)

    def medium_inner(kv_ext, count):
        return toeplitz_conv(kv_ext, medium_filter, count)

    normed = normalized(tokens, norm_gain[0])
    proj = project(normed, in_weight[0])
    first = gated_mix(proj, feat_filter[0], short_inner, short_filter.shape[1] - 1)
    first_full = lax.all_gather(first, "mp", axis=1, tiled=True)
    delta = jnp.dot(
        first_full,
        lax.all_gather(out_weight, "seq", axis=0, tiled=True),
        preferred_element_type=jnp.float32,
    )
    stream = (tokens.astype(jnp.float32) + delta).astype(jnp.bfloat16)
    normed_next = normalized(stream, norm_gain[1])
    proj_next = project(normed_next, in_weight[1])
    mixed = gated_mix(proj_next, feat_filter[1], medium_inner, medium_filter.shape[1] - 1)
    return (stream, mixed)


def solution(mesh):
    placed = (
        P("seq", "mp"),
        P(),
        P(None, None, "seq", "mp"),
        P(None, None, None, "mp"),
        P("mp", None),
        P("mp", None),
        P("seq", "mp"),
    )
    return jax.shard_map(
        local,
        mesh=mesh,
        in_specs=placed,
        out_specs=(P("seq", "mp"), P("seq", "mp")),
        check_vma=False,
    )
```

profile of v0, /device:TPU:0, one launch (start us, length us, event | category | flops | bytes accessed | tf_op | source)
XLA Modules:
  0.0 1372.1 jit_solution(6332828895257846258)
XLA Ops:
  7.9 6.8 fusion.102
  15.6 25.2 %all-gather.9.cloned.1.call-done = bf16[384,4096]{1,0:T(8,128)(2,1)} async-done(((bf16[384,1024]{1,0:T(8,128)(2,1)}), bf16[384,4096]{1,0:T(8,128)(2,1)}) %all-gather.9.cloned.1.call-update) | async-done | bytes 3145744 | tf_op jit(solution)/shard_map/all_gather | solution.py:40
  40.8 2.7 fusion.4
  43.6 479.3 %all-gather.17.cloned.1.call-done = bf16[1,3,4096,1024]{3,2,1,0:T(8,128)(2,1)} async-done(((bf16[1,3,512,1024]{3,2,1,0:T(8,128)(2,1)}), bf16[1,3,4096,1024]{3,2,1,0:T(8,128)(2,1)}) %all-gather.17.cloned.1.call-update) | async-done | bytes 25165840 | tf_op jit(solution)/shard_map/all_gather | solution.py:50
  522.8 14.7 %convert_bitcast_fusion.1 = bf16[3,384,1024]{2,1,0:T(8,128)(2,1)S(1)} fusion(bf16[1,3,4096,1024]{3,2,1,0:T(8,128)(2,1)} %all-gather.17.cloned.1.call-done, bf16[384,4096]{1,0:T(8,128)(2,1)S(1)} %copy-done.2, f32[4096]{0:T(1024)S(1)} %bitcast.263, f32[384]{0:T(512)S(1)} %add_rsqrt_fusion.1), kind=kOutput, calls=%fused_computation.33 | convolution fusion | flops 9671147520 | bytes 30688768 | tf_op jit(solution)/shard_map/rd,cdf->crf/dot_general | solution.py:47
  537.6 1.7 collective-permute-start
  542.4 5.0 collective-permute-start.1
  549.0 2.6 fusion.57
  551.7 98.8 %all-gather.13.cloned.1.call-done = bf16[4096,1024]{1,0:T(8,128)(2,1)} async-done(((bf16[512,1024]{1,0:T(8,128)(2,1)}), bf16[4096,1024]{1,0:T(8,128)(2,1)}) %all-gather.13.cloned.1.call-update) | async-done | bytes 8388624 | tf_op jit(solution)/shard_map/all_gather | solution.py:86
  650.5 28.7 %all-gather.11.cloned.1.call-done = bf16[384,4096]{1,0:T(8,128)(2,1)} async-done(((bf16[384,1024]{1,0:T(8,128)(2,1)}), bf16[384,4096]{1,0:T(8,128)(2,1)}) %all-gather.11.cloned.1.call-update) | async-done | bytes 3145744 | tf_op jit(solution)/shard_map/all_gather | solution.py:83
  679.2 8.6 add_convert_fusion
  688.5 28.1 %all-gather.15.cloned.1.call-done = bf16[384,4096]{1,0:T(8,128)(2,1)} async-done(((bf16[384,1024]{1,0:T(8,128)(2,1)}), bf16[384,4096]{1,0:T(8,128)(2,1)}) %all-gather.15.cloned.1.call-update) | async-done | bytes 3145744 | tf_op jit(solution)/shard_map/all_gather | solution.py:40
  716.6 2.7 fusion.7
  719.3 479.1 %all-gather.19.cloned.1.call-done = bf16[1,3,4096,1024]{3,2,1,0:T(8,128)(2,1)} async-done(((bf16[1,3,512,1024]{3,2,1,0:T(8,128)(2,1)}), bf16[1,3,4096,1024]{3,2,1,0:T(8,128)(2,1)}) %all-gather.19.cloned.1.call-update) | async-done | bytes 25165840 | tf_op jit(solution)/shard_map/all_gather | solution.py:50
  1198.5 14.0 %convert_bitcast_fusion = bf16[3,384,1024]{2,1,0:T(8,128)(2,1)S(1)} fusion(bf16[1,3,4096,1024]{3,2,1,0:T(8,128)(2,1)} %all-gather.19.cloned.1.call-done, bf16[384,4096]{1,0:T(8,128)(2,1)S(1)} %copy-done.3, f32[4096]{0:T(1024)S(1)} %bitcast.262, f32[384]{0:T(512)S(1)} %add_rsqrt_fusion), kind=kOutput, calls=%fused_computation.32 | convolution fusion | flops 9671147520 | bytes 30688768 | tf_op jit(solution)/shard_map/rd,cdf->crf/dot_general | solution.py:47
  1212.5 2.3 collective-permute-start.2
  1218.5 4.5 collective-permute-start.3
  1223.2 54.4 %gather_fusion.1 = f32[16384,64]{1,0:T(8,128)} fusion(f32[64,128]{0,1:T(8,128)S(1)} %copy.17, s32[16384]{0:T(1024)S(1)} %fusion.97), kind=kCustom, calls=%fused_computation.1 | custom fusion | bytes 8454144 | tf_op jit(solution)/shard_map/gather | solution.py:33
  1277.6 7.3 copy.22
  1284.9 54.4 %gather_fusion = f32[16384,64]{1,0:T(8,128)} fusion(f32[64,128]{0,1:T(8,128)S(1)} %copy.17, s32[16384]{0:T(1024)S(1)} %fusion.95), kind=kCustom, calls=%fused_computation | custom fusion | bytes 8454144 | tf_op jit(solution)/shard_map/gather | solution.py:32
  1339.3 7.3 copy.18
  1351.0 5.2 fusion.10
  1356.3 3.4 add_bitcast_fusion
  1362.4 2.8 fusion.51
  (76 shorter events, 17.8 us)
Async XLA Ops:
  7.2 33.7 %all-gather.9.cloned.1.call-start = ((), (), s32[]{:S(2)}) async-start(), calls=%async_computation | async-start | bytes 3932160 | tf_op jit(solution)/shard_map/all_gather | solution.py:40
  7.9 514.9 %all-gather.17.cloned.1.call-start = ((), (), s32[]{:S(2)}) async-start(), calls=%async_computation.4 | async-start | bytes 28311552 | tf_op jit(solution)/shard_map/all_gather | solution.py:50
  14.8 0.8 copy-start.7
  14.8 635.7 %all-gather.13.cloned.1.call-start = ((), (), s32[]{:S(2)}) async-start(), calls=%async_computation.2 | async-start | bytes 9437184 | tf_op jit(solution)/shard_map/all_gather | solution.py:86
  15.5 663.7 %all-gather.11.cloned.1.call-start = ((), (), s32[]{:S(2)}) async-start(), calls=%async_computation.1 | async-start | bytes 3932160 | tf_op jit(solution)/shard_map/all_gather | solution.py:83
  40.8 482.0 %copy-start.2 = (bf16[384,4096]{1,0:T(8,128)(2,1)S(1)}, bf16[384,4096]{1,0:T(8,128)(2,1)}, u32[]{:S(2)}) copy-start(bf16[384,4096]{1,0:T(8,128)(2,1)} %all-gather.9.cloned.1.call-done) | copy-start | bytes 9437188
  522.8 16.5 %copy-start.5 = (f32[2,3,3,1024]{3,0,2,1:T(2,128)S(1)}, f32[2,3,3,1024]{3,0,2,1:T(2,128)}, u32[]{:S(2)}) copy-start(f32[2,3,3,1024]{3,0,2,1:T(2,128)} %param.10) | copy-start | bytes 221188
  537.6 3.1 collective-permute-start
  541.3 6.0 copy-start.8
  542.4 6.4 collective-permute-start.1
  549.0 130.3 %copy-start.4 = (bf16[384,1024]{1,0:T(8,128)(2,1)S(1)}, bf16[384,1024]{1,0:T(8,128)(2,1)}, u32[]{:S(2)}) copy-start(bf16[384,1024]{1,0:T(8,128)(2,1)} %param.7) | copy-start | bytes 2359300
  551.6 164.9 %all-gather.15.cloned.1.call-start = ((), (), s32[]{:S(2)}) async-start(), calls=%async_computation.3 | async-start | bytes 3932160 | tf_op jit(solution)/shard_map/all_gather | solution.py:40
  687.9 510.6 %all-gather.19.cloned.1.call-start = ((), (), s32[]{:S(2)}) async-start(), calls=%async_computation.5 | async-start | bytes 28311552 | tf_op jit(solution)/shard_map/all_gather | solution.py:50
  716.6 481.9 %copy-start.3 = (bf16[384,4096]{1,0:T(8,128)(2,1)S(1)}, bf16[384,4096]{1,0:T(8,128)(2,1)}, u32[]{:S(2)}) copy-start(bf16[384,4096]{1,0:T(8,128)(2,1)} %all-gather.15.cloned.1.call-done) | copy-start | bytes 9437188
  1212.5 3.6 collective-permute-start.2
  1216.7 6.3 copy-start.6
  1218.5 129.6 %collective-permute-start.3 = (bf16[127,1024]{1,0:T(8,128)(2,1)}, bf16[127,1024]{1,0:T(8,128)(2,1)S(1)}, u32[]{:S(2)}, u32[]{:S(2)}) collective-permute-start(bf16[127,1024]{1,0:T(8,128)(2,1)} %slice.472), channel_id=1, source_target_pairs={{0,4},{4,8},{8,12},{12,16},{16,20},{20,24},{24,28},{1,5},{5,9},{9,... | collective-permute-start | bytes 780296 | tf_op jit(solution)/shard_map/ppermute | solution.py:10
  1351.0 5.3 copy-start
  1351.0 5.3 copy-start.1
Sparse Core Ops, SparseCore 0:
  9.6 31.2 all-gather.8
  42.4 480.4 all-gather.16
  525.0 125.4 all-gather.12
  652.5 26.6 all-gather.10
  688.0 28.5 all-gather.14
  718.0 480.4 all-gather.18
where the time goes:
time: 1370 us
  waiting for transfers between devices  1140 us (83%)
  local copies, waits for them, and re-layouts  138 us (10%)
  matrix products  46 us (3%)
  other arithmetic  15.5 us (1%)
  between operations  14.4 us (1%)
  starting transfers between devices  13.8 us (1%)
    all_gather x2, waiting for transfers between devices, project(): lax.all_gather(weights, 'seq', axis=1, tiled=True)  958 us
    all_gather x1, waiting for transfers between devices, local(): lax.all_gather(out_weight, 'seq', axis=0, tiled=True)  98.8 us
    gather x2, local copies, waits for them, and re-layouts, toeplitz_conv(): filt[:, jnp.clip(lag + width, 0, width - 1)]  61.7 us
    gather x2, local copies, waits for them, and re-layouts, toeplitz_conv(): current = jnp.where(lag >= 0, filt[:, jnp.clip(lag, 0, width - 1)], 0.0)  61.7 us
    all_gather x2, waiting for transfers between devices, normalized(): full = lax.all_gather(stream_loc, 'mp', axis=1, tiled=True)  53.3 us
    dot_general x2, matrix products, project(): jnp.einsum('rd,cdf->crf', normed, lax.all_gather(weights, 'seq', axis=1,...  28.8 us
    all_gather x1, waiting for transfers between devices, local(): first_full = lax.all_gather(first, 'mp', axis=1, tiled=True)  28.7 us
  transfers between devices with their start and end apart: 10, of which 9 were waited for; matrix products, arithmetic and copies ran while one was open for 12% of the time, Pallas kernels for 0%

commit v1 on v0

v1 whole, which is shorter than its diff:
```python
import functools

import jax
import jax.numpy as jnp
from jax import lax
from jax.experimental import pallas as pl
from jax.experimental.pallas import tpu as pltpu
from jax.sharding import Mesh, PartitionSpec as P

AXES = ("z", "y", "x", "c")


def factors(mesh):
    seq, mp = mesh.shape["seq"], mesh.shape["mp"]
    along_y = 1
    while 2 * along_y * along_y < seq:
        along_y *= 2
    return seq // along_y, along_y, mp // 2, 2


def rotate(value, axis, by):
    size = lax.axis_size(axis)
    return lax.ppermute(value, axis, [(i, (i + by) % size) for i in range(size)])


def split_kernel(place, *refs):
    del place
    gain = refs[0][...]
    half = (len(refs) - 1) // 2
    for source, target in zip(refs[1 : 1 + half], refs[1 + half :]):
        target[...] = (source[0, 0].astype(jnp.float32) * gain).astype(jnp.bfloat16)


def split_weights(in_weight, block, gain, z_at):
    parts = lax.axis_size("z")
    rows, columns = in_weight.shape[2], in_weight.shape[3] // parts
    if columns % 128:
        pieces = []
        for k in range(parts):
            begin = lax.rem(z_at + k, parts) * columns
            piece = lax.dynamic_slice_in_dim(in_weight[block], begin, columns, 2)
            piece = (piece.astype(jnp.float32) * gain).astype(jnp.bfloat16)
            pieces.append(piece.transpose(1, 0, 2).reshape(rows, 3 * columns))
        return pieces

    def source(k):
        return pl.BlockSpec((1, 1, rows, columns), lambda c, at: (block, c, 0, lax.rem(at[0] + k, parts)))

    return pl.pallas_call(
        split_kernel,
        grid_spec=pltpu.PrefetchScalarGridSpec(
            num_scalar_prefetch=1,
            grid=(3,),
            in_specs=[pl.BlockSpec((rows, 1), lambda c, at: (0, 0))] + [source(k) for k in range(parts)],
            out_specs=[pl.BlockSpec((rows, columns), lambda c, at: (0, c)) for _ in range(parts)],
        ),
        out_shape=[jax.ShapeDtypeStruct((rows, 3 * columns), jnp.bfloat16)] * parts,
    )(z_at[None], gain, *[in_weight] * parts)


def slot_of(z_from, x_at, c_at):
    x_size, c_size = lax.axis_size("x"), lax.axis_size("c")
    x_from, c_from = z_from // c_size, z_from % c_size
    return ((x_at - x_from) % x_size) * c_size + (c_at - c_from) % c_size


def over_y(pieces, where):
    z_at, y_at, x_at, c_at = where
    parts, y_size = lax.axis_size("z"), lax.axis_size("y")
    rows, columns = pieces[0].shape
    whole = jnp.zeros((parts, y_size, rows, columns), pieces[0].dtype)
    for k, piece in enumerate(pieces):
        slot = slot_of((z_at - k) % parts, x_at, c_at)
        for j in range(y_size):
            moved = rotate(piece, "y", j) if j else piece
            whole = lax.dynamic_update_slice(whole, moved[None, None], (slot, (y_at - j) % y_size, 0, 0))
    return whole.reshape(parts * y_size * rows, columns)


def all_features(piece):
    found = [piece] + [rotate(piece, "x", d) for d in range(1, lax.axis_size("x"))]
    return [rotate(p, "c", d) if d else p for p in found for d in range(lax.axis_size("c"))]


def ring(value):
    out = [value]
    for _ in range(lax.axis_size("z") - 1):
        out.append(rotate(out[-1], "z", 1))
    return out


def project(pieces, weights):
    out = []
    for piece in pieces:
        full = jnp.concatenate(all_features(piece), axis=1)
        values = full.astype(jnp.float32)
        scale = lax.rsqrt(jnp.mean(values * values, axis=-1, keepdims=True) + 1e-06)
        out.append((jnp.dot(full, weights, preferred_element_type=jnp.float32) * scale).astype(jnp.bfloat16))
    return out


def earlier_rows(pieces, count, z_at, y_at):
    parts, y_size = len(pieces), lax.axis_size("y")
    tails = [rotate(p[p.shape[0] - count :], "y", 1) for p in pieces]
    out = []
    for k in range(parts):
        wrapped = jnp.where(z_at == k, jnp.zeros_like(tails[k]), tails[(k + 1) % parts])
        out.append(jnp.where(y_at == 0, wrapped, tails[k]))
    return out


def causal(extended, taps, count):
    reach = taps.shape[0] - 1
    offset = extended.shape[0] - count - reach
    total = 0.0
    for index in range(reach + 1):
        begin = offset + reach - index
        total = total + taps[index] * extended[begin : begin + count]
    return total


def toeplitz_kernel(row_ref, out_ref):
    width = out_ref.shape[1]
    rows = jnp.broadcast_to(row_ref[0], (width, 3 * width))
    turned = pltpu.roll(rows, 0, 1, stride=1, stride_axis=0)
    out_ref[0] = turned[:, : 2 * width].astype(out_ref.dtype)


def toeplitz(filt):
    groups, width = filt.shape
    row = jnp.zeros((groups, 1, 3 * width), jnp.float32).at[:, 0, 1 : width + 1].set(filt[:, ::-1])
    return pl.pallas_call(
        toeplitz_kernel,
        grid=(groups,),
        in_specs=[pl.BlockSpec((1, 1, 3 * width), lambda g: (g, 0, 0))],
        out_specs=pl.BlockSpec((1, width, 2 * width), lambda g: (g, 0, 0)),
        out_shape=jax.ShapeDtypeStruct((groups, width, 2 * width), jnp.bfloat16),
    )(row)


def medium(extended, matrix):
    groups, width = matrix.shape[0], matrix.shape[1]
    blocks = extended.reshape(extended.shape[0] // width, width, groups, -1)
    pairs = jnp.concatenate([blocks[:-1], blocks[1:]], axis=1)
    out = jnp.einsum("gik,bkgc->bigc", matrix, pairs, preferred_element_type=jnp.float32)
    return out.reshape(out.shape[0] * width, -1)


def channels_of(value, z_at, axis):
    size = value.shape[axis] // lax.axis_size("z")
    return lax.dynamic_slice_in_dim(value, z_at * size, size, axis)


def home(pieces, z_at):
    parts = len(pieces)
    back = jnp.stack([rotate(p, "z", -k) if k else p for k, p in enumerate(pieces)])
    ordered = [lax.dynamic_index_in_dim(back, (j - z_at) % parts, 0, keepdims=False) for j in range(parts)]
    return jnp.concatenate(ordered, axis=1)


def local(tokens, norm_gain, in_weight, feat_filter, short_filter, medium_filter, out_weight):
    where = tuple(lax.axis_index(a) for a in AXES)
    z_at, y_at, x_at, c_at = where
    parts = lax.axis_size("z")
    rows = in_weight.shape[2]
    count = tokens.shape[0]
    width = in_weight.shape[3] // parts
    begin = (z_at * lax.axis_size("y") + y_at) * rows
    gains = lax.dynamic_slice_in_dim(norm_gain, begin, rows, 1)[:, :, None]
    feat = channels_of(feat_filter, z_at, 3)
    short = channels_of(short_filter, z_at, 0)
    short_taps = jnp.repeat(short.T, width // short.shape[0], axis=1)
    matrix = toeplitz(channels_of(medium_filter, z_at, 0))
    span = medium_filter.shape[1]
    reach = feat.shape[2] - 1

    def weights_of(block):
        pieces = split_weights(in_weight, block, gains[block], z_at)
        return over_y([rotate(p, "z", k) if k else p for k, p in enumerate(pieces)], where)

    def third(value, c):
        return value[:, c * width : (c + 1) * width].astype(jnp.float32)

    weights = weights_of(0)
    out_rows = over_y(ring(out_weight), where)
    weights_next = weights_of(1)

    proj = project(ring(tokens), weights)
    gated = []
    for piece, before in zip(proj, earlier_rows(proj, 8, z_at, y_at)):
        extended = jnp.concatenate([before, piece], axis=0)
        more = count + short_taps.shape[0] - 1
        query = causal(third(extended, 0), feat[0, 0], count)
        kv = causal(third(extended, 1), feat[0, 1], more) * causal(third(extended, 2), feat[0, 2], more)
        kv = kv.astype(jnp.bfloat16).astype(jnp.float32)
        gated.append((query * causal(kv, short_taps, count)).astype(jnp.bfloat16))
    first = jnp.concatenate(all_features(home(gated, z_at)), axis=1)
    delta = jnp.dot(first, out_rows, preferred_element_type=jnp.float32)
    stream = (tokens.astype(jnp.float32) + delta).astype(jnp.bfloat16)

    proj = project(ring(stream), weights_next)
    queries, kvs = [], []
    for piece, before in zip(proj, earlier_rows(proj, 8, z_at, y_at)):
        extended = jnp.concatenate([before, piece], axis=0)
        queries.append(causal(third(extended, 0), feat[1, 0], count))
        kv = causal(third(extended, 1), feat[1, 1], count) * causal(third(extended, 2), feat[1, 2], count)
        kvs.append(kv.astype(jnp.bfloat16))
    gated = []
    for query, kv, before in zip(queries, kvs, earlier_rows(kvs, span, z_at, y_at)):
        inner = medium(jnp.concatenate([before, kv], axis=0), matrix)
        gated.append((query * inner).astype(jnp.bfloat16))
    return stream, home(gated, z_at)


def solution(mesh):
    wide = Mesh(mesh.devices.reshape(factors(mesh)), AXES)
    seq, mp = ("z", "y"), ("x", "c")
    placed = (
        P(seq, mp),
        P(),
        P(None, None, seq, mp),
        P(None, None, None, mp),
        P(mp, None),
        P(mp, None),
        P(seq, mp),
    )
    return jax.shard_map(
        local,
        mesh=wide,
        in_specs=placed,
        out_specs=(P(seq, mp), P(seq, mp)),
        check_vma=False,
    )
```

time: 1370 us -> 553 us (0.40)
  waiting for transfers between devices: 1140 us -> 256 us
  starting transfers between devices: 13.8 us -> 135 us
  local copies, waits for them, and re-layouts: 138 us -> 70.7 us
  Pallas kernels: 0 us -> 18.1 us
    all_gather x6 -> x0, waiting for transfers between devices: 1140 us -> none  [the longest x2 958 us: project(): lax.all_gather(weights, 'seq', axis=1, tiled=True)]
    ppermute x4 -> x72, waiting for transfers between devices: 3.02 us -> 256 us  [rotate(): lax.ppermute(value, axis, [(i, (i + by) % size) for i in range(size)])]
    gather x4 -> x0, local copies, waits for them, and re-layouts: 123 us -> none  [the longest x2 61.7 us: toeplitz_conv(): filt[:, jnp.clip(lag + width, 0, width - 1)]]
    ppermute x4 -> x72, starting transfers between devices: 13.4 us -> 135 us  [rotate(): lax.ppermute(value, axis, [(i, (i + by) % size) for i in range(size)])]
    dynamic_update_slice x0 -> x24, local copies, waits for them, and re-layouts: none -> 18.9 us  [over_y(): lax.dynamic_update_slice(whole, moved[None, None], (slot, (y_at - j) % y_...]
    pallas_call x0 -> x3, Pallas kernels: none -> 18.1 us  [the longest x2 9.72 us: split_weights(): pl.pallas_call(split_kernel, grid_spec=pltpu.PrefetchScalarGridSpec(num_s...]
    dot_general x5 -> x13, matrix products: 46 us -> 43 us  [the longest x8 32.3 us: project(): jnp.dot(full, weights, preferred_element_type=jnp.float32) * scale]
  transfers between devices with their start and end apart: 10 -> 72, of which waited for: 9 -> 22; matrix products, arithmetic and copies ran while one was open for 12% -> 20% of each run, Pallas kernels for 0% -> 3%
where the time goes in v1:
time: 553 us; the launch traced here: 545 us
  waiting for transfers between devices  256 us (46%)
  starting transfers between devices  135 us (24%)
  local copies, waits for them, and re-layouts  70.7 us (13%)
  matrix products  43 us (8%)
  other arithmetic  18.9 us (3%)
  Pallas kernels  18.1 us (3%)
    ppermute x72, waiting for transfers between devices, rotate(): lax.ppermute(value, axis, [(i, (i + by) % size) for i in range(size)])  256 us
    ppermute x72, starting transfers between devices, rotate(): lax.ppermute(value, axis, [(i, (i + by) % size) for i in range(size)])  135 us
    dot_general x8, matrix products, project(): jnp.dot(full, weights, preferred_element_type=jnp.float32) * scale  32.3 us
    dynamic_update_slice x24, local copies, waits for them, and re-layouts, over_y(): lax.dynamic_update_slice(whole, moved[None, None], (slot, (y_at - j) % y_...  18.9 us
    slice x20, local copies, waits for them, and re-layouts, medium(): pairs = jnp.concatenate([blocks[:-1], blocks[1:]], axis=1)  18.5 us
  transfers between devices with their start and end apart: 72, of which 22 were waited for; matrix products, arithmetic and copies ran while one was open for 20% of the time, Pallas kernels for 3%

profile of v1, /device:TPU:0, one launch (start us, length us, event | category | flops | bytes accessed | tf_op | source)
XLA Modules:
  0.0 544.7 jit_solution(3301196371929527184)
XLA Ops:
  41.4 7.9 %collective-permute-done.43 = bf16[512,768]{1,0:T(8,128)(2,1)} collective-permute-done((bf16[512,768]{1,0:T(8,128)(2,1)}, bf16[512,768]{1,0:T(8,128)(2,1)}, u32[]{:S(2)}, u32[]{:S(2)}) %collective-permute-start.43) | collective-permute-done | bytes 786464 | tf_op jit(solution)/shard_map/ppermute | solution.py:23
  50.5 6.6 %collective-permute-done.5 = bf16[512,768]{1,0:T(8,128)(2,1)S(1)} collective-permute-done((bf16[512,768]{1,0:T(8,128)(2,1)S(1)}, bf16[512,768]{1,0:T(8,128)(2,1)S(1)}, u32[]{:S(2)}, u32[]{:S(2)}) %collective-permute-start.5) | collective-permute-done | bytes 786464 | tf_op jit(solution)/shard_map/ppermute | solution.py:23
  58.4 12.5 %collective-permute-done.32 = bf16[512,1024]{1,0:T(8,128)(2,1)S(1)} collective-permute-done((bf16[512,1024]{1,0:T(8,128)(2,1)S(1)}, bf16[512,1024]{1,0:T(8,128)(2,1)S(1)}, u32[]{:S(2)}, u32[]{:S(2)}) %collective-permute-start.32) | collective-permute-done | bytes 1048608 | tf_op jit(solution)/shard_map/ppermute | solution.py:23
  73.5 38.1 %collective-permute-done.7 = bf16[512,768]{1,0:T(8,128)(2,1)S(1)} collective-permute-done((bf16[512,768]{1,0:T(8,128)(2,1)S(1)}, bf16[512,768]{1,0:T(8,128)(2,1)S(1)}, u32[]{:S(2)}, u32[]{:S(2)}) %collective-permute-start.7) | collective-permute-done | bytes 786464 | tf_op jit(solution)/shard_map/ppermute | solution.py:23
  113.9 15.6 %collective-permute-start.16 = (bf16[384,1024]{1,0:T(8,128)(2,1)S(1)}, bf16[384,1024]{1,0:T(8,128)(2,1)S(1)}, u32[]{:S(2)}, u32[]{:S(2)}) collective-permute-start(bf16[384,1024]{1,0:T(8,128)(2,1)S(1)} %collective-permute-done), channel_id=1, source_target_pairs={{0,8},{8,16},{16,24},{24,0},{1,9},{9,17},{17,25},{25,1},{2,10},{10... | collective-permute-start | bytes 2359304 | tf_op jit(solution)/shard_map/ppermute | solution.py:23
  132.6 15.6 %collective-permute-start.35 = (bf16[512,1024]{1,0:T(8,128)(2,1)S(1)}, bf16[512,1024]{1,0:T(8,128)(2,1)S(1)}, u32[]{:S(2)}, u32[]{:S(2)}) collective-permute-start(bf16[512,1024]{1,0:T(8,128)(2,1)S(1)} %collective-permute-done.33), channel_id=1, source_target_pairs={{0,8},{8,16},{16,24},{24,0},{1,9},{9,17},{17,25},{25,1},{2,10},{10... | collective-permute-start | bytes 3145736 | tf_op jit(solution)/shard_map/ppermute | solution.py:23
  157.5 12.9 %collective-permute-start.22 = (bf16[384,1024]{1,0:T(8,128)(2,1)S(1)}, bf16[384,1024]{1,0:T(8,128)(2,1)S(1)}, u32[]{:S(2)}, u32[]{:S(2)}) collective-permute-start(bf16[384,1024]{1,0:T(8,128)(2,1)S(1)} %collective-permute-done.16), channel_id=1, source_target_pairs={{0,8},{8,16},{16,24},{24,0},{1,9},{9,17},{17,25},{25,1},{2,10},{10... | collective-permute-start | bytes 2359304 | tf_op jit(solution)/shard_map/ppermute | solution.py:23
  173.1 13.8 %collective-permute-done.18 = bf16[384,1024]{1,0:T(8,128)(2,1)S(1)} collective-permute-done((bf16[384,1024]{1,0:T(8,128)(2,1)S(1)}, bf16[384,1024]{1,0:T(8,128)(2,1)S(1)}, u32[]{:S(2)}, u32[]{:S(2)}) %collective-permute-start.18) | collective-permute-done | bytes 786464 | tf_op jit(solution)/shard_map/ppermute | solution.py:23
  195.8 16.9 %collective-permute-done.24 = bf16[384,1024]{1,0:T(8,128)(2,1)S(1)} collective-permute-done((bf16[384,1024]{1,0:T(8,128)(2,1)S(1)}, bf16[384,1024]{1,0:T(8,128)(2,1)S(1)}, u32[]{:S(2)}, u32[]{:S(2)}) %collective-permute-start.24) | collective-permute-done | bytes 786464 | tf_op jit(solution)/shard_map/ppermute | solution.py:23
  239.9 17.6 %collective-permute-done.37 = bf16[512,1024]{1,0:T(8,128)(2,1)S(1)} collective-permute-done((bf16[512,1024]{1,0:T(8,128)(2,1)S(1)}, bf16[512,1024]{1,0:T(8,128)(2,1)S(1)}, u32[]{:S(2)}, u32[]{:S(2)}) %collective-permute-start.37) | collective-permute-done | bytes 1048608 | tf_op jit(solution)/shard_map/ppermute | solution.py:23
  261.7 9.8 %collective-permute-start.46 = (bf16[512,768]{1,0:T(8,128)(2,1)S(1)}, bf16[512,768]{1,0:T(8,128)(2,1)S(1)}, u32[]{:S(2)}, u32[]{:S(2)}) collective-permute-start(bf16[512,768]{1,0:T(8,128)(2,1)S(1)} %copy-done.14), channel_id=1, source_target_pairs={{0,16},{8,24},{16,0},{24,8},{1,17},{9,25},{17,1},{25,9},{2,18},{10... | collective-permute-start | bytes 2359304 | tf_op jit(solution)/shard_map/ppermute | solution.py:23
  276.9 10.1 %collective-permute-done.44 = bf16[512,768]{1,0:T(8,128)(2,1)S(1)} collective-permute-done((bf16[512,768]{1,0:T(8,128)(2,1)S(1)}, bf16[512,768]{1,0:T(8,128)(2,1)S(1)}, u32[]{:S(2)}, u32[]{:S(2)}) %collective-permute-start.44) | collective-permute-done | bytes 786464 | tf_op jit(solution)/shard_map/ppermute | solution.py:23
  288.0 9.5 %collective-permute-done.36 = bf16[512,1024]{1,0:T(8,128)(2,1)S(1)} collective-permute-done((bf16[512,1024]{1,0:T(8,128)(2,1)S(1)}, bf16[512,1024]{1,0:T(8,128)(2,1)S(1)}, u32[]{:S(2)}, u32[]{:S(2)}) %collective-permute-start.36) | collective-permute-done | bytes 1048608 | tf_op jit(solution)/shard_map/ppermute | solution.py:23
  300.2 23.1 %collective-permute-done.46 = bf16[512,768]{1,0:T(8,128)(2,1)S(1)} collective-permute-done((bf16[512,768]{1,0:T(8,128)(2,1)S(1)}, bf16[512,768]{1,0:T(8,128)(2,1)S(1)}, u32[]{:S(2)}, u32[]{:S(2)}) %collective-permute-start.46) | collective-permute-done | bytes 786464 | tf_op jit(solution)/shard_map/ppermute | solution.py:23
  323.8 16.3 %collective-permute-done.48 = bf16[512,768]{1,0:T(8,128)(2,1)S(1)} collective-permute-done((bf16[512,768]{1,0:T(8,128)(2,1)S(1)}, bf16[512,768]{1,0:T(8,128)(2,1)S(1)}, u32[]{:S(2)}, u32[]{:S(2)}) %collective-permute-start.48) | collective-permute-done | bytes 786464 | tf_op jit(solution)/shard_map/ppermute | solution.py:23
  343.5 6.0 %add_convert_fusion = bf16[384,1024]{1,0:T(8,128)(2,1)S(1)} fusion(bf16[384,1024]{1,0:T(8,128)(2,1)S(1)} %copy-done.5, bf16[384,4096]{1,0:T(8,128)(2,1)S(1)} %constant_dynamic-update-slice_fusion.16, bf16[4096,1024]{1,0:T(8,128)(2,1)} %bitcast.44), kind=kOutput, calls=%fused_computation.9 | convolution fusion | flops 3222405120 | bytes 13107200 | tf_op jit(solution)/shard_map/dot_general | solution.py:198
  351.5 8.9 %collective-permute-start.39 = (bf16[384,1024]{1,0:T(8,128)(2,1)S(1)}, bf16[384,1024]{1,0:T(8,128)(2,1)S(1)}, u32[]{:S(2)}, u32[]{:S(2)}) collective-permute-start(bf16[384,1024]{1,0:T(8,128)(2,1)S(1)} %add_convert_fusion), channel_id=1, source_target_pairs={{0,8},{8,16},{16,24},{24,0},{1,9},{9,17},{17,25},{25,1},{2,10},{10... | collective-permute-start | bytes 2359304 | tf_op jit(solution)/shard_map/ppermute | solution.py:23
  366.1 10.4 %collective-permute-done.39 = bf16[384,1024]{1,0:T(8,128)(2,1)S(1)} collective-permute-done((bf16[384,1024]{1,0:T(8,128)(2,1)S(1)}, bf16[384,1024]{1,0:T(8,128)(2,1)S(1)}, u32[]{:S(2)}, u32[]{:S(2)}) %collective-permute-start.39) | collective-permute-done | bytes 786464 | tf_op jit(solution)/shard_map/ppermute | solution.py:23
  378.1 13.8 %collective-permute-start.55 = (bf16[384,1024]{1,0:T(8,128)(2,1)S(1)}, bf16[384,1024]{1,0:T(8,128)(2,1)S(1)}, u32[]{:S(2)}, u32[]{:S(2)}) collective-permute-start(bf16[384,1024]{1,0:T(8,128)(2,1)S(1)} %collective-permute-done.39), channel_id=1, source_target_pairs={{0,8},{8,16},{16,24},{24,0},{1,9},{9,17},{17,25},{25,1},{2,10},{10... | collective-permute-start | bytes 2359304 | tf_op jit(solution)/shard_map/ppermute | solution.py:23
  398.6 14.3 %collective-permute-done.55 = bf16[384,1024]{1,0:T(8,128)(2,1)S(1)} collective-permute-done((bf16[384,1024]{1,0:T(8,128)(2,1)S(1)}, bf16[384,1024]{1,0:T(8,128)(2,1)S(1)}, u32[]{:S(2)}, u32[]{:S(2)}) %collective-permute-start.55) | collective-permute-done | bytes 786464 | tf_op jit(solution)/shard_map/ppermute | solution.py:23
  415.8 17.1 %collective-permute-done.57 = bf16[384,1024]{1,0:T(8,128)(2,1)S(1)} collective-permute-done((bf16[384,1024]{1,0:T(8,128)(2,1)S(1)}, bf16[384,1024]{1,0:T(8,128)(2,1)S(1)}, u32[]{:S(2)}, u32[]{:S(2)}) %collective-permute-start.57) | collective-permute-done | bytes 786464 | tf_op jit(solution)/shard_map/ppermute | solution.py:23
  439.0 17.4 %collective-permute-done.64 = bf16[384,1024]{1,0:T(8,128)(2,1)S(1)} collective-permute-done((bf16[384,1024]{1,0:T(8,128)(2,1)S(1)}, bf16[384,1024]{1,0:T(8,128)(2,1)S(1)}, u32[]{:S(2)}, u32[]{:S(2)}) %collective-permute-start.64) | collective-permute-done | bytes 786464 | tf_op jit(solution)/shard_map/ppermute | solution.py:23
  480.5 8.4 %shard_map.88 = bf16[16,128,256]{2,1,0:T(8,128)(2,1)} custom-call(f32[16,1,384]{2,1,0:T(1,128)} %copy-done.11), custom_call_target="tpu_custom_call" | custom-call | tf_op jit(solution)/shard_map/pallas_call | solution.py:132
  531.7 5.9 %collective-permute-done.71 = bf16[384,256]{1,0:T(8,128)(2,1)S(1)} collective-permute-done((bf16[384,256]{1,0:T(8,128)(2,1)S(1)}, bf16[384,256]{1,0:T(8,128)(2,1)S(1)}, u32[]{:S(2)}, u32[]{:S(2)}) %collective-permute-start.71) | collective-permute-done | bytes 196640 | tf_op jit(solution)/shard_map/ppermute | solution.py:23
  (353 shorter events, 213.6 us)
Async XLA Ops:
  32.8 38.1 %collective-permute-start.32 = (bf16[512,1024]{1,0:T(8,128)(2,1)S(1)}, bf16[512,1024]{1,0:T(8,128)(2,1)S(1)}, u32[]{:S(2)}, u32[]{:S(2)}) collective-permute-start(bf16[512,1024]{1,0:T(8,128)(2,1)S(1)} %copy-done.3), channel_id=1, source_target_pairs={{0,4},{4,0},{1,5},{5,1},{2,6},{6,2},{3,7},{7,3},{8,12},{12,8},{9,1... | collective-permute-start | bytes 3145736 | tf_op jit(solution)/shard_map/ppermute | solution.py:23
  36.3 96.2 %collective-permute-start.33 = (bf16[512,1024]{1,0:T(8,128)(2,1)S(1)}, bf16[512,1024]{1,0:T(8,128)(2,1)S(1)}, u32[]{:S(2)}, u32[]{:S(2)}) collective-permute-start(bf16[512,1024]{1,0:T(8,128)(2,1)S(1)} %copy-done.3), channel_id=1, source_target_pairs={{0,8},{8,16},{16,24},{24,0},{1,9},{9,17},{17,25},{25,1},{2,10},{10... | collective-permute-start | bytes 3145736 | tf_op jit(solution)/shard_map/ppermute | solution.py:23
  38.0 73.6 %collective-permute-start.7 = (bf16[512,768]{1,0:T(8,128)(2,1)S(1)}, bf16[512,768]{1,0:T(8,128)(2,1)S(1)}, u32[]{:S(2)}, u32[]{:S(2)}) collective-permute-start(bf16[512,768]{1,0:T(8,128)(2,1)S(1)} %copy-done.17), channel_id=1, source_target_pairs={{0,16},{8,24},{16,0},{24,8},{1,17},{9,25},{17,1},{25,9},{2,18},{10... | collective-permute-start | bytes 2359304 | tf_op jit(solution)/shard_map/ppermute | solution.py:23
  49.3 62.9 %collective-permute-start.14 = (bf16[384,1024]{1,0:T(8,128)(2,1)S(1)}, bf16[384,1024]{1,0:T(8,128)(2,1)S(1)}, u32[]{:S(2)}, u32[]{:S(2)}) collective-permute-start(bf16[384,1024]{1,0:T(8,128)(2,1)S(1)} %collective-permute-done.13), channel_id=1, source_target_pairs={{0,1},{1,0},{2,3},{3,2},{4,5},{5,4},{6,7},{7,6},{8,9},{9,8},{10,11... | collective-permute-start | bytes 2359304 | tf_op jit(solution)/shard_map/ppermute | solution.py:23
  57.1 56.8 %collective-permute-start.9 = (bf16[512,768]{1,0:T(8,128)(2,1)S(1)}, bf16[512,768]{1,0:T(8,128)(2,1)S(1)}, u32[]{:S(2)}, u32[]{:S(2)}) collective-permute-start(bf16[512,768]{1,0:T(8,128)(2,1)S(1)} %copy-done.16), channel_id=1, source_target_pairs={{0,24},{8,0},{16,8},{24,16},{1,25},{9,1},{17,9},{25,17},{2,26},{10... | collective-permute-start | bytes 2359304 | tf_op jit(solution)/shard_map/ppermute | solution.py:23
  70.9 58.6 %collective-permute-start.6 = (bf16[512,768]{1,0:T(8,128)(2,1)S(1)}, bf16[512,768]{1,0:T(8,128)(2,1)S(1)}, u32[]{:S(2)}, u32[]{:S(2)}) collective-permute-start(bf16[512,768]{1,0:T(8,128)(2,1)S(1)} %collective-permute-done.5), channel_id=1, source_target_pairs={{0,4},{4,0},{1,5},{5,1},{2,6},{6,2},{3,7},{7,3},{8,12},{12,8},{9,1... | collective-permute-start | bytes 2359304 | tf_op jit(solution)/shard_map/ppermute | solution.py:23
  111.6 36.6 %collective-permute-start.2 = (bf16[384,1024]{1,0:T(8,128)(2,1)S(1)}, bf16[384,1024]{1,0:T(8,128)(2,1)S(1)}, u32[]{:S(2)}, u32[]{:S(2)}) collective-permute-start(bf16[384,1024]{1,0:T(8,128)(2,1)S(1)} %collective-permute-done), channel_id=1, source_target_pairs={{0,2},{2,0},{1,3},{3,1},{4,6},{6,4},{5,7},{7,5},{8,10},{10,8},{9,1... | collective-permute-start | bytes 2359304 | tf_op jit(solution)/shard_map/ppermute | solution.py:23
  113.9 43.6 %collective-permute-start.16 = (bf16[384,1024]{1,0:T(8,128)(2,1)S(1)}, bf16[384,1024]{1,0:T(8,128)(2,1)S(1)}, u32[]{:S(2)}, u32[]{:S(2)}) collective-permute-start(bf16[384,1024]{1,0:T(8,128)(2,1)S(1)} %collective-permute-done), channel_id=1, source_target_pairs={{0,8},{8,16},{16,24},{24,0},{1,9},{9,17},{17,25},{25,1},{2,10},{10... | collective-permute-start | bytes 2359304 | tf_op jit(solution)/shard_map/ppermute | solution.py:23
  132.6 37.9 %collective-permute-start.1 = (bf16[384,1024]{1,0:T(8,128)(2,1)S(1)}, bf16[384,1024]{1,0:T(8,128)(2,1)S(1)}, u32[]{:S(2)}, u32[]{:S(2)}) collective-permute-start(bf16[384,1024]{1,0:T(8,128)(2,1)S(1)} %collective-permute-done), channel_id=1, source_target_pairs={{0,1},{1,0},{2,3},{3,2},{4,5},{5,4},{6,7},{7,6},{8,9},{9,8},{10,11... | collective-permute-start | bytes 2359304 | tf_op jit(solution)/shard_map/ppermute | solution.py:23
  132.6 96.9 %collective-permute-start.35 = (bf16[512,1024]{1,0:T(8,128)(2,1)S(1)}, bf16[512,1024]{1,0:T(8,128)(2,1)S(1)}, u32[]{:S(2)}, u32[]{:S(2)}) collective-permute-start(bf16[512,1024]{1,0:T(8,128)(2,1)S(1)} %collective-permute-done.33), channel_id=1, source_target_pairs={{0,8},{8,16},{16,24},{24,0},{1,9},{9,17},{17,25},{25,1},{2,10},{10... | collective-permute-start | bytes 3145736 | tf_op jit(solution)/shard_map/ppermute | solution.py:23
  156.5 71.4 %collective-permute-start.15 = (bf16[8,768]{1,0:T(8,128)(2,1)S(1)}, bf16[8,768]{1,0:T(8,128)(2,1)S(1)}, u32[]{:S(2)}, u32[]{:S(2)}) collective-permute-start(bf16[8,768]{1,0:T(8,128)(2,1)S(1)} %slice.906), channel_id=1, source_target_pairs={{0,4},{4,0},{1,5},{5,1},{2,6},{6,2},{3,7},{7,3},{8,12},{12,8},{9,1... | collective-permute-start | bytes 36872 | tf_op jit(solution)/shard_map/ppermute | solution.py:23
  192.4 37.2 %collective-permute-start.11 = (bf16[8,768]{1,0:T(8,128)(2,1)S(1)}, bf16[8,768]{1,0:T(8,128)(2,1)S(1)}, u32[]{:S(2)}, u32[]{:S(2)}) collective-permute-start(bf16[8,768]{1,0:T(8,128)(2,1)S(1)} %slice.905), channel_id=1, source_target_pairs={{0,4},{4,0},{1,5},{5,1},{2,6},{6,2},{3,7},{7,3},{8,12},{12,8},{9,1... | collective-permute-start | bytes 36872 | tf_op jit(solution)/shard_map/ppermute | solution.py:23
  227.9 46.0 %collective-permute-start.34 = (bf16[512,1024]{1,0:T(8,128)(2,1)S(1)}, bf16[512,1024]{1,0:T(8,128)(2,1)S(1)}, u32[]{:S(2)}, u32[]{:S(2)}) collective-permute-start(bf16[512,1024]{1,0:T(8,128)(2,1)S(1)} %collective-permute-done.33), channel_id=1, source_target_pairs={{0,4},{4,0},{1,5},{5,1},{2,6},{6,2},{3,7},{7,3},{8,12},{12,8},{9,1... | collective-permute-start | bytes 3145736 | tf_op jit(solution)/shard_map/ppermute | solution.py:23
  235.2 36.3 %collective-permute-start.27 = (bf16[384,256]{1,0:T(8,128)(2,1)S(1)}, bf16[384,256]{1,0:T(8,128)(2,1)S(1)}, u32[]{:S(2)}, u32[]{:S(2)}) collective-permute-start(bf16[384,256]{1,0:T(8,128)(2,1)S(1)} %fusion.88), channel_id=1, source_target_pairs={{0,16},{8,24},{16,0},{24,8},{1,17},{9,25},{17,1},{25,9},{2,18},{10... | collective-permute-start | bytes 589832 | tf_op jit(solution)/shard_map/ppermute | solution.py:23
  261.7 61.7 %collective-permute-start.46 = (bf16[512,768]{1,0:T(8,128)(2,1)S(1)}, bf16[512,768]{1,0:T(8,128)(2,1)S(1)}, u32[]{:S(2)}, u32[]{:S(2)}) collective-permute-start(bf16[512,768]{1,0:T(8,128)(2,1)S(1)} %copy-done.14), channel_id=1, source_target_pairs={{0,16},{8,24},{16,0},{24,8},{1,17},{9,25},{17,1},{25,9},{2,18},{10... | collective-permute-start | bytes 2359304 | tf_op jit(solution)/shard_map/ppermute | solution.py:23
  271.9 68.7 %collective-permute-start.38 = (bf16[512,1024]{1,0:T(8,128)(2,1)S(1)}, bf16[512,1024]{1,0:T(8,128)(2,1)S(1)}, u32[]{:S(2)}, u32[]{:S(2)}) collective-permute-start(bf16[512,1024]{1,0:T(8,128)(2,1)S(1)} %collective-permute-done.37), channel_id=1, source_target_pairs={{0,4},{4,0},{1,5},{5,1},{2,6},{6,2},{3,7},{7,3},{8,12},{12,8},{9,1... | collective-permute-start | bytes 3145736 | tf_op jit(solution)/shard_map/ppermute | solution.py:23
  287.0 53.2 %collective-permute-start.48 = (bf16[512,768]{1,0:T(8,128)(2,1)S(1)}, bf16[512,768]{1,0:T(8,128)(2,1)S(1)}, u32[]{:S(2)}, u32[]{:S(2)}) collective-permute-start(bf16[512,768]{1,0:T(8,128)(2,1)S(1)} %copy-done.13), channel_id=1, source_target_pairs={{0,24},{8,0},{16,8},{24,16},{1,25},{9,1},{17,9},{25,17},{2,26},{10... | collective-permute-start | bytes 2359304 | tf_op jit(solution)/shard_map/ppermute | solution.py:23
  297.6 45.7 %collective-permute-start.29 = (bf16[384,1024]{1,0:T(8,128)(2,1)S(1)}, bf16[384,1024]{1,0:T(8,128)(2,1)S(1)}, u32[]{:S(2)}, u32[]{:S(2)}) collective-permute-start(bf16[384,1024]{1,0:T(8,128)(2,1)S(1)} %pad_maximum_fusion.2), channel_id=1, source_target_pairs={{0,1},{1,0},{2,3},{3,2},{4,5},{5,4},{6,7},{7,6},{8,9},{9,8},{10,11... | collective-permute-start | bytes 2359304 | tf_op jit(solution)/shard_map/ppermute | solution.py:23
  298.6 44.8 %collective-permute-start.31 = (bf16[384,1024]{1,0:T(8,128)(2,1)S(1)}, bf16[384,1024]{1,0:T(8,128)(2,1)S(1)}, u32[]{:S(2)}, u32[]{:S(2)}) collective-permute-start(bf16[384,1024]{1,0:T(8,128)(2,1)S(1)} %collective-permute-done.30), channel_id=1, source_target_pairs={{0,1},{1,0},{2,3},{3,2},{4,5},{5,4},{6,7},{7,6},{8,9},{9,8},{10,11... | collective-permute-start | bytes 2359304 | tf_op jit(solution)/shard_map/ppermute | solution.py:23
  340.6 37.4 %collective-permute-start.49 = (bf16[512,768]{1,0:T(8,128)(2,1)S(1)}, bf16[512,768]{1,0:T(8,128)(2,1)S(1)}, u32[]{:S(2)}, u32[]{:S(2)}) collective-permute-start(bf16[512,768]{1,0:T(8,128)(2,1)S(1)} %collective-permute-done.48), channel_id=1, source_target_pairs={{0,4},{4,0},{1,5},{5,1},{2,6},{6,2},{3,7},{7,3},{8,12},{12,8},{9,1... | collective-permute-start | bytes 2359304 | tf_op jit(solution)/shard_map/ppermute | solution.py:23
  378.1 36.5 %collective-permute-start.40 = (bf16[384,1024]{1,0:T(8,128)(2,1)S(1)}, bf16[384,1024]{1,0:T(8,128)(2,1)S(1)}, u32[]{:S(2)}, u32[]{:S(2)}) collective-permute-start(bf16[384,1024]{1,0:T(8,128)(2,1)S(1)} %collective-permute-done.39), channel_id=1, source_target_pairs={{0,1},{1,0},{2,3},{3,2},{4,5},{5,4},{6,7},{7,6},{8,9},{9,8},{10,11... | collective-permute-start | bytes 2359304 | tf_op jit(solution)/shard_map/ppermute | solution.py:23
  398.1 66.8 %collective-permute-start.54 = (bf16[8,768]{1,0:T(8,128)(2,1)S(1)}, bf16[8,768]{1,0:T(8,128)(2,1)S(1)}, u32[]{:S(2)}, u32[]{:S(2)}) collective-permute-start(bf16[8,768]{1,0:T(8,128)(2,1)S(1)} %slice.990), channel_id=1, source_target_pairs={{0,4},{4,0},{1,5},{5,1},{2,6},{6,2},{3,7},{7,3},{8,12},{12,8},{9,1... | collective-permute-start | bytes 36872 | tf_op jit(solution)/shard_map/ppermute | solution.py:23
  469.2 36.4 %collective-permute-start.61 = (bf16[128,256]{1,0:T(8,128)(2,1)}, bf16[128,256]{1,0:T(8,128)(2,1)S(1)}, u32[]{:S(2)}, u32[]{:S(2)}) collective-permute-start(bf16[128,256]{1,0:T(8,128)(2,1)} %slice.1016), channel_id=1, source_target_pairs={{0,4},{4,0},{1,5},{5,1},{2,6},{6,2},{3,7},{7,3},{8,12},{12,8},{9,1... | collective-permute-start | bytes 196616 | tf_op jit(solution)/shard_map/ppermute | solution.py:23
  470.5 35.1 %collective-permute-start.60 = (bf16[128,256]{1,0:T(8,128)(2,1)}, bf16[128,256]{1,0:T(8,128)(2,1)}, u32[]{:S(2)}, u32[]{:S(2)}) collective-permute-start(bf16[128,256]{1,0:T(8,128)(2,1)} %slice.1007), channel_id=1, source_target_pairs={{0,4},{4,0},{1,5},{5,1},{2,6},{6,2},{3,7},{7,3},{8,12},{12,8},{9,1... | collective-permute-start | bytes 196616 | tf_op jit(solution)/shard_map/ppermute | solution.py:23
  (67 other events, 1707.9 us)

commit v2 on v1

v2 whole, which is shorter than its diff:
```python
import functools

import jax
import jax.numpy as jnp
from jax import lax
from jax.experimental import pallas as pl
from jax.experimental.pallas import tpu as pltpu
from jax.sharding import Mesh, PartitionSpec as P

AXES = ("z", "y", "x", "c")
SHORT_CALL = pl.CostEstimate(flops=1, bytes_accessed=1, transcendentals=0)


def factors(mesh):
    seq, mp = mesh.shape["seq"], mesh.shape["mp"]
    along_y = 1
    while 2 * along_y * along_y < seq:
        along_y *= 2
    return seq // along_y, along_y, mp // 2, 2


def rotate(value, axis, by):
    size = lax.axis_size(axis)
    return lax.ppermute(value, axis, [(i, (i + by) % size) for i in range(size)])


def blank_kernel(out_ref):
    del out_ref


def blank(shape, dtype):
    return pl.pallas_call(
        blank_kernel, out_specs=pl.BlockSpec(memory_space=pl.ANY), out_shape=jax.ShapeDtypeStruct(shape, dtype)
    )()


class Steps:
    def __init__(self):
        self.gate, self.open = (), []

    def __call__(self, send, value, *earlier, wait=True):
        found = send(after(value, *self.gate, *earlier))
        if wait:
            self.open.append(found)
        return found

    def then(self, *others):
        self.gate, self.open = tuple(self.open) + others, []


def after(value, *earlier):
    return lax.optimization_barrier((value, *earlier))[0]


def split_kernel(source, gain, target):
    target[0] = (source[0, 0].astype(jnp.float32) * gain[...]).astype(jnp.bfloat16)


def split_weights(in_weight, block, c, gain):
    parts = lax.axis_size("z")
    rows, columns = in_weight.shape[2], in_weight.shape[3] // parts
    if columns % 128:
        scaled = (in_weight[block, c].astype(jnp.float32) * gain).astype(jnp.bfloat16)
        return scaled.reshape(rows, parts, columns).transpose(1, 0, 2)
    return pl.pallas_call(
        split_kernel,
        grid=(parts,),
        in_specs=[
            pl.BlockSpec((1, 1, rows, columns), lambda k: (block, c, 0, k)),
            pl.BlockSpec((rows, 1), lambda k: (0, 0)),
        ],
        out_specs=pl.BlockSpec((1, rows, columns), lambda k: (k, 0, 0)),
        cost_estimate=SHORT_CALL,
        out_shape=jax.ShapeDtypeStruct((parts, rows, columns), jnp.bfloat16),
    )(in_weight, gain)


def exchange(pieces):
    return lax.all_to_all(pieces, "z", 0, 0, tiled=True)


def others(axis, value, send):
    moves = [functools.partial(rotate, axis=axis, by=j) for j in range(1, lax.axis_size(axis))]
    return [value] + [send(move, value) for move in moves]


def at_once(move, value):
    return move(value)


def slot_of(z_from, x_at, c_at):
    x_size, c_size = lax.axis_size("x"), lax.axis_size("c")
    x_from, c_from = z_from // c_size, z_from % c_size
    return ((x_at - x_from) % x_size) * c_size + (c_at - c_from) % c_size


def placed_rows(found, places, where):
    _, y_at, x_at, c_at = where
    parts, y_size = lax.axis_size("z"), lax.axis_size("y")
    rows, columns = found[0][0].shape
    whole = blank((parts, y_size, rows, columns), found[0][0].dtype)
    for group, place in zip(found, places):
        slot = slot_of(place, x_at, c_at)
        for j, piece in enumerate(group):
            whole = lax.dynamic_update_slice(whole, piece[None, None], (slot, (y_at - j) % y_size, 0, 0))
    return whole.reshape(parts * y_size * rows, columns)


def all_of_c(found):
    return [rotate(p, "c", d) if d else p for p in found for d in range(lax.axis_size("c"))]


def next_along_z(value):
    return rotate(value, "z", 1)


def project_kernel(groups, order_ref, *refs):
    count = len(refs) - 5
    pieces = refs[: count - 3 * (order_ref.shape[0] - groups[1])]
    weights = refs[len(pieces) : count]
    out_ref, held, total, squares, arrived = refs[-5:]
    step = pl.program_id(0)
    y_size = len(weights) // 3
    deep, width = weights[0].shape[1], weights[0].shape[2]
    rows = pieces[0].shape[0]

    def arrival(g, r):
        return pltpu.make_async_copy(
            pieces[g * groups[1] + r], held.at[r, pl.ds(g * rows, rows)], arrived.at[r, g]
        )

    @pl.when(step == 0)
    def _():
        for r in range(groups[1]):
            for g in range(groups[0]):
                arrival(g, r).start()
        total[...] = jnp.zeros_like(total)
        squares[...] = jnp.zeros_like(squares)

    for r in range(groups[1]):

        @pl.when(step == r)
        def _(r=r):
            for g in range(groups[0]):
                arrival(g, r).wait()

    for g in range(groups[0]):
        these = slice(g * rows, (g + 1) * rows)
        values = held[step, these].astype(jnp.float32)
        squares[these] += jnp.sum(values * values, axis=1, keepdims=True)
    for c in range(3):
        some = 0.0
        for j in range(y_size):
            begin = pl.multiple_of(order_ref[groups[1] + j] * deep, deep)
            some = some + jnp.dot(
                held[step, :, pl.ds(begin, deep)], weights[c * y_size + j][0], preferred_element_type=jnp.float32
            )
        total[:, c * width : (c + 1) * width] += some

    @pl.when(step == groups[1] - 1)
    def _():
        scale = lax.rsqrt(squares[...] / (groups[1] * pieces[0].shape[1]) + 1e-06)
        out_ref[...] = (total[...] * scale).astype(out_ref.dtype)


def project(found, weights, order):
    groups = (len(found), len(found[0]))
    flat = [w for group in weights for w in group]
    pieces = [p for group in found for p in group]
    rows, features_here = pieces[0].shape
    width = flat[0].shape[2]
    out = pl.pallas_call(
        functools.partial(project_kernel, groups),
        grid_spec=pltpu.PrefetchScalarGridSpec(
            num_scalar_prefetch=1,
            grid=(groups[1],),
            in_specs=[pl.BlockSpec(memory_space=pl.ANY)] * len(pieces)
            + [pl.BlockSpec((1,) + w.shape[1:], lambda r, order: (order[r], 0, 0)) for w in flat],
            out_specs=pl.BlockSpec((groups[0] * rows, 3 * width), lambda r, order: (0, 0)),
            scratch_shapes=[
                pltpu.VMEM((groups[1], groups[0] * rows, features_here), jnp.bfloat16),
                pltpu.VMEM((groups[0] * rows, 3 * width), jnp.float32),
                pltpu.VMEM((groups[0] * rows, 1), jnp.float32),
                pltpu.SemaphoreType.DMA((groups[1], groups[0])),
            ],
        ),
        out_shape=jax.ShapeDtypeStruct((groups[0] * rows, 3 * width), jnp.bfloat16),
        compiler_params=pltpu.CompilerParams(vmem_limit_bytes=48 * 2**20),
    )(order, *pieces, *flat)
    return out.reshape(groups[0], rows, 3 * width)


def mix_table(z_at, y_at, places):
    parts = len(places)
    stacked = jnp.stack(places)
    behind = jnp.where(y_at == 0, stacked[(stacked - 1) % parts], jnp.arange(parts))
    some = jnp.where((y_at == 0) & (stacked == 0), 0, 1)
    return jnp.stack([behind, some, stacked]).astype(jnp.int32)


def delayed(value, by):
    return pltpu.roll(value, by, 0) if by else value


def taps_sum(value, taps):
    total = taps[0] * value
    for s in range(1, len(taps)):
        total = total + taps[s] * delayed(value, s)
    return total


def features(lanes, width, start, table_ref, proj_ref, before_ref, feat_ref):
    some = table_ref[1, pl.program_id(0)].astype(jnp.float32)
    out = []
    for c in range(3):
        begin = c * width + start
        before = before_ref[0, :, begin : begin + lanes].astype(jnp.float32) * some
        value = jnp.concatenate([before, proj_ref[0, :, begin : begin + lanes].astype(jnp.float32)], axis=0)
        taps = [feat_ref[c, s : s + 1, start : start + lanes] for s in range(feat_ref.shape[1])]
        out.append(taps_sum(value, taps))
    return out


def short_kernel(table_ref, proj_ref, before_ref, feat_ref, taps_ref, out_ref):
    width = out_ref.shape[2]
    lanes = min(128, width)
    rim = before_ref.shape[1]
    for start in range(0, width, lanes):
        query, key, value = features(lanes, width, start, table_ref, proj_ref, before_ref, feat_ref)
        kv = (key * value).astype(jnp.bfloat16).astype(jnp.float32)
        taps = [taps_ref[s : s + 1, start : start + lanes] for s in range(taps_ref.shape[0])]
        inner = taps_sum(kv, taps)
        out_ref[0, :, start : start + lanes] = (query[rim:] * inner[rim:]).astype(out_ref.dtype)


def gate_kernel(table_ref, proj_ref, before_ref, feat_ref, query_ref, kv_ref):
    width = kv_ref.shape[2]
    lanes = min(128, width)
    rim = before_ref.shape[1]
    for start in range(0, width, lanes):
        query, key, value = features(lanes, width, start, table_ref, proj_ref, before_ref, feat_ref)
        query_ref[0, :, start : start + lanes] = query[rim:]
        kv_ref[0, :, start : start + lanes] = (key[rim:] * value[rim:]).astype(kv_ref.dtype)


def medium_kernel(table_ref, query_ref, kv_ref, before_ref, matrix_ref, out_ref):
    groups, span = matrix_ref.shape[0], matrix_ref.shape[1]
    count, width = out_ref.shape[1], out_ref.shape[2]
    lanes = min(128, width)
    per_group = width // groups
    some = table_ref[1, pl.program_id(0)]
    before = before_ref[0]
    before = jnp.where(some > 0, before, jnp.zeros_like(before))
    lane = lax.broadcasted_iota(jnp.int32, (span, lanes), 1) // per_group
    for block in range(count // span):
        own = kv_ref[0, block * span : (block + 1) * span]
        pair = jnp.concatenate([before, own], axis=0)
        before = own
        rows = slice(block * span, (block + 1) * span)
        for start in range(0, width, lanes):
            inner = jnp.zeros((span, lanes), jnp.float32)
            for g in range(lanes // per_group):
                taken = jnp.dot(
                    matrix_ref[start // per_group + g], pair[:, start : start + lanes], preferred_element_type=jnp.float32
                )
                inner = jnp.where(lane == g, taken, inner)
            query = query_ref[0, rows, start : start + lanes]
            out_ref[0, rows, start : start + lanes] = (query * inner).astype(out_ref.dtype)


def whole_spec(value):
    return pl.BlockSpec(value.shape, lambda i, table: (0,) * value.ndim)


def piece_spec(value, which=None):
    def index(i, table):
        return (i if which is None else table[which, i], 0, 0)

    return pl.BlockSpec((1,) + value.shape[1:], index)


def short_mix(proj, feat, taps, table):
    before = rotate(proj[:, proj.shape[1] - 16 :], "y", 1)
    out = jax.ShapeDtypeStruct(proj.shape[:2] + (proj.shape[2] // 3,), jnp.bfloat16)
    return pl.pallas_call(
        short_kernel,
        grid_spec=pltpu.PrefetchScalarGridSpec(
            num_scalar_prefetch=1,
            grid=(proj.shape[0],),
            in_specs=[piece_spec(proj), piece_spec(before, 0), whole_spec(feat), whole_spec(taps)],
            out_specs=piece_spec(out, 2),
        ),
        cost_estimate=SHORT_CALL,
        out_shape=out,
    )(table, proj, before, feat, taps)


def medium_mix(proj, feat, matrix, table):
    before = rotate(proj[:, proj.shape[1] - 16 :], "y", 1)
    shape = proj.shape[:2] + (proj.shape[2] // 3,)
    query = jax.ShapeDtypeStruct(shape, jnp.float32)
    kv = jax.ShapeDtypeStruct(shape, jnp.bfloat16)
    query, kv = pl.pallas_call(
        gate_kernel,
        grid_spec=pltpu.PrefetchScalarGridSpec(
            num_scalar_prefetch=1,
            grid=(proj.shape[0],),
            in_specs=[piece_spec(proj), piece_spec(before, 0), whole_spec(feat)],
            out_specs=[piece_spec(query), piece_spec(kv)],
        ),
        cost_estimate=SHORT_CALL,
        out_shape=[query, kv],
    )(table, proj, before, feat)
    before = rotate(kv[:, kv.shape[1] - matrix.shape[1] :], "y", 1)
    return pl.pallas_call(
        medium_kernel,
        grid_spec=pltpu.PrefetchScalarGridSpec(
            num_scalar_prefetch=1,
            grid=(proj.shape[0],),
            in_specs=[piece_spec(query), piece_spec(kv), piece_spec(before, 0), whole_spec(matrix)],
            out_specs=piece_spec(kv, 2),
        ),
        cost_estimate=SHORT_CALL,
        out_shape=jax.ShapeDtypeStruct(shape, jnp.bfloat16),
    )(table, query, kv, before, matrix)


def toeplitz_kernel(row_ref, out_ref):
    width = out_ref.shape[1]
    rows = jnp.broadcast_to(row_ref[0], (width, 3 * width))
    turned = pltpu.roll(rows, 0, 1, stride=1, stride_axis=0)
    out_ref[0] = turned[:, : 2 * width].astype(out_ref.dtype)


def toeplitz(filt):
    groups, width = filt.shape
    row = jnp.concatenate([jnp.zeros((groups, 1)), filt[:, ::-1], jnp.zeros((groups, 2 * width - 1))], axis=1)[:, None]
    return pl.pallas_call(
        toeplitz_kernel,
        grid=(groups,),
        in_specs=[pl.BlockSpec((1, 1, 3 * width), lambda g: (g, 0, 0))],
        out_specs=pl.BlockSpec((1, width, 2 * width), lambda g: (g, 0, 0)),
        cost_estimate=SHORT_CALL,
        out_shape=jax.ShapeDtypeStruct((groups, width, 2 * width), jnp.bfloat16),
    )(row)


def channels_of(value, z_at, axis):
    size = value.shape[axis] // lax.axis_size("z")
    return lax.dynamic_slice_in_dim(value, z_at * size, size, axis)


def home(pieces):
    back = exchange(pieces)
    return jnp.concatenate([back[k] for k in range(back.shape[0])], axis=1)


def local(tokens, norm_gain, in_weight, feat_filter, short_filter, medium_filter, out_weight):
    where = tuple(lax.axis_index(a) for a in AXES)
    z_at, y_at, x_at, c_at = where
    parts = lax.axis_size("z")
    rows = in_weight.shape[2]
    width = in_weight.shape[3] // parts
    begin = (z_at * lax.axis_size("y") + y_at) * rows
    gains = lax.dynamic_slice_in_dim(norm_gain, begin, rows, 1)[:, :, None]
    feat = channels_of(feat_filter, z_at, 3)
    short = channels_of(short_filter, z_at, 0)
    short_taps = jnp.repeat(short.T, width // short.shape[0], axis=1)
    matrix = toeplitz(channels_of(medium_filter, z_at, 0))
    places = [(z_at - k) % parts for k in range(parts)]
    table = mix_table(z_at, y_at, places)
    x_size, c_size, y_size = (lax.axis_size(a) for a in ("x", "c", "y"))
    order = [((x_at - d) % x_size) * c_size + (c_at - e) % c_size for d in range(x_size) for e in range(c_size)]
    order = jnp.stack(order + [(y_at - j) % y_size for j in range(y_size)]).astype(jnp.int32)

    def split(block, c):
        return split_weights(in_weight, block, c, gains[block])

    step = Steps()
    ring, found, came, weights = [tokens], [], [], []
    rows_ring, held = [out_weight], []
    for k in range(parts):
        if k < parts - 1:
            ring.append(step(next_along_z, ring[k]))
        else:
            rows_ring.append(step(next_along_z, out_weight))
        if k < 3:
            came.append(step(exchange, split(0, k)))
        found.append(others("x", ring[k], step))
        if k == 0:
            held.append(others("y", out_weight, step))
        elif k <= 3:
            weights.append(others("y", came[k - 1], step))
        step.then(*([matrix] if k == 1 else []))
    proj = project([all_of_c(group) for group in found], weights, order)
    gated = short_mix(proj, feat[0], short_taps, table)
    back = home(gated)
    for k in range(1, parts):
        if k < parts - 1:
            rows_ring.append(step(next_along_z, rows_ring[k]))
            held.append(others("y", rows_ring[k], step))
            step.then()
    held.append(others("y", rows_ring[-1], step))
    came, weights_next = [], []
    for k in range(4):
        if k < 3:
            came.append(step(exchange, split(1, k), back))
        if k:
            weights_next.append(others("y", came[k - 1], step))
        step.then()
    first = jnp.concatenate(all_of_c(others("x", back, at_once)), axis=1)
    out_rows = placed_rows(held, places, where)
    delta = jnp.dot(first, out_rows, preferred_element_type=jnp.float32)
    stream = (tokens.astype(jnp.float32) + delta).astype(jnp.bfloat16)

    step = Steps()
    ring, found = [stream], []
    for k in range(parts):
        if k < parts - 1:
            ring.append(step(next_along_z, ring[k]))
        found.append(others("x", ring[k], step))
        step.then()
    found = [all_of_c(group) for group in found[:-1]] + [found[-1]]
    proj = [project(found[:2], weights_next, order)]
    for group in found[2:-1]:
        proj.append(project([group], weights_next, order))
    last = found[-1][:1] + [after(p, *proj) for p in found[-1][1:]]
    proj.append(project([all_of_c(last)], weights_next, order))
    gated = medium_mix(jnp.concatenate(proj), feat[1], matrix, table)
    return stream, home(gated)


def solution(mesh):
    wide = Mesh(mesh.devices.reshape(factors(mesh)), AXES)
    seq, mp = ("z", "y"), ("x", "c")
    placed = (
        P(seq, mp),
        P(),
        P(None, None, seq, mp),
        P(None, None, None, mp),
        P(mp, None),
        P(mp, None),
        P(seq, mp),
    )
    return jax.shard_map(
        local,
        mesh=wide,
        in_specs=placed,
        out_specs=(P(seq, mp), P(seq, mp)),
        check_vma=False,
    )
```

time: 553 us -> 493 us (0.89); the launches traced: 545 us -> 491 us
  Pallas kernels: 18.1 us -> 91.1 us
  starting transfers between devices: 135 us -> 66.9 us
  matrix products: 43 us -> 8.63 us
  local copies, waits for them, and re-layouts: 70.7 us -> 36.7 us
  blocking collectives: 0 us -> 22.7 us
  other arithmetic: 18.9 us -> 3.22 us
    ppermute x72 -> x49, starting transfers between devices: 135 us -> 36 us  [rotate(): lax.ppermute(value, axis, [(i, (i + by) % size) for i in range(size)])]
    pallas_call x2 -> x14, Pallas kernels: 9.72 us -> 82.7 us  [the longest x4 42 us: project(): pl.pallas_call(functools.partial(project_kernel, groups), grid_spec=pltpu...]
    all_to_all x0 -> x7, waiting for transfers between devices: none -> 56.1 us  [exchange(): return lax.all_to_all(pieces, 'z', 0, 0, tiled=True)]
    ppermute x72 -> x49, waiting for transfers between devices: 256 us -> 205 us  [rotate(): lax.ppermute(value, axis, [(i, (i + by) % size) for i in range(size)])]
    dot_general x12 -> x0, matrix products: 37 us -> none  [the longest x8 32.3 us: project(): jnp.dot(full, weights, preferred_element_type=jnp.float32) * scale]
    all_to_all x0 -> x7, starting transfers between devices: none -> 30.9 us  [exchange(): return lax.all_to_all(pieces, 'z', 0, 0, tiled=True)]
    all_to_all x0 -> x1, blocking collectives: none -> 22.7 us  [exchange(): return lax.all_to_all(pieces, 'z', 0, 0, tiled=True)]
    slice x34 -> x4, local copies, waits for them, and re-layouts: 21.9 us -> 2.76 us  [the longest x1 0.97 us: medium_mix(): before = rotate(kv[:, kv.shape[1] - matrix.shape[1]:], 'y', 1)]
  transfers between devices with their start and end apart: 72 -> 56, of which waited for: 22 -> 28; matrix products, arithmetic and copies ran while one was open for 20% -> 8% of each run, Pallas kernels for 3% -> 14%
where the time goes in v2:
time: 493 us; the launch traced here: 491 us
  waiting for transfers between devices  261 us (53%)
  Pallas kernels  91.1 us (18%)
  starting transfers between devices  66.9 us (14%)
  local copies, waits for them, and re-layouts  36.7 us (7%)
  blocking collectives  22.7 us (5%)
  matrix products  8.63 us (2%)
    ppermute x49, waiting for transfers between devices, rotate(): lax.ppermute(value, axis, [(i, (i + by) % size) for i in range(size)])  205 us
    all_to_all x7, waiting for transfers between devices, exchange(): return lax.all_to_all(pieces, 'z', 0, 0, tiled=True)  56.1 us
    pallas_call x4, Pallas kernels, project(): pl.pallas_call(functools.partial(project_kernel, groups), grid_spec=pltpu...  42 us
    ppermute x49, starting transfers between devices, rotate(): lax.ppermute(value, axis, [(i, (i + by) % size) for i in range(size)])  36 us
    all_to_all x7, starting transfers between devices, exchange(): return lax.all_to_all(pieces, 'z', 0, 0, tiled=True)  30.9 us
    all_to_all x1, blocking collectives, exchange(): return lax.all_to_all(pieces, 'z', 0, 0, tiled=True)  22.7 us
    pallas_call x6, Pallas kernels, split_weights(): pl.pallas_call(split_kernel, grid=(parts,), in_specs=[pl.BlockSpec((1, 1,...  22.2 us
    dynamic_update_slice x8, local copies, waits for them, and re-layouts, placed_rows(): lax.dynamic_update_slice(whole, piece[None, None], (slot, (y_at - j) % y_...  15.9 us
  transfers between devices with their start and end apart: 56, of which 28 were waited for; matrix products, arithmetic and copies ran while one was open for 8% of the time, Pallas kernels for 14%

profile of v2, /device:TPU:0, one launch (start us, length us, event | category | flops | bytes accessed | tf_op | source)
XLA Modules:
  0.0 491.0 jit_solution(13152966661420680566)
XLA Ops:
  6.1 6.3 %all-to-all-start = ((bf16[4,512,256]{2,1,0:T(8,128)(2,1)}), bf16[4,512,256]{2,1,0:T(8,128)(2,1)}, u32[]{:S(2)}, u32[]{:S(2)}) async-start(bf16[4,512,256]{2,1,0:T(8,128)(2,1)} %shard_map.86), calls=%async_computation | async-start | bytes 2097152 | tf_op jit(solution)/shard_map/all_to_all | solution.py:79
  21.2 11.5 %collective-permute-done.1.refs_2_ = bf16[384,1024]{1,0:T(8,128)(2,1)S(1)} collective-permute-done((bf16[384,1024]{1,0:T(8,128)(2,1)S(1)}, bf16[384,1024]{1,0:T(8,128)(2,1)S(1)}, u32[]{:S(2)}, u32[]{:S(2)}) %collective-permute-start.1) | collective-permute-done | bytes 786464 | tf_op jit(solution)/shard_map/ppermute | solution.py:24
  32.7 17.8 %collective-permute-done.3.refs_4_ = bf16[384,1024]{1,0:T(8,128)(2,1)S(1)} collective-permute-done((bf16[384,1024]{1,0:T(8,128)(2,1)S(1)}, bf16[384,1024]{1,0:T(8,128)(2,1)S(1)}, u32[]{:S(2)}, u32[]{:S(2)}) %collective-permute-start.3) | collective-permute-done | bytes 786464 | tf_op jit(solution)/shard_map/ppermute | solution.py:24
  68.9 8.5 %shard_map.88.matrix_ref = bf16[16,128,256]{2,1,0:T(8,128)(2,1)} custom-call(f32[16,1,384]{2,1,0:T(1,128)} %broadcast_in_dim.40.row_ref), custom_call_target="tpu_custom_call" | custom-call | flops 1 | bytes 1 | tf_op jit(solution)/shard_map/pallas_call | solution.py:338
  79.3 17.7 %collective-permute-done.8.refs_8_ = bf16[384,1024]{1,0:T(8,128)(2,1)} collective-permute-done((bf16[384,1024]{1,0:T(8,128)(2,1)S(1)}, bf16[384,1024]{1,0:T(8,128)(2,1)}, u32[]{:S(2)}, u32[]{:S(2)}) %collective-permute-start.8) | collective-permute-done | bytes 786464 | tf_op jit(solution)/shard_map/ppermute | solution.py:24
  110.8 15.1 %collective-permute-done.11.refs_10_ = bf16[384,1024]{1,0:T(8,128)(2,1)} collective-permute-done((bf16[384,1024]{1,0:T(8,128)(2,1)}, bf16[384,1024]{1,0:T(8,128)(2,1)}, u32[]{:S(2)}, u32[]{:S(2)}) %collective-permute-start.11) | collective-permute-done | bytes 786464 | tf_op jit(solution)/shard_map/ppermute | solution.py:24
  125.9 17.4 %collective-permute-done.13.refs_12_ = bf16[384,1024]{1,0:T(8,128)(2,1)} collective-permute-done((bf16[384,1024]{1,0:T(8,128)(2,1)}, bf16[384,1024]{1,0:T(8,128)(2,1)}, u32[]{:S(2)}, u32[]{:S(2)}) %collective-permute-start.13) | collective-permute-done | bytes 786464 | tf_op jit(solution)/shard_map/ppermute | solution.py:24
  154.6 15.1 %collective-permute-done.16.refs_14_ = bf16[384,1024]{1,0:T(8,128)(2,1)} collective-permute-done((bf16[384,1024]{1,0:T(8,128)(2,1)}, bf16[384,1024]{1,0:T(8,128)(2,1)}, u32[]{:S(2)}, u32[]{:S(2)}) %collective-permute-start.16) | collective-permute-done | bytes 786464 | tf_op jit(solution)/shard_map/ppermute | solution.py:24
  178.8 18.6 %shard_map.90 = bf16[1536,768]{1,0:T(8,128)(2,1)} custom-call(s32[6]{0:T(128)S(1)} %stack.75.order_ref, bf16[384,1024]{1,0:T(8,128)(2,1)S(1)} %copy-done.6, bf16[384,1024]{1,0:T(8,128)(2,1)} %collective-permute-done.refs_1_, bf16[384,1024]{1,0:T(8,128)(2,1)S(1)} %collective-permute-done.1.refs_2_, bf16[384,1024]{1,0:T(8,128)(2,1)} %collective-permute-done.2.refs_3_, ...), custom_call_target="tpu_custom_call" | custom-call | tf_op jit(solution)/shard_map/pallas_call | solution.py:172
  206.7 6.1 %shard_map.91 = bf16[4,384,256]{2,1,0:T(8,128)(2,1)} custom-call(s32[3,4]{1,0:T(4,128)} %pad_add_fusion.table_ref, bf16[4,384,768]{2,1,0:T(8,128)(2,1)} %bitcast.91, bf16[4,16,768]{2,1,0:T(8,128)(2,1)} %copy-done.13, f32[3,3,256]{2,1,0:T(4,128)} %bitcast.94, f32[7,256]{1,0:T(8,128)} %reshape.204.taps_ref), custom_call_target="tpu_custom_call" | custom-call | flops 1 | bytes 1 | tf_op jit(solution)/shard_map/pallas_call | solution.py:285
  237.7 21.5 %all-to-all-done.3 = bf16[4,384,256]{2,1,0:T(8,128)(2,1)S(1)} async-done(((bf16[4,384,256]{2,1,0:T(8,128)(2,1)}), bf16[4,384,256]{2,1,0:T(8,128)(2,1)S(1)}, u32[]{:S(2)}, u32[]{:S(2)}) %all-to-all-start.3) | async-done | bytes 786464 | tf_op jit(solution)/shard_map/all_to_all | solution.py:79
  271.9 8.6 %collective-permute-done.21 = bf16[384,1024]{1,0:T(8,128)(2,1)} collective-permute-done((bf16[384,1024]{1,0:T(8,128)(2,1)}, bf16[384,1024]{1,0:T(8,128)(2,1)}, u32[]{:S(2)}, u32[]{:S(2)}) %collective-permute-start.21) | collective-permute-done | bytes 786464 | tf_op jit(solution)/shard_map/ppermute | solution.py:24
  285.8 8.1 %collective-permute-done.28 = bf16[512,1024]{1,0:T(8,128)(2,1)S(1)} collective-permute-done((bf16[512,1024]{1,0:T(8,128)(2,1)}, bf16[512,1024]{1,0:T(8,128)(2,1)S(1)}, u32[]{:S(2)}, u32[]{:S(2)}) %collective-permute-start.28) | collective-permute-done | bytes 1048608 | tf_op jit(solution)/shard_map/ppermute | solution.py:24
  301.2 8.6 %add_convert_fusion.refs_0_ = bf16[384,1024]{1,0:T(8,128)(2,1)} fusion(bf16[384,1024]{1,0:T(8,128)(2,1)S(1)} %copy-done.6, bf16[384,4096]{1,0:T(8,128)(2,1)} %constant_dynamic-update-slice_fusion, bf16[4096,1024]{1,0:T(8,128)(2,1)} %bitcast.92), kind=kOutput, calls=%fused_computation.2 | convolution fusion | flops 3222405120 | bytes 13107200 | tf_op jit(solution)/shard_map/dot_general | solution.py:413
  316.2 8.7 %collective-permute-done.36.refs_9_.refs_5_ = bf16[4,512,256]{2,1,0:T(8,128)(2,1)S(1)} collective-permute-done((bf16[4,512,256]{2,1,0:T(8,128)(2,1)S(1)}, bf16[4,512,256]{2,1,0:T(8,128)(2,1)S(1)}, u32[]{:S(2)}, u32[]{:S(2)}) %collective-permute-start.36) | collective-permute-done | bytes 1048608 | tf_op jit(solution)/shard_map/ppermute | solution.py:24
  324.9 16.8 %all-to-all-done.5.refs_10_.refs_6_ = bf16[4,512,256]{2,1,0:T(8,128)(2,1)} async-done(((bf16[4,512,256]{2,1,0:T(8,128)(2,1)}), bf16[4,512,256]{2,1,0:T(8,128)(2,1)}, u32[]{:S(2)}, u32[]{:S(2)}) %all-to-all-start.5) | async-done | bytes 1048608 | tf_op jit(solution)/shard_map/all_to_all | solution.py:79
  349.0 34.4 %collective-permute-done.39.refs_0_ = bf16[384,1024]{1,0:T(8,128)(2,1)S(1)} collective-permute-done((bf16[384,1024]{1,0:T(8,128)(2,1)}, bf16[384,1024]{1,0:T(8,128)(2,1)S(1)}, u32[]{:S(2)}, u32[]{:S(2)}) %collective-permute-start.39) | collective-permute-done | bytes 786464 | tf_op jit(solution)/shard_map/ppermute | solution.py:24
  388.5 12.5 %collective-permute-done.41.refs_2_ = bf16[384,1024]{1,0:T(8,128)(2,1)} collective-permute-done((bf16[384,1024]{1,0:T(8,128)(2,1)S(1)}, bf16[384,1024]{1,0:T(8,128)(2,1)}, u32[]{:S(2)}, u32[]{:S(2)}) %collective-permute-start.41) | collective-permute-done | bytes 786464 | tf_op jit(solution)/shard_map/ppermute | solution.py:24
  401.5 7.0 %collective-permute-done.43.refs_0_ = bf16[384,1024]{1,0:T(8,128)(2,1)S(1)} collective-permute-done((bf16[384,1024]{1,0:T(8,128)(2,1)S(1)}, bf16[384,1024]{1,0:T(8,128)(2,1)S(1)}, u32[]{:S(2)}, u32[]{:S(2)}) %collective-permute-start.43) | collective-permute-done | bytes 786464 | tf_op jit(solution)/shard_map/ppermute | solution.py:24
  419.6 11.3 %shard_map.96 = bf16[768,768]{1,0:T(8,128)(2,1)} custom-call(s32[6]{0:T(128)S(1)} %stack.75.order_ref, bf16[384,1024]{1,0:T(8,128)(2,1)} %add_convert_fusion.refs_0_, bf16[384,1024]{1,0:T(8,128)(2,1)S(1)} %collective-permute-done.29.refs_1_, bf16[384,1024]{1,0:T(8,128)(2,1)} %collective-permute-done.30.refs_2_, ...), custom_call_target="tpu_custom_call" | custom-call | tf_op jit(solution)/shard_map/pallas_call | solution.py:172
  433.3 6.1 %shard_map.98 = bf16[384,768]{1,0:T(8,128)(2,1)S(1)} custom-call(s32[6]{0:T(128)S(1)} %stack.75.order_ref, bf16[384,1024]{1,0:T(8,128)(2,1)S(1)} %collective-permute-done.43.refs_0_, bf16[384,1024]{1,0:T(8,128)(2,1)S(1)} %collective-permute-done.44.refs_1_, bf16[384,1024]{1,0:T(8,128)(2,1)S(1)} %collective-permute-done.45.refs_2_, ...), custom_call_target="tpu_custom_call" | custom-call | tf_op jit(solution)/shard_map/pallas_call | solution.py:172
  452.0 7.4 %collective-permute-done.48.before_ref = bf16[4,128,256]{2,1,0:T(8,128)(2,1)S(1)} collective-permute-done((bf16[4,128,256]{2,1,0:T(8,128)(2,1)S(1)}, bf16[4,128,256]{2,1,0:T(8,128)(2,1)S(1)}, u32[]{:S(2)}, u32[]{:S(2)}) %collective-permute-start.48) | collective-permute-done | bytes 262176 | tf_op jit(solution)/shard_map/ppermute | solution.py:24
  460.1 7.3 %shard_map.100 = bf16[4,384,256]{2,1,0:T(8,128)(2,1)} custom-call(s32[3,4]{1,0:T(4,128)} %pad_add_fusion.table_ref, f32[4,384,256]{2,1,0:T(8,128)} %get-tuple-element.48.query_ref, bf16[4,384,256]{2,1,0:T(8,128)(2,1)} %get-tuple-element.49.kv_ref, bf16[4,128,256]{2,1,0:T(8,128)(2,1)} %copy-done.12, bf16[16,128,256]{2,1,0:T(8,128)(2,1)} %shard_map.88.matrix_ref), custom_call_target="tpu_custom_call" | custom-call | flops 1 | bytes 1 | tf_op jit(solution)/shard_map/pallas_call | solution.py:315
  467.3 22.7 %all_to_all.40 = bf16[4,384,256]{2,1,0:T(8,128)(2,1)S(1)} all-to-all(bf16[4,384,256]{2,1,0:T(8,128)(2,1)} %shard_map.100), channel_id=1, replica_groups=mesh['z'=4,'y'=2,'x'=2,'c'=2] {'z'}, dimensions={0} | all-to-all | bytes 1572864 | tf_op jit(solution)/shard_map/all_to_all | solution.py:79
  (184 shorter events, 175.1 us)
Async XLA Ops:
  6.1 49.0 %all-to-all-start = ((bf16[4,512,256]{2,1,0:T(8,128)(2,1)}), bf16[4,512,256]{2,1,0:T(8,128)(2,1)}, u32[]{:S(2)}, u32[]{:S(2)}) async-start(bf16[4,512,256]{2,1,0:T(8,128)(2,1)} %shard_map.86), calls=%async_computation | async-start | bytes 2097152 | tf_op jit(solution)/shard_map/all_to_all | solution.py:79
  12.5 38.0 %collective-permute-start.5 = (bf16[512,1024]{1,0:T(8,128)(2,1)}, bf16[512,1024]{1,0:T(8,128)(2,1)}, u32[]{:S(2)}, u32[]{:S(2)}) collective-permute-start(bf16[512,1024]{1,0:T(8,128)(2,1)} %param.13), channel_id=1, source_target_pairs={{0,4},{4,0},{1,5},{5,1},{2,6},{6,2},{3,7},{7,3},{8,12},{12,8},{9,1... | collective-permute-start | bytes 3145736 | tf_op jit(solution)/shard_map/ppermute | solution.py:24
  15.5 35.0 %collective-permute-start.3 = (bf16[384,1024]{1,0:T(8,128)(2,1)S(1)}, bf16[384,1024]{1,0:T(8,128)(2,1)S(1)}, u32[]{:S(2)}, u32[]{:S(2)}) collective-permute-start(bf16[384,1024]{1,0:T(8,128)(2,1)S(1)} %copy-done.6), channel_id=1, source_target_pairs={{0,8},{8,16},{16,24},{24,0},{1,9},{9,17},{17,25},{25,1},{2,10},{10... | collective-permute-start | bytes 2359304 | tf_op jit(solution)/shard_map/ppermute | solution.py:24
  55.1 46.4 %all-to-all-start.1 = ((bf16[4,512,256]{2,1,0:T(8,128)(2,1)}), bf16[4,512,256]{2,1,0:T(8,128)(2,1)}, u32[]{:S(2)}, u32[]{:S(2)}) async-start(bf16[4,512,256]{2,1,0:T(8,128)(2,1)} %shard_map.87), calls=%async_computation.1 | async-start | bytes 2097152 | tf_op jit(solution)/shard_map/all_to_all | solution.py:79
  59.4 37.6 %collective-permute-start.10 = (bf16[4,512,256]{2,1,0:T(8,128)(2,1)}, bf16[4,512,256]{2,1,0:T(8,128)(2,1)}, u32[]{:S(2)}, u32[]{:S(2)}) collective-permute-start(bf16[4,512,256]{2,1,0:T(8,128)(2,1)} %all-to-all-done.refs_16_), channel_id=1, source_target_pairs={{0,4},{4,0},{1,5},{5,1},{2,6},{6,2},{3,7},{7,3},{8,12},{12,8},{9,1... | collective-permute-start | bytes 3145736 | tf_op jit(solution)/shard_map/ppermute | solution.py:24
  62.5 34.5 %collective-permute-start.8 = (bf16[384,1024]{1,0:T(8,128)(2,1)S(1)}, bf16[384,1024]{1,0:T(8,128)(2,1)}, u32[]{:S(2)}, u32[]{:S(2)}) collective-permute-start(bf16[384,1024]{1,0:T(8,128)(2,1)S(1)} %collective-permute-done.3.refs_4_), channel_id=1, source_target_pairs={{0,8},{8,16},{16,24},{24,0},{1,9},{9,17},{17,25},{25,1},{2,10},{10... | collective-permute-start | bytes 2359304 | tf_op jit(solution)/shard_map/ppermute | solution.py:24
  101.6 46.4 %all-to-all-start.2 = ((bf16[4,512,256]{2,1,0:T(8,128)(2,1)}), bf16[4,512,256]{2,1,0:T(8,128)(2,1)}, u32[]{:S(2)}, u32[]{:S(2)}) async-start(bf16[4,512,256]{2,1,0:T(8,128)(2,1)} %shard_map.89), calls=%async_computation.2 | async-start | bytes 2097152 | tf_op jit(solution)/shard_map/all_to_all | solution.py:79
  105.8 37.6 %collective-permute-start.15 = (bf16[4,512,256]{2,1,0:T(8,128)(2,1)}, bf16[4,512,256]{2,1,0:T(8,128)(2,1)}, u32[]{:S(2)}, u32[]{:S(2)}) collective-permute-start(bf16[4,512,256]{2,1,0:T(8,128)(2,1)} %all-to-all-done.1.refs_18_), channel_id=1, source_target_pairs={{0,4},{4,0},{1,5},{5,1},{2,6},{6,2},{3,7},{7,3},{8,12},{12,8},{9,1... | collective-permute-start | bytes 3145736 | tf_op jit(solution)/shard_map/ppermute | solution.py:24
  108.9 34.5 %collective-permute-start.13 = (bf16[384,1024]{1,0:T(8,128)(2,1)}, bf16[384,1024]{1,0:T(8,128)(2,1)}, u32[]{:S(2)}, u32[]{:S(2)}) collective-permute-start(bf16[384,1024]{1,0:T(8,128)(2,1)} %collective-permute-done.8.refs_8_), channel_id=1, source_target_pairs={{0,8},{8,16},{16,24},{24,0},{1,9},{9,17},{17,25},{25,1},{2,10},{10... | collective-permute-start | bytes 2359304 | tf_op jit(solution)/shard_map/ppermute | solution.py:24
  110.8 39.2 %collective-permute-start = (bf16[384,1024]{1,0:T(8,128)(2,1)S(1)}, bf16[384,1024]{1,0:T(8,128)(2,1)}, u32[]{:S(2)}, u32[]{:S(2)}) collective-permute-start(bf16[384,1024]{1,0:T(8,128)(2,1)S(1)} %copy-done.6), channel_id=1, source_target_pairs={{0,1},{1,0},{2,3},{3,2},{4,5},{5,4},{6,7},{7,6},{8,9},{9,8},{10,11... | collective-permute-start | bytes 2359304 | tf_op jit(solution)/shard_map/ppermute | solution.py:24
  151.9 26.2 %collective-permute-start.7 = (bf16[384,1024]{1,0:T(8,128)(2,1)}, bf16[384,1024]{1,0:T(8,128)(2,1)}, u32[]{:S(2)}, u32[]{:S(2)}) collective-permute-start(bf16[384,1024]{1,0:T(8,128)(2,1)} %collective-permute-done.6.refs_6_), channel_id=1, source_target_pairs={{0,1},{1,0},{2,3},{3,2},{4,5},{5,4},{6,7},{7,6},{8,9},{9,8},{10,11... | collective-permute-start | bytes 2359304 | tf_op jit(solution)/shard_map/ppermute | solution.py:24
  178.1 52.5 %collective-permute-start.24 = (bf16[512,1024]{1,0:T(8,128)(2,1)}, bf16[512,1024]{1,0:T(8,128)(2,1)}, u32[]{:S(2)}, u32[]{:S(2)}) collective-permute-start(bf16[512,1024]{1,0:T(8,128)(2,1)} %collective-permute-done.23), channel_id=1, source_target_pairs={{0,4},{4,0},{1,5},{5,1},{2,6},{6,2},{3,7},{7,3},{8,12},{12,8},{9,1... | collective-permute-start | bytes 3145736 | tf_op jit(solution)/shard_map/ppermute | solution.py:24
  178.7 51.9 %collective-permute-start.25 = (bf16[512,1024]{1,0:T(8,128)(2,1)}, bf16[512,1024]{1,0:T(8,128)(2,1)}, u32[]{:S(2)}, u32[]{:S(2)}) collective-permute-start(bf16[512,1024]{1,0:T(8,128)(2,1)} %collective-permute-done.23), channel_id=1, source_target_pairs={{0,8},{8,16},{16,24},{24,0},{1,9},{9,17},{17,25},{25,1},{2,10},{10... | collective-permute-start | bytes 3145736 | tf_op jit(solution)/shard_map/ppermute | solution.py:24
  212.8 46.3 %all-to-all-start.3 = ((bf16[4,384,256]{2,1,0:T(8,128)(2,1)}), bf16[4,384,256]{2,1,0:T(8,128)(2,1)S(1)}, u32[]{:S(2)}, u32[]{:S(2)}) async-start(bf16[4,384,256]{2,1,0:T(8,128)(2,1)} %shard_map.91), calls=%async_computation.3 | async-start | bytes 1572864 | tf_op jit(solution)/shard_map/all_to_all | solution.py:79
  230.6 31.8 %collective-permute-start.26 = (bf16[512,1024]{1,0:T(8,128)(2,1)}, bf16[512,1024]{1,0:T(8,128)(2,1)}, u32[]{:S(2)}, u32[]{:S(2)}) collective-permute-start(bf16[512,1024]{1,0:T(8,128)(2,1)} %collective-permute-done.25), channel_id=1, source_target_pairs={{0,4},{4,0},{1,5},{5,1},{2,6},{6,2},{3,7},{7,3},{8,12},{12,8},{9,1... | collective-permute-start | bytes 3145736 | tf_op jit(solution)/shard_map/ppermute | solution.py:24
  231.1 31.3 %collective-permute-start.27 = (bf16[512,1024]{1,0:T(8,128)(2,1)}, bf16[512,1024]{1,0:T(8,128)(2,1)S(1)}, u32[]{:S(2)}, u32[]{:S(2)}) collective-permute-start(bf16[512,1024]{1,0:T(8,128)(2,1)} %collective-permute-done.25), channel_id=1, source_target_pairs={{0,8},{8,16},{16,24},{24,0},{1,9},{9,17},{17,25},{25,1},{2,10},{10... | collective-permute-start | bytes 3145736 | tf_op jit(solution)/shard_map/ppermute | solution.py:24
  263.4 31.5 %all-to-all-start.4 = ((bf16[4,512,256]{2,1,0:T(8,128)(2,1)}), bf16[4,512,256]{2,1,0:T(8,128)(2,1)S(1)}, u32[]{:S(2)}, u32[]{:S(2)}) async-start(bf16[4,512,256]{2,1,0:T(8,128)(2,1)} %shard_map.93), calls=%async_computation.4 | async-start | bytes 2097152 | tf_op jit(solution)/shard_map/all_to_all | solution.py:79
  294.9 46.7 %all-to-all-start.5 = ((bf16[4,512,256]{2,1,0:T(8,128)(2,1)}), bf16[4,512,256]{2,1,0:T(8,128)(2,1)}, u32[]{:S(2)}, u32[]{:S(2)}) async-start(bf16[4,512,256]{2,1,0:T(8,128)(2,1)} %shard_map.94), calls=%async_computation.5 | async-start | bytes 2097152 | tf_op jit(solution)/shard_map/all_to_all | solution.py:79
  309.9 36.0 %collective-permute-start.32 = (bf16[384,1024]{1,0:T(8,128)(2,1)}, bf16[384,1024]{1,0:T(8,128)(2,1)}, u32[]{:S(2)}, u32[]{:S(2)}) collective-permute-start(bf16[384,1024]{1,0:T(8,128)(2,1)} %add_convert_fusion.refs_0_), channel_id=1, source_target_pairs={{0,8},{8,16},{16,24},{24,0},{1,9},{9,17},{17,25},{25,1},{2,10},{10... | collective-permute-start | bytes 2359304 | tf_op jit(solution)/shard_map/ppermute | solution.py:24
  311.9 34.0 %collective-permute-start.30 = (bf16[384,1024]{1,0:T(8,128)(2,1)}, bf16[384,1024]{1,0:T(8,128)(2,1)}, u32[]{:S(2)}, u32[]{:S(2)}) collective-permute-start(bf16[384,1024]{1,0:T(8,128)(2,1)} %add_convert_fusion.refs_0_), channel_id=1, source_target_pairs={{0,2},{2,0},{1,3},{3,1},{4,6},{6,4},{5,7},{7,5},{8,10},{10,8},{9,1... | collective-permute-start | bytes 2359304 | tf_op jit(solution)/shard_map/ppermute | solution.py:24
  341.7 46.4 %all-to-all-start.6 = ((bf16[4,512,256]{2,1,0:T(8,128)(2,1)}), bf16[4,512,256]{2,1,0:T(8,128)(2,1)}, u32[]{:S(2)}, u32[]{:S(2)}) async-start(bf16[4,512,256]{2,1,0:T(8,128)(2,1)} %shard_map.95), calls=%async_computation.6 | async-start | bytes 2097152 | tf_op jit(solution)/shard_map/all_to_all | solution.py:79
  345.9 37.4 %collective-permute-start.39 = (bf16[384,1024]{1,0:T(8,128)(2,1)}, bf16[384,1024]{1,0:T(8,128)(2,1)S(1)}, u32[]{:S(2)}, u32[]{:S(2)}) collective-permute-start(bf16[384,1024]{1,0:T(8,128)(2,1)} %collective-permute-done.32.refs_4_), channel_id=1, source_target_pairs={{0,8},{8,16},{16,24},{24,0},{1,9},{9,17},{17,25},{25,1},{2,10},{10... | collective-permute-start | bytes 2359304 | tf_op jit(solution)/shard_map/ppermute | solution.py:24
  347.9 35.5 %collective-permute-start.34 = (bf16[384,1024]{1,0:T(8,128)(2,1)}, bf16[384,1024]{1,0:T(8,128)(2,1)}, u32[]{:S(2)}, u32[]{:S(2)}) collective-permute-start(bf16[384,1024]{1,0:T(8,128)(2,1)} %collective-permute-done.32.refs_4_), channel_id=1, source_target_pairs={{0,2},{2,0},{1,3},{3,1},{4,6},{6,4},{5,7},{7,5},{8,10},{10,8},{9,1... | collective-permute-start | bytes 2359304 | tf_op jit(solution)/shard_map/ppermute | solution.py:24
  348.5 35.5 %collective-permute-start.37 = (bf16[4,512,256]{2,1,0:T(8,128)(2,1)}, bf16[4,512,256]{2,1,0:T(8,128)(2,1)}, u32[]{:S(2)}, u32[]{:S(2)}) collective-permute-start(bf16[4,512,256]{2,1,0:T(8,128)(2,1)} %all-to-all-done.5.refs_10_.refs_6_), channel_id=1, source_target_pairs={{0,4},{4,0},{1,5},{5,1},{2,6},{6,2},{3,7},{7,3},{8,12},{12,8},{9,1... | collective-permute-start | bytes 3145736 | tf_op jit(solution)/shard_map/ppermute | solution.py:24
  (48 other events, 882.9 us)

commit v3 on v2

--- a/solution.py
+++ b/solution.py
@@ -8,7 +8,9 @@
 from jax.sharding import Mesh, PartitionSpec as P
 
 AXES = ("z", "y", "x", "c")
+MIB = 2**20
 SHORT_CALL = pl.CostEstimate(flops=1, bytes_accessed=1, transcendentals=0)
+SMALL = pltpu.CompilerParams(vmem_limit_bytes=10 * MIB)
 
 
 def factors(mesh):
@@ -22,16 +24,6 @@
 def rotate(value, axis, by):
     size = lax.axis_size(axis)
     return lax.ppermute(value, axis, [(i, (i + by) % size) for i in range(size)])
-
-
-def blank_kernel(out_ref):
-    del out_ref
-
-
-def blank(shape, dtype):
-    return pl.pallas_call(
-        blank_kernel, out_specs=pl.BlockSpec(memory_space=pl.ANY), out_shape=jax.ShapeDtypeStruct(shape, dtype)
-    )()
 
 
 class Steps:
@@ -71,6 +63,7 @@
         ],
         out_specs=pl.BlockSpec((1, rows, columns), lambda k: (k, 0, 0)),
         cost_estimate=SHORT_CALL,
+        compiler_params=SMALL,
         out_shape=jax.ShapeDtypeStruct((parts, rows, columns), jnp.bfloat16),
     )(in_weight, gain)
 
@@ -94,16 +87,59 @@
     return ((x_at - x_from) % x_size) * c_size + (c_at - c_from) % c_size
 
 
-def placed_rows(found, places, where):
+def joined_kernel(blocks, place_ref, tokens_ref, *refs):
+    firsts, rows = refs[:blocks], refs[blocks:-5]
+    out_ref, first_held, rows_held, first_came, rows_came = refs[-5:]
+    parts = place_ref.shape[0] // 2
+    y_size = len(rows) // parts
+    deep = rows[0].shape[0]
+
+    def first_arrival(r):
+        return pltpu.make_async_copy(firsts[r], first_held.at[r], first_came.at[r])
+
+    def rows_arrival(n):
+        return pltpu.make_async_copy(rows[n], rows_held.at[n], rows_came.at[n])
+
+    for r in range(blocks):
+        first_arrival(r).start()
+    for n in range(len(rows)):
+        rows_arrival(n).start()
+    for r in range(blocks):
+        first_arrival(r).wait()
+    total = tokens_ref[...].astype(jnp.float32)
+    for n in range(len(rows)):
+        rows_arrival(n).wait()
+        begin = pl.multiple_of(place_ref[parts + n % y_size] * deep, deep)
+        total = total + jnp.dot(
+            first_held[place_ref[n // y_size], :, pl.ds(begin, deep)], rows_held[n], preferred_element_type=jnp.float32
+        )
+    out_ref[...] = total.astype(out_ref.dtype)
+
+
+def joined(tokens, first, held, places, where):
     _, y_at, x_at, c_at = where
-    parts, y_size = lax.axis_size("z"), lax.axis_size("y")
-    rows, columns = found[0][0].shape
-    whole = blank((parts, y_size, rows, columns), found[0][0].dtype)
-    for group, place in zip(found, places):
-        slot = slot_of(place, x_at, c_at)
-        for j, piece in enumerate(group):
-            whole = lax.dynamic_update_slice(whole, piece[None, None], (slot, (y_at - j) % y_size, 0, 0))
-    return whole.reshape(parts * y_size * rows, columns)
+    parts, y_size = len(held), len(held[0])
+    place = [slot_of(p, x_at, c_at) for p in places] + [(y_at - j) % y_size for j in range(y_size)]
+    place += [y_at * 0] * (2 * parts - len(place))
+    rows = [w for group in held for w in group]
+    anywhere = pl.BlockSpec(memory_space=pl.ANY)
+    return pl.pallas_call(
+        functools.partial(joined_kernel, len(first)),
+        grid_spec=pltpu.PrefetchScalarGridSpec(
+            num_scalar_prefetch=1,
+            grid=(1,),
+            in_specs=[pl.BlockSpec(tokens.shape, lambda i, place: (0, 0))] + [anywhere] * (len(first) + len(rows)),
+            out_specs=pl.BlockSpec(tokens.shape, lambda i, place: (0, 0)),
+            scratch_shapes=[
+                pltpu.VMEM((len(first),) + first[0].shape, jnp.bfloat16),
+                pltpu.VMEM((len(rows),) + rows[0].shape, jnp.bfloat16),
+                pltpu.SemaphoreType.DMA((len(first),)),
+                pltpu.SemaphoreType.DMA((len(rows),)),
+            ],
+        ),
+        out_shape=jax.ShapeDtypeStruct(tokens.shape, tokens.dtype),
+        compiler_params=pltpu.CompilerParams(vmem_limit_bytes=48 * 2**20),
+    )(jnp.stack(place).astype(jnp.int32), tokens, *first, *rows)
 
 
 def all_of_c(found):
@@ -169,6 +205,7 @@
     pieces = [p for group in found for p in group]
     rows, features_here = pieces[0].shape
     width = flat[0].shape[2]
+    needed = groups[0] * rows * (groups[1] * features_here * 2 + 3 * width * 8 + 512) + 12 * flat[0][0].size * len(flat) // 3
     out = pl.pallas_call(
         functools.partial(project_kernel, groups),
         grid_spec=pltpu.PrefetchScalarGridSpec(
@@ -279,8 +316,11 @@
     return pl.BlockSpec((1,) + value.shape[1:], index)
 
 
-def short_mix(proj, feat, taps, table):
-    before = rotate(proj[:, proj.shape[1] - 16 :], "y", 1)
+def tails(pieces, count):
+    return rotate(pieces[:, pieces.shape[1] - count :], "y", 1)
+
+
+def short_mix(proj, before, feat, taps, table):
     out = jax.ShapeDtypeStruct(proj.shape[:2] + (proj.shape[2] // 3,), jnp.bfloat16)
     return pl.pallas_call(
         short_kernel,
@@ -291,12 +331,13 @@
             out_specs=piece_spec(out, 2),
         ),
         cost_estimate=SHORT_CALL,
+        compiler_params=SMALL,
         out_shape=out,
     )(table, proj, before, feat, taps)
 
 
-def medium_mix(proj, feat, matrix, table):
-    before = rotate(proj[:, proj.shape[1] - 16 :], "y", 1)
+def medium_mix(proj, feat, matrix, table, z_at):
+    before = tails(proj, 16)
     shape = proj.shape[:2] + (proj.shape[2] // 3,)
     query = jax.ShapeDtypeStruct(shape, jnp.float32)
     kv = jax.ShapeDtypeStruct(shape, jnp.bfloat16)
@@ -309,18 +350,34 @@
             out_specs=[piece_spec(query), piece_spec(kv)],
         ),
         cost_estimate=SHORT_CALL,
+        compiler_params=SMALL,
         out_shape=[query, kv],
     )(table, proj, before, feat)
-    before = rotate(kv[:, kv.shape[1] - matrix.shape[1] :], "y", 1)
+    before = tails(kv, matrix.shape[1])
+    parts = proj.shape[0]
+    far = medium(query, kv, before, matrix, table, range(parts // 2, parts))
+    close = medium(query, kv, before, matrix, table, range(parts // 2))
+    made = [close[k] for k in range(parts // 2)] + [far[k] for k in range(parts - parts // 2)]
+    back = [rotate(piece, "z", -k) if k else piece for k, piece in enumerate(made)]
+    stacked = jnp.stack(back)
+    ordered = [lax.dynamic_index_in_dim(stacked, (k - z_at) % parts, 0, keepdims=False) for k in range(parts)]
+    return jnp.concatenate(ordered, axis=1)
+
+
+def medium(query, kv, before, matrix, table, which):
+    count = len(which)
+    table = jnp.concatenate([table[:, which.start : which.stop], jnp.arange(which.start, which.stop, dtype=jnp.int32)[None]])
+    shape = (count,) + kv.shape[1:]
     return pl.pallas_call(
         medium_kernel,
         grid_spec=pltpu.PrefetchScalarGridSpec(
             num_scalar_prefetch=1,
-            grid=(proj.shape[0],),
-            in_specs=[piece_spec(query), piece_spec(kv), piece_spec(before, 0), whole_spec(matrix)],
-            out_specs=piece_spec(kv, 2),
+            grid=(count,),
+            in_specs=[piece_spec(query, 3), piece_spec(kv, 3), piece_spec(before, 0), whole_spec(matrix)],
+            out_specs=piece_spec(kv),
         ),
         cost_estimate=SHORT_CALL,
+        compiler_params=SMALL,
         out_shape=jax.ShapeDtypeStruct(shape, jnp.bfloat16),
     )(table, query, kv, before, matrix)
 
@@ -341,6 +398,7 @@
         in_specs=[pl.BlockSpec((1, 1, 3 * width), lambda g: (g, 0, 0))],
         out_specs=pl.BlockSpec((1, width, 2 * width), lambda g: (g, 0, 0)),
         cost_estimate=SHORT_CALL,
+        compiler_params=SMALL,
         out_shape=jax.ShapeDtypeStruct((groups, width, 2 * width), jnp.bfloat16),
     )(row)
 
@@ -379,6 +437,7 @@
     step = Steps()
     ring, found, came, weights = [tokens], [], [], []
     rows_ring, held = [out_weight], []
+    splits = [split(1, c) for c in range(3)]
     for k in range(parts):
         if k < parts - 1:
             ring.append(step(next_along_z, ring[k]))
@@ -386,48 +445,52 @@
             rows_ring.append(step(next_along_z, out_weight))
         if k < 3:
             came.append(step(exchange, split(0, k)))
-        found.append(others("x", ring[k], step))
+        found.append([others("c", ring[k], step)])
+        fresh = others("x", ring[k], step)[1:]
+        if k:
+            found[k - 1] += [others("c", piece, step) for piece in waiting]
+        waiting = fresh
         if k == 0:
             held.append(others("y", out_weight, step))
         elif k <= 3:
             weights.append(others("y", came[k - 1], step))
-        step.then(*([matrix] if k == 1 else []))
-    proj = project([all_of_c(group) for group in found], weights, order)
-    gated = short_mix(proj, feat[0], short_taps, table)
-    back = home(gated)
-    for k in range(1, parts):
-        if k < parts - 1:
-            rows_ring.append(step(next_along_z, rows_ring[k]))
-            held.append(others("y", rows_ring[k], step))
-            step.then()
-    held.append(others("y", rows_ring[-1], step))
-    came, weights_next = [], []
-    for k in range(4):
-        if k < 3:
-            came.append(step(exchange, split(1, k), back))
-        if k:
-            weights_next.append(others("y", came[k - 1], step))
-        step.then()
-    first = jnp.concatenate(all_of_c(others("x", back, at_once)), axis=1)
-    out_rows = placed_rows(held, places, where)
-    delta = jnp.dot(first, out_rows, preferred_element_type=jnp.float32)
-    stream = (tokens.astype(jnp.float32) + delta).astype(jnp.bfloat16)
-
-    step = Steps()
+        step.then(*([matrix] if k == 1 else splits if k == 2 else []))
+    found[-1] += [others("c", piece, at_once) for piece in waiting]
+    proj = project([sum(group, []) for group in found], weights, order)
+    near = tails(after(proj, *step.gate), 16)
+    for k in range(1, parts - 1):
+        rows_ring.append(step(next_along_z, rows_ring[k]))
+        held.append(others("y", after(rows_ring[k], near) if k == parts - 2 else rows_ring[k], step))
+        step.then(proj)
+    gated = short_mix(proj, near, feat[0], short_taps, table)
+    back = home(after(gated, rows_ring[-1], *held[-1]))
+    held.append(others("y", after(rows_ring[-1], *held[-1]), at_once))
+    first = all_of_c(others("x", after(back, *held[-1]), at_once))
+    step.then(*step.gate, back)
+    came, weights_next = [step(exchange, splits[0])], []
+    came.append(exchange(after(splits[1], came[0], *first)))
+    stream = joined(tokens, first, held, places, where)
+
+    step.then(stream)
     ring, found = [stream], []
     for k in range(parts):
         if k < parts - 1:
             ring.append(step(next_along_z, ring[k]))
-        found.append(others("x", ring[k], step))
+        if k == 1:
+            came.append(step(exchange, splits[2]))
+        found.append([others("c", ring[k], step)])
+        fresh = others("x", ring[k], step)[1:]
+        if k:
+            found[k - 1] += [others("c", piece, step) for piece in waiting]
+        waiting = fresh
+        if k < 3:
+            weights_next.append(others("y", came[k], step))
         step.then()
-    found = [all_of_c(group) for group in found[:-1]] + [found[-1]]
-    proj = [project(found[:2], weights_next, order)]
-    for group in found[2:-1]:
-        proj.append(project([group], weights_next, order))
-    last = found[-1][:1] + [after(p, *proj) for p in found[-1][1:]]
-    proj.append(project([all_of_c(last)], weights_next, order))
-    gated = medium_mix(jnp.concatenate(proj), feat[1], matrix, table)
-    return stream, home(gated)
+    early = [sum(group, []) for group in found[:-1]]
+    proj = [project(early, weights_next, order)]
+    found[-1] += [others("c", after(piece, *proj), at_once) for piece in waiting]
+    proj.append(project([sum(found[-1], [])], weights_next, order))
+    return stream, medium_mix(jnp.concatenate(proj), feat[1], matrix, table, z_at)
 
 
 def solution(mesh):

time: 493 us -> 471 us (0.955)
  blocking collectives: 22.7 us -> 0 us
  Pallas kernels: 91.1 us -> 71 us
  waiting for transfers between devices: 261 us -> 280 us
  starting transfers between devices: 66.9 us -> 80.2 us
  matrix products: 8.63 us -> 0 us
    ppermute x49 -> x52, waiting for transfers between devices: 205 us -> 233 us  [rotate(): lax.ppermute(value, axis, [(i, (i + by) % size) for i in range(size)])]
    all_to_all x1 -> x0, blocking collectives: 22.7 us -> none  [exchange(): return lax.all_to_all(pieces, 'z', 0, 0, tiled=True)]
    unnamed x40 -> x66, local copies, waits for them, and re-layouts: 11.9 us -> 28.6 us
    dynamic_update_slice x8 -> x0, local copies, waits for them, and re-layouts: 15.9 us -> none  [placed_rows(): lax.dynamic_update_slice(whole, piece[None, None], (slot, (y_at - j) % y_...]
    pallas_call x6, Pallas kernels: 22.2 us -> 10.6 us  [split_weights(): pl.pallas_call(split_kernel, grid=(parts,), in_specs=[pl.BlockSpec((1, 1,...]
    ppermute x49 -> x52, starting transfers between devices: 36 us -> 46.7 us  [rotate(): lax.ppermute(value, axis, [(i, (i + by) % size) for i in range(size)])]
    all_to_all x7, waiting for transfers between devices: 56.1 us -> 47.2 us  [exchange(): return lax.all_to_all(pieces, 'z', 0, 0, tiled=True)]
    dot_general x1 -> x0, matrix products: 8.63 us -> none  [local(): delta = jnp.dot(first, out_rows, preferred_element_type=jnp.float32)]
  transfers between devices with their start and end apart: 56 -> 59, of which waited for: 28 -> 36; matrix products, arithmetic and copies ran while one was open for 8% -> 1% of each run, Pallas kernels for 14% -> 12%
where the time goes in v3:
time: 471 us; the launch traced here: 468 us
  waiting for transfers between devices  280 us (59%)
  starting transfers between devices  80.2 us (17%)
  Pallas kernels  71 us (15%)
  local copies, waits for them, and re-layouts  33 us (7%)
    ppermute x52, waiting for transfers between devices, rotate(): lax.ppermute(value, axis, [(i, (i + by) % size) for i in range(size)])  233 us
    all_to_all x7, waiting for transfers between devices, exchange(): return lax.all_to_all(pieces, 'z', 0, 0, tiled=True)  47.2 us
    ppermute x52, starting transfers between devices, rotate(): lax.ppermute(value, axis, [(i, (i + by) % size) for i in range(size)])  46.7 us
    pallas_call x3, Pallas kernels, project(): pl.pallas_call(functools.partial(project_kernel, groups), grid_spec=pltpu...  39.6 us
    all_to_all x7, starting transfers between devices, exchange(): return lax.all_to_all(pieces, 'z', 0, 0, tiled=True)  33.5 us
    unnamed x66, local copies, waits for them, and re-layouts  28.6 us
    pallas_call x6, Pallas kernels, split_weights(): pl.pallas_call(split_kernel, grid=(parts,), in_specs=[pl.BlockSpec((1, 1,...  10.6 us
  transfers between devices with their start and end apart: 59, of which 36 were waited for; matrix products, arithmetic and copies ran while one was open for 1% of the time, Pallas kernels for 12%

profile of v3, /device:TPU:0, one launch (start us, length us, event | category | flops | bytes accessed | tf_op | source)
XLA Modules:
  0.0 468.4 jit_solution(8182414082030741463)
XLA Ops:
  6.4 6.4 %all-to-all-start = ((bf16[4,512,256]{2,1,0:T(8,128)(2,1)}), bf16[4,512,256]{2,1,0:T(8,128)(2,1)}, u32[]{:S(2)}, u32[]{:S(2)}) async-start(bf16[4,512,256]{2,1,0:T(8,128)(2,1)} %shard_map.86), calls=%async_computation | async-start | bytes 2097152 | tf_op jit(solution)/shard_map/all_to_all | solution.py:72
  22.6 11.8 %collective-permute-done.1.refs_2_ = bf16[384,1024]{1,0:T(8,128)(2,1)} collective-permute-done((bf16[384,1024]{1,0:T(8,128)(2,1)S(1)}, bf16[384,1024]{1,0:T(8,128)(2,1)}, u32[]{:S(2)}, u32[]{:S(2)}) %collective-permute-start.1) | collective-permute-done | bytes 786464 | tf_op jit(solution)/shard_map/ppermute | solution.py:26
  34.5 16.5 %collective-permute-done.2.refs_4_ = bf16[384,1024]{1,0:T(8,128)(2,1)} collective-permute-done((bf16[384,1024]{1,0:T(8,128)(2,1)S(1)}, bf16[384,1024]{1,0:T(8,128)(2,1)}, u32[]{:S(2)}, u32[]{:S(2)}) %collective-permute-start.2) | collective-permute-done | bytes 786464 | tf_op jit(solution)/shard_map/ppermute | solution.py:26
  72.2 9.5 %collective-permute-done.6.refs_6_ = bf16[384,1024]{1,0:T(8,128)(2,1)} collective-permute-done((bf16[384,1024]{1,0:T(8,128)(2,1)}, bf16[384,1024]{1,0:T(8,128)(2,1)}, u32[]{:S(2)}, u32[]{:S(2)}) %collective-permute-start.6) | collective-permute-done | bytes 786464 | tf_op jit(solution)/shard_map/ppermute | solution.py:26
  81.7 15.7 %collective-permute-done.7.refs_8_ = bf16[384,1024]{1,0:T(8,128)(2,1)} collective-permute-done((bf16[384,1024]{1,0:T(8,128)(2,1)}, bf16[384,1024]{1,0:T(8,128)(2,1)}, u32[]{:S(2)}, u32[]{:S(2)}) %collective-permute-start.7) | collective-permute-done | bytes 786464 | tf_op jit(solution)/shard_map/ppermute | solution.py:26
  97.4 4.6 all-to-all-done.1.refs_18_
  120.3 7.8 %collective-permute-done.11.refs_10_ = bf16[384,1024]{1,0:T(8,128)(2,1)} collective-permute-done((bf16[384,1024]{1,0:T(8,128)(2,1)}, bf16[384,1024]{1,0:T(8,128)(2,1)}, u32[]{:S(2)}, u32[]{:S(2)}) %collective-permute-start.11) | collective-permute-done | bytes 786464 | tf_op jit(solution)/shard_map/ppermute | solution.py:26
  128.1 15.7 %collective-permute-done.12.refs_12_ = bf16[384,1024]{1,0:T(8,128)(2,1)} collective-permute-done((bf16[384,1024]{1,0:T(8,128)(2,1)}, bf16[384,1024]{1,0:T(8,128)(2,1)}, u32[]{:S(2)}, u32[]{:S(2)}) %collective-permute-start.12) | collective-permute-done | bytes 786464 | tf_op jit(solution)/shard_map/ppermute | solution.py:26
  153.6 16.5 %collective-permute-done.16.refs_14_ = bf16[384,1024]{1,0:T(8,128)(2,1)} collective-permute-done((bf16[384,1024]{1,0:T(8,128)(2,1)}, bf16[384,1024]{1,0:T(8,128)(2,1)}, u32[]{:S(2)}, u32[]{:S(2)}) %collective-permute-start.16) | collective-permute-done | bytes 786464 | tf_op jit(solution)/shard_map/ppermute | solution.py:26
  178.9 18.8 %shard_map.93 = bf16[1536,768]{1,0:T(8,128)(2,1)} custom-call(s32[6]{0:T(128)S(1)} %stack.109.order_ref, bf16[384,1024]{1,0:T(8,128)(2,1)S(1)} %copy-done.12, bf16[384,1024]{1,0:T(8,128)(2,1)S(1)} %collective-permute-done.refs_1_, bf16[384,1024]{1,0:T(8,128)(2,1)} %collective-permute-done.1.refs_2_, bf16[384,1024]{1,0:T(8,128)(2,1)} %collective-permute-done.4.refs_3_, ...), custom_call_target="tpu_custom_call" | custom-call | tf_op jit(solution)/shard_map/pallas_call | solution.py:209
  213.7 14.0 %collective-permute-done.23.refs_10_ = bf16[512,1024]{1,0:T(8,128)(2,1)} collective-permute-done((bf16[512,1024]{1,0:T(8,128)(2,1)}, bf16[512,1024]{1,0:T(8,128)(2,1)}, u32[]{:S(2)}, u32[]{:S(2)}) %collective-permute-start.23) | collective-permute-done | bytes 1048608 | tf_op jit(solution)/shard_map/ppermute | solution.py:26
  228.2 5.1 %all-to-all-start.3 = ((bf16[4,384,256]{2,1,0:T(8,128)(2,1)}), bf16[4,384,256]{2,1,0:T(8,128)(2,1)S(1)}, u32[]{:S(2)}, u32[]{:S(2)}) async-start(bf16[4,384,256]{2,1,0:T(8,128)(2,1)} %shard_map.94), calls=%async_computation.3 | async-start | bytes 1572864 | tf_op jit(solution)/shard_map/all_to_all | solution.py:72
  235.0 17.0 %all-to-all-done.3 = bf16[4,384,256]{2,1,0:T(8,128)(2,1)S(1)} async-done(((bf16[4,384,256]{2,1,0:T(8,128)(2,1)}), bf16[4,384,256]{2,1,0:T(8,128)(2,1)S(1)}, u32[]{:S(2)}, u32[]{:S(2)}) %all-to-all-start.3) | async-done | bytes 786464 | tf_op jit(solution)/shard_map/all_to_all | solution.py:72
  258.3 4.8 %all-to-all-start.4 = ((bf16[4,512,256]{2,1,0:T(8,128)(2,1)}), bf16[4,512,256]{2,1,0:T(8,128)(2,1)S(1)}, u32[]{:S(2)}, u32[]{:S(2)}) async-start(bf16[4,512,256]{2,1,0:T(8,128)(2,1)} %shard_map.90), calls=%async_computation.4 | async-start | bytes 2097152 | tf_op jit(solution)/shard_map/all_to_all | solution.py:72
  263.1 10.7 %collective-permute-done.27.refs_2_ = bf16[384,1024]{1,0:T(8,128)(2,1)} collective-permute-done((bf16[384,1024]{1,0:T(8,128)(2,1)}, bf16[384,1024]{1,0:T(8,128)(2,1)}, u32[]{:S(2)}, u32[]{:S(2)}) %collective-permute-start.27) | collective-permute-done | bytes 786464 | tf_op jit(solution)/shard_map/ppermute | solution.py:26
  274.6 11.0 %all-to-all-done.4.refs_12_.refs_4_ = bf16[4,512,256]{2,1,0:T(8,128)(2,1)S(1)} async-done(((bf16[4,512,256]{2,1,0:T(8,128)(2,1)}), bf16[4,512,256]{2,1,0:T(8,128)(2,1)S(1)}, u32[]{:S(2)}, u32[]{:S(2)}) %all-to-all-start.4) | async-done | bytes 1048608 | tf_op jit(solution)/shard_map/all_to_all | solution.py:72
  294.0 7.0 %shard_map.95.refs_0_ = bf16[384,1024]{1,0:T(8,128)(2,1)} custom-call(s32[8]{0:T(128)S(1)} %stack.91.place_ref, bf16[384,1024]{1,0:T(8,128)(2,1)S(1)} %copy-done.12, bf16[384,1024]{1,0:T(8,128)(2,1)} %pad_maximum_fusion.1.refs_0_, bf16[384,1024]{1,0:T(8,128)(2,1)S(1)} %copy-done.24, bf16[384,1024]{1,0:T(8,128)(2,1)} %collective-permute-done.27.refs_2_, ...), custom_call_target="tpu_custom_call" | custom-call | tf_op jit(solution)/shard_map/pallas_call | solution.py:126
  304.8 21.7 %collective-permute-done.31.refs_4_ = bf16[384,1024]{1,0:T(8,128)(2,1)} collective-permute-done((bf16[384,1024]{1,0:T(8,128)(2,1)}, bf16[384,1024]{1,0:T(8,128)(2,1)}, u32[]{:S(2)}, u32[]{:S(2)}) %collective-permute-start.31) | collective-permute-done | bytes 786464 | tf_op jit(solution)/shard_map/ppermute | solution.py:26
  339.9 33.2 %collective-permute-done.36.refs_8_ = bf16[384,1024]{1,0:T(8,128)(2,1)} collective-permute-done((bf16[384,1024]{1,0:T(8,128)(2,1)}, bf16[384,1024]{1,0:T(8,128)(2,1)}, u32[]{:S(2)}, u32[]{:S(2)}) %collective-permute-start.36) | collective-permute-done | bytes 786464 | tf_op jit(solution)/shard_map/ppermute | solution.py:26
  380.5 19.0 %collective-permute-done.41.refs_0_ = bf16[384,1024]{1,0:T(8,128)(2,1)S(1)} collective-permute-done((bf16[384,1024]{1,0:T(8,128)(2,1)}, bf16[384,1024]{1,0:T(8,128)(2,1)S(1)}, u32[]{:S(2)}, u32[]{:S(2)}) %collective-permute-start.41) | collective-permute-done | bytes 786464 | tf_op jit(solution)/shard_map/ppermute | solution.py:26
  409.7 14.8 %shard_map.96 = bf16[1152,768]{1,0:T(8,128)(2,1)} custom-call(s32[6]{0:T(128)S(1)} %stack.109.order_ref, bf16[384,1024]{1,0:T(8,128)(2,1)S(1)} %copy-done.13, bf16[384,1024]{1,0:T(8,128)(2,1)S(1)} %copy-done.18, bf16[384,1024]{1,0:T(8,128)(2,1)} %collective-permute-done.30.refs_2_, bf16[384,1024]{1,0:T(8,128)(2,1)S(1)} %copy-done.22, ...), custom_call_target="tpu_custom_call" | custom-call | tf_op jit(solution)/shard_map/pallas_call | solution.py:209
  428.0 6.1 %shard_map.97 = bf16[384,768]{1,0:T(8,128)(2,1)S(1)} custom-call(s32[6]{0:T(128)S(1)} %stack.109.order_ref, bf16[384,1024]{1,0:T(8,128)(2,1)S(1)} %collective-permute-done.41.refs_0_, bf16[384,1024]{1,0:T(8,128)(2,1)S(1)} %collective-permute-done.44.refs_1_, bf16[384,1024]{1,0:T(8,128)(2,1)S(1)} %collective-permute-done.45.refs_2_, ...), custom_call_target="tpu_custom_call" | custom-call | tf_op jit(solution)/shard_map/pallas_call | solution.py:209
  443.2 5.8 %collective-permute-done.48.before_ref = bf16[4,128,256]{2,1,0:T(8,128)(2,1)S(1)} collective-permute-done((bf16[4,128,256]{2,1,0:T(8,128)(2,1)S(1)}, bf16[4,128,256]{2,1,0:T(8,128)(2,1)S(1)}, u32[]{:S(2)}, u32[]{:S(2)}) %collective-permute-start.48) | collective-permute-done | bytes 262176 | tf_op jit(solution)/shard_map/ppermute | solution.py:26
  461.4 5.9 %collective-permute-done.50 = bf16[384,256]{1,0:T(8,128)(2,1)S(1)} collective-permute-done((bf16[384,256]{1,0:T(8,128)(2,1)S(1)}, bf16[384,256]{1,0:T(8,128)(2,1)S(1)}, u32[]{:S(2)}, u32[]{:S(2)}) %collective-permute-start.50) | collective-permute-done | bytes 196640 | tf_op jit(solution)/shard_map/ppermute | solution.py:26
  (215 shorter events, 167.8 us)
Async XLA Ops:
  6.4 49.1 %all-to-all-start = ((bf16[4,512,256]{2,1,0:T(8,128)(2,1)}), bf16[4,512,256]{2,1,0:T(8,128)(2,1)}, u32[]{:S(2)}, u32[]{:S(2)}) async-start(bf16[4,512,256]{2,1,0:T(8,128)(2,1)} %shard_map.86), calls=%async_computation | async-start | bytes 2097152 | tf_op jit(solution)/shard_map/all_to_all | solution.py:72
  12.9 38.1 %collective-permute-start.3 = (bf16[512,1024]{1,0:T(8,128)(2,1)}, bf16[512,1024]{1,0:T(8,128)(2,1)S(1)}, u32[]{:S(2)}, u32[]{:S(2)}) collective-permute-start(bf16[512,1024]{1,0:T(8,128)(2,1)} %refs_4_.1), channel_id=1, source_target_pairs={{0,4},{4,0},{1,5},{5,1},{2,6},{6,2},{3,7},{7,3},{8,12},{12,8},{9,1... | collective-permute-start | bytes 3145736 | tf_op jit(solution)/shard_map/ppermute | solution.py:26
  15.9 35.1 %collective-permute-start.2 = (bf16[384,1024]{1,0:T(8,128)(2,1)S(1)}, bf16[384,1024]{1,0:T(8,128)(2,1)}, u32[]{:S(2)}, u32[]{:S(2)}) collective-permute-start(bf16[384,1024]{1,0:T(8,128)(2,1)S(1)} %copy-done.12), channel_id=1, source_target_pairs={{0,8},{8,16},{16,24},{24,0},{1,9},{9,17},{17,25},{25,1},{2,10},{10... | collective-permute-start | bytes 2359304 | tf_op jit(solution)/shard_map/ppermute | solution.py:26
  55.5 46.4 %all-to-all-start.1 = ((bf16[4,512,256]{2,1,0:T(8,128)(2,1)}), bf16[4,512,256]{2,1,0:T(8,128)(2,1)}, u32[]{:S(2)}, u32[]{:S(2)}) async-start(bf16[4,512,256]{2,1,0:T(8,128)(2,1)} %shard_map.87), calls=%async_computation.1 | async-start | bytes 2097152 | tf_op jit(solution)/shard_map/all_to_all | solution.py:72
  59.8 37.6 %collective-permute-start.8 = (bf16[4,512,256]{2,1,0:T(8,128)(2,1)}, bf16[4,512,256]{2,1,0:T(8,128)(2,1)}, u32[]{:S(2)}, u32[]{:S(2)}) collective-permute-start(bf16[4,512,256]{2,1,0:T(8,128)(2,1)} %all-to-all-done.refs_16_), channel_id=1, source_target_pairs={{0,4},{4,0},{1,5},{5,1},{2,6},{6,2},{3,7},{7,3},{8,12},{12,8},{9,1... | collective-permute-start | bytes 3145736 | tf_op jit(solution)/shard_map/ppermute | solution.py:26
  63.4 34.0 %collective-permute-start.7 = (bf16[384,1024]{1,0:T(8,128)(2,1)}, bf16[384,1024]{1,0:T(8,128)(2,1)}, u32[]{:S(2)}, u32[]{:S(2)}) collective-permute-start(bf16[384,1024]{1,0:T(8,128)(2,1)} %collective-permute-done.2.refs_4_), channel_id=1, source_target_pairs={{0,8},{8,16},{16,24},{24,0},{1,9},{9,17},{17,25},{25,1},{2,10},{10... | collective-permute-start | bytes 2359304 | tf_op jit(solution)/shard_map/ppermute | solution.py:26
  102.0 46.4 %all-to-all-start.2 = ((bf16[4,512,256]{2,1,0:T(8,128)(2,1)}), bf16[4,512,256]{2,1,0:T(8,128)(2,1)}, u32[]{:S(2)}, u32[]{:S(2)}) async-start(bf16[4,512,256]{2,1,0:T(8,128)(2,1)} %shard_map.89), calls=%async_computation.2 | async-start | bytes 2097152 | tf_op jit(solution)/shard_map/all_to_all | solution.py:72
  106.2 37.6 %collective-permute-start.13 = (bf16[4,512,256]{2,1,0:T(8,128)(2,1)}, bf16[4,512,256]{2,1,0:T(8,128)(2,1)}, u32[]{:S(2)}, u32[]{:S(2)}) collective-permute-start(bf16[4,512,256]{2,1,0:T(8,128)(2,1)} %all-to-all-done.1.refs_18_), channel_id=1, source_target_pairs={{0,4},{4,0},{1,5},{5,1},{2,6},{6,2},{3,7},{7,3},{8,12},{12,8},{9,1... | collective-permute-start | bytes 3145736 | tf_op jit(solution)/shard_map/ppermute | solution.py:26
  109.8 34.0 %collective-permute-start.12 = (bf16[384,1024]{1,0:T(8,128)(2,1)}, bf16[384,1024]{1,0:T(8,128)(2,1)}, u32[]{:S(2)}, u32[]{:S(2)}) collective-permute-start(bf16[384,1024]{1,0:T(8,128)(2,1)} %collective-permute-done.7.refs_8_), channel_id=1, source_target_pairs={{0,8},{8,16},{16,24},{24,0},{1,9},{9,17},{17,25},{25,1},{2,10},{10... | collective-permute-start | bytes 2359304 | tf_op jit(solution)/shard_map/ppermute | solution.py:26
  148.3 24.4 %collective-permute-start.18 = (bf16[4,512,256]{2,1,0:T(8,128)(2,1)}, bf16[4,512,256]{2,1,0:T(8,128)(2,1)}, u32[]{:S(2)}, u32[]{:S(2)}) collective-permute-start(bf16[4,512,256]{2,1,0:T(8,128)(2,1)} %all-to-all-done.2.refs_20_), channel_id=1, source_target_pairs={{0,4},{4,0},{1,5},{5,1},{2,6},{6,2},{3,7},{7,3},{8,12},{12,8},{9,1... | collective-permute-start | bytes 3145736 | tf_op jit(solution)/shard_map/ppermute | solution.py:26
  149.9 25.9 %collective-permute-start.19 = (bf16[512,1024]{1,0:T(8,128)(2,1)}, bf16[512,1024]{1,0:T(8,128)(2,1)}, u32[]{:S(2)}, u32[]{:S(2)}) collective-permute-start(bf16[512,1024]{1,0:T(8,128)(2,1)} %refs_4_.1), channel_id=1, source_target_pairs={{0,8},{8,16},{16,24},{24,0},{1,9},{9,17},{17,25},{25,1},{2,10},{10... | collective-permute-start | bytes 3145736 | tf_op jit(solution)/shard_map/ppermute | solution.py:26
  175.8 25.0 %collective-permute-start.21 = (bf16[512,1024]{1,0:T(8,128)(2,1)}, bf16[512,1024]{1,0:T(8,128)(2,1)}, u32[]{:S(2)}, u32[]{:S(2)}) collective-permute-start(bf16[512,1024]{1,0:T(8,128)(2,1)} %collective-permute-done.19.refs_6_), channel_id=1, source_target_pairs={{0,8},{8,16},{16,24},{24,0},{1,9},{9,17},{17,25},{25,1},{2,10},{10... | collective-permute-start | bytes 3145736 | tf_op jit(solution)/shard_map/ppermute | solution.py:26
  175.8 25.0 %collective-permute-start.22 = (bf16[512,1024]{1,0:T(8,128)(2,1)}, bf16[512,1024]{1,0:T(8,128)(2,1)}, u32[]{:S(2)}, u32[]{:S(2)}) collective-permute-start(bf16[512,1024]{1,0:T(8,128)(2,1)} %collective-permute-done.19.refs_6_), channel_id=1, source_target_pairs={{0,4},{4,0},{1,5},{5,1},{2,6},{6,2},{3,7},{7,3},{8,12},{12,8},{9,1... | collective-permute-start | bytes 3145736 | tf_op jit(solution)/shard_map/ppermute | solution.py:26
  200.8 26.9 %collective-permute-start.23 = (bf16[512,1024]{1,0:T(8,128)(2,1)}, bf16[512,1024]{1,0:T(8,128)(2,1)}, u32[]{:S(2)}, u32[]{:S(2)}) collective-permute-start(bf16[512,1024]{1,0:T(8,128)(2,1)} %collective-permute-done.21.refs_8_), channel_id=1, source_target_pairs={{0,8},{8,16},{16,24},{24,0},{1,9},{9,17},{17,25},{25,1},{2,10},{10... | collective-permute-start | bytes 3145736 | tf_op jit(solution)/shard_map/ppermute | solution.py:26
  203.5 24.7 %collective-permute-start.24 = (bf16[512,1024]{1,0:T(8,128)(2,1)}, bf16[512,1024]{1,0:T(8,128)(2,1)}, u32[]{:S(2)}, u32[]{:S(2)}) collective-permute-start(bf16[512,1024]{1,0:T(8,128)(2,1)} %collective-permute-done.21.refs_8_), channel_id=1, source_target_pairs={{0,4},{4,0},{1,5},{5,1},{2,6},{6,2},{3,7},{7,3},{8,12},{12,8},{9,1... | collective-permute-start | bytes 3145736 | tf_op jit(solution)/shard_map/ppermute | solution.py:26
  258.3 27.3 %all-to-all-start.4 = ((bf16[4,512,256]{2,1,0:T(8,128)(2,1)}), bf16[4,512,256]{2,1,0:T(8,128)(2,1)S(1)}, u32[]{:S(2)}, u32[]{:S(2)}) async-start(bf16[4,512,256]{2,1,0:T(8,128)(2,1)} %shard_map.90), calls=%async_computation.4 | async-start | bytes 2097152 | tf_op jit(solution)/shard_map/all_to_all | solution.py:72
  285.6 45.6 %all-to-all-start.6 = ((bf16[4,512,256]{2,1,0:T(8,128)(2,1)}), bf16[4,512,256]{2,1,0:T(8,128)(2,1)}, u32[]{:S(2)}, u32[]{:S(2)}) async-start(bf16[4,512,256]{2,1,0:T(8,128)(2,1)} %shard_map.91), calls=%async_computation.6 | async-start | bytes 2097152 | tf_op jit(solution)/shard_map/all_to_all | solution.py:72
  301.0 26.4 %collective-permute-start.32 = (bf16[4,512,256]{2,1,0:T(8,128)(2,1)S(1)}, bf16[4,512,256]{2,1,0:T(8,128)(2,1)S(1)}, u32[]{:S(2)}, u32[]{:S(2)}) collective-permute-start(bf16[4,512,256]{2,1,0:T(8,128)(2,1)S(1)} %all-to-all-done.4.refs_12_.refs_4_), channel_id=1, source_target_pairs={{0,4},{4,0},{1,5},{5,1},{2,6},{6,2},{3,7},{7,3},{8,12},{12,8},{9,1... | collective-permute-start | bytes 3145736 | tf_op jit(solution)/shard_map/ppermute | solution.py:26
  331.2 46.4 %all-to-all-start.5 = ((bf16[4,512,256]{2,1,0:T(8,128)(2,1)}), bf16[4,512,256]{2,1,0:T(8,128)(2,1)}, u32[]{:S(2)}, u32[]{:S(2)}) async-start(bf16[4,512,256]{2,1,0:T(8,128)(2,1)} %copy-done.11), calls=%async_computation.5 | async-start | bytes 2097152 | tf_op jit(solution)/shard_map/all_to_all | solution.py:72
  335.5 42.1 %collective-permute-start.37 = (bf16[4,512,256]{2,1,0:T(8,128)(2,1)}, bf16[4,512,256]{2,1,0:T(8,128)(2,1)}, u32[]{:S(2)}, u32[]{:S(2)}) collective-permute-start(bf16[4,512,256]{2,1,0:T(8,128)(2,1)} %all-to-all-done.6.refs_14_.refs_6_), channel_id=1, source_target_pairs={{0,4},{4,0},{1,5},{5,1},{2,6},{6,2},{3,7},{7,3},{8,12},{12,8},{9,1... | collective-permute-start | bytes 3145736 | tf_op jit(solution)/shard_map/ppermute | solution.py:26
  337.2 35.8 %collective-permute-start.36 = (bf16[384,1024]{1,0:T(8,128)(2,1)}, bf16[384,1024]{1,0:T(8,128)(2,1)}, u32[]{:S(2)}, u32[]{:S(2)}) collective-permute-start(bf16[384,1024]{1,0:T(8,128)(2,1)} %collective-permute-done.31.refs_4_), channel_id=1, source_target_pairs={{0,8},{8,16},{16,24},{24,0},{1,9},{9,17},{17,25},{25,1},{2,10},{10... | collective-permute-start | bytes 2359304 | tf_op jit(solution)/shard_map/ppermute | solution.py:26
  339.1 33.9 %collective-permute-start.34 = (bf16[384,1024]{1,0:T(8,128)(2,1)}, bf16[384,1024]{1,0:T(8,128)(2,1)S(1)}, u32[]{:S(2)}, u32[]{:S(2)}) collective-permute-start(bf16[384,1024]{1,0:T(8,128)(2,1)} %collective-permute-done.31.refs_4_), channel_id=1, source_target_pairs={{0,1},{1,0},{2,3},{3,2},{4,5},{5,4},{6,7},{7,6},{8,9},{9,8},{10,11... | collective-permute-start | bytes 2359304 | tf_op jit(solution)/shard_map/ppermute | solution.py:26
  339.1 34.8 %collective-permute-start.35 = (bf16[384,1024]{1,0:T(8,128)(2,1)}, bf16[384,1024]{1,0:T(8,128)(2,1)}, u32[]{:S(2)}, u32[]{:S(2)}) collective-permute-start(bf16[384,1024]{1,0:T(8,128)(2,1)} %collective-permute-done.31.refs_4_), channel_id=1, source_target_pairs={{0,2},{2,0},{1,3},{3,1},{4,6},{6,4},{5,7},{7,5},{8,10},{10,8},{9,1... | collective-permute-start | bytes 2359304 | tf_op jit(solution)/shard_map/ppermute | solution.py:26
  339.6 34.3 %collective-permute-start.33 = (bf16[384,1024]{1,0:T(8,128)(2,1)}, bf16[384,1024]{1,0:T(8,128)(2,1)S(1)}, u32[]{:S(2)}, u32[]{:S(2)}) collective-permute-start(bf16[384,1024]{1,0:T(8,128)(2,1)} %collective-permute-done.30.refs_2_), channel_id=1, source_target_pairs={{0,1},{1,0},{2,3},{3,2},{4,5},{5,4},{6,7},{7,6},{8,9},{9,8},{10,11... | collective-permute-start | bytes 2359304 | tf_op jit(solution)/shard_map/ppermute | solution.py:26
  (67 other events, 843.2 us)

commit v4 on v3

--- a/solution.py
+++ b/solution.py
@@ -63,7 +63,7 @@
         ],
         out_specs=pl.BlockSpec((1, rows, columns), lambda k: (k, 0, 0)),
         cost_estimate=SHORT_CALL,
-        compiler_params=SMALL,
+        compiler_params=pltpu.CompilerParams(vmem_limit_bytes=10 * MIB),
         out_shape=jax.ShapeDtypeStruct((parts, rows, columns), jnp.bfloat16),
     )(in_weight, gain)
 
@@ -138,7 +138,7 @@
             ],
         ),
         out_shape=jax.ShapeDtypeStruct(tokens.shape, tokens.dtype),
-        compiler_params=pltpu.CompilerParams(vmem_limit_bytes=48 * 2**20),
+        compiler_params=pltpu.CompilerParams(vmem_limit_bytes=60 * MIB),
     )(jnp.stack(place).astype(jnp.int32), tokens, *first, *rows)
 
 
@@ -222,7 +222,7 @@
             ],
         ),
         out_shape=jax.ShapeDtypeStruct((groups[0] * rows, 3 * width), jnp.bfloat16),
-        compiler_params=pltpu.CompilerParams(vmem_limit_bytes=48 * 2**20),
+        compiler_params=pltpu.CompilerParams(vmem_limit_bytes=60 * MIB),
     )(order, *pieces, *flat)
     return out.reshape(groups[0], rows, 3 * width)
 
@@ -328,7 +328,7 @@
             num_scalar_prefetch=1,
             grid=(proj.shape[0],),
             in_specs=[piece_spec(proj), piece_spec(before, 0), whole_spec(feat), whole_spec(taps)],
-            out_specs=piece_spec(out, 2),
+            out_specs=piece_spec(out),
         ),
         cost_estimate=SHORT_CALL,
         compiler_params=SMALL,
@@ -336,12 +336,11 @@
     )(table, proj, before, feat, taps)
 
 
-def medium_mix(proj, feat, matrix, table, z_at):
-    before = tails(proj, 16)
+def gate(proj, before, feat, table):
     shape = proj.shape[:2] + (proj.shape[2] // 3,)
     query = jax.ShapeDtypeStruct(shape, jnp.float32)
     kv = jax.ShapeDtypeStruct(shape, jnp.bfloat16)
-    query, kv = pl.pallas_call(
+    return pl.pallas_call(
         gate_kernel,
         grid_spec=pltpu.PrefetchScalarGridSpec(
             num_scalar_prefetch=1,
@@ -353,27 +352,33 @@
         compiler_params=SMALL,
         out_shape=[query, kv],
     )(table, proj, before, feat)
-    before = tails(kv, matrix.shape[1])
-    parts = proj.shape[0]
-    far = medium(query, kv, before, matrix, table, range(parts // 2, parts))
-    close = medium(query, kv, before, matrix, table, range(parts // 2))
-    made = [close[k] for k in range(parts // 2)] + [far[k] for k in range(parts - parts // 2)]
-    back = [rotate(piece, "z", -k) if k else piece for k, piece in enumerate(made)]
-    stacked = jnp.stack(back)
-    ordered = [lax.dynamic_index_in_dim(stacked, (k - z_at) % parts, 0, keepdims=False) for k in range(parts)]
-    return jnp.concatenate(ordered, axis=1)
-
-
-def medium(query, kv, before, matrix, table, which):
-    count = len(which)
-    table = jnp.concatenate([table[:, which.start : which.stop], jnp.arange(which.start, which.stop, dtype=jnp.int32)[None]])
+
+
+def medium_mix(early, last, feat, matrix, table, z_at):
+    parts, span = table.shape[1], matrix.shape[1]
+    near_early, near_last = tails(early, 16), tails(last, 16)
+    inside = jnp.minimum(table[:, : parts - 1], parts - 2)
+    query, kv = gate(after(early, last), near_early, feat, inside)
+    far_early = tails(kv, span)
+    close = medium(query, kv, far_early, matrix, table[:, : parts - 2])
+    made = [close[k] for k in range(parts - 2)]
+    query, kv = gate(
+        jnp.concatenate([early[-1:], last]), jnp.concatenate([near_early, near_last]), feat, table[:, parts - 2 :]
+    )
+    far = jnp.concatenate([far_early, tails(kv[1:], span)])
+    distant = medium(query, kv, far, matrix, table[:, parts - 2 :])
+    return home(made + [distant[0], distant[1]], z_at)
+
+
+def medium(query, kv, before, matrix, table):
+    count = table.shape[1]
     shape = (count,) + kv.shape[1:]
     return pl.pallas_call(
         medium_kernel,
         grid_spec=pltpu.PrefetchScalarGridSpec(
             num_scalar_prefetch=1,
             grid=(count,),
-            in_specs=[piece_spec(query, 3), piece_spec(kv, 3), piece_spec(before, 0), whole_spec(matrix)],
+            in_specs=[piece_spec(query), piece_spec(kv), piece_spec(before, 0), whole_spec(matrix)],
             out_specs=piece_spec(kv),
         ),
         cost_estimate=SHORT_CALL,
@@ -408,9 +413,11 @@
     return lax.dynamic_slice_in_dim(value, z_at * size, size, axis)
 
 
-def home(pieces):
-    back = exchange(pieces)
-    return jnp.concatenate([back[k] for k in range(back.shape[0])], axis=1)
+def home(pieces, z_at):
+    parts = len(pieces)
+    stacked = jnp.stack([rotate(piece, "z", -k) if k else piece for k, piece in enumerate(pieces)])
+    ordered = [lax.dynamic_index_in_dim(stacked, (k - z_at) % parts, 0, keepdims=False) for k in range(parts)]
+    return jnp.concatenate(ordered, axis=1)
 
 
 def local(tokens, norm_gain, in_weight, feat_filter, short_filter, medium_filter, out_weight):
@@ -463,34 +470,56 @@
         held.append(others("y", after(rows_ring[k], near) if k == parts - 2 else rows_ring[k], step))
         step.then(proj)
     gated = short_mix(proj, near, feat[0], short_taps, table)
-    back = home(after(gated, rows_ring[-1], *held[-1]))
+    gated = after(gated, rows_ring[-1], *held[-1])
+    back = home([gated[k] for k in range(parts)], z_at)
     held.append(others("y", after(rows_ring[-1], *held[-1]), at_once))
-    first = all_of_c(others("x", after(back, *held[-1]), at_once))
+    first = all_of_c([after(piece, *held[-1]) for piece in others("x", back, at_once)])
     step.then(*step.gate, back)
     came, weights_next = [step(exchange, splits[0])], []
     came.append(exchange(after(splits[1], came[0], *first)))
     stream = joined(tokens, first, held, places, where)
 
     step.then(stream)
-    ring, found = [stream], []
-    for k in range(parts):
-        if k < parts - 1:
-            ring.append(step(next_along_z, ring[k]))
-        if k == 1:
-            came.append(step(exchange, splits[2]))
+    ring, found, swapped = [stream], [], []
+
+    def swap(k):
         found.append([others("c", ring[k], step)])
-        fresh = others("x", ring[k], step)[1:]
-        if k:
-            found[k - 1] += [others("c", piece, step) for piece in waiting]
-        waiting = fresh
-        if k < 3:
-            weights_next.append(others("y", came[k], step))
+        swapped.append(others("x", ring[k], step)[1:])
+
+    def spread(k):
+        found[k] += [others("c", piece, step) for piece in swapped[k]]
+
+    ring.append(step(next_along_z, ring[0]))
+    weights_next.append(others("y", came[0], step))
+    swap(0)
+    step.then()
+    came.append(step(exchange, splits[2]))
+    weights_next.append(others("y", came[1], step))
+    swap(1)
+    spread(0)
+    step.then()
+    for k in range(2, parts):
+        ring.append(step(next_along_z, ring[k - 1]))
+        if k == 2:
+            weights_next.append(others("y", came[2], functools.partial(step, wait=False)))
+        else:
+            swap(k - 1)
+        spread(k - 1 if k == 2 else k - 2) if k != 3 else None
         step.then()
-    early = [sum(group, []) for group in found[:-1]]
-    proj = [project(early, weights_next, order)]
-    found[-1] += [others("c", after(piece, *proj), at_once) for piece in waiting]
-    proj.append(project([sum(found[-1], [])], weights_next, order))
-    return stream, medium_mix(jnp.concatenate(proj), feat[1], matrix, table, z_at)
+    early = project([sum(group, []) for group in found[:2]], weights_next, order)
+    step.then(*step.gate, early)
+    spread(parts - 2)
+    count = stream.shape[0]
+    half = count // 2
+    near_half = others("x", ring[-1][:half], step)[1:]
+    far_half = [step(next_along_z, piece[half:]) for piece in swapped[-1]]
+    halves = [[others("c", ring[-1][:half], at_once)], [others("c", ring[-1][half:], at_once)]]
+    early = [early] + [project([sum(group, [])], weights_next, order) for group in found[2:]]
+    early = jnp.concatenate(early)
+    for group, more in zip(halves, (near_half, far_half)):
+        group += [others("c", after(piece, early), at_once) for piece in more]
+    last = project([sum(group, []) for group in halves], weights_next, order).reshape(1, count, -1)
+    return stream, medium_mix(early, last, feat[1], matrix, table, z_at)
 
 
 def solution(mesh):

time: 471 us -> 456 us (0.968)
  waiting for transfers between devices: 280 us -> 253 us
  Pallas kernels: 71 us -> 83.7 us
  local copies, waits for them, and re-layouts: 33 us -> 27.8 us
    all_to_all x7 -> x6, waiting for transfers between devices: 47.2 us -> 29.8 us  [exchange(): return lax.all_to_all(pieces, 'z', 0, 0, tiled=True)]
    unnamed x66 -> x68, local copies, waits for them, and re-layouts: 28.6 us -> 18.3 us
    ppermute x52 -> x60, waiting for transfers between devices: 233 us -> 224 us  [rotate(): lax.ppermute(value, axis, [(i, (i + by) % size) for i in range(size)])]
    pallas_call x3 -> x4, Pallas kernels: 39.6 us -> 47.2 us  [project(): pl.pallas_call(functools.partial(project_kernel, groups), grid_spec=pltpu...]
    ppermute x52 -> x60, starting transfers between devices: 46.7 us -> 53.8 us  [rotate(): lax.ppermute(value, axis, [(i, (i + by) % size) for i in range(size)])]
    all_to_all x7 -> x6, starting transfers between devices: 33.5 us -> 28.5 us  [exchange(): return lax.all_to_all(pieces, 'z', 0, 0, tiled=True)]
  transfers between devices with their start and end apart: 59 -> 66, of which waited for: 36 -> 38; matrix products, arithmetic and copies ran while one was open for 1% -> 3% of each run, Pallas kernels for 12% -> 17%
where the time goes in v4:
time: 456 us; the launch traced here: 453 us
  waiting for transfers between devices  253 us (55%)
  Pallas kernels  83.7 us (18%)
  starting transfers between devices  82.3 us (18%)
  local copies, waits for them, and re-layouts  27.8 us (6%)
    ppermute x60, waiting for transfers between devices, rotate(): lax.ppermute(value, axis, [(i, (i + by) % size) for i in range(size)])  224 us
    ppermute x60, starting transfers between devices, rotate(): lax.ppermute(value, axis, [(i, (i + by) % size) for i in range(size)])  53.8 us
    pallas_call x4, Pallas kernels, project(): pl.pallas_call(functools.partial(project_kernel, groups), grid_spec=pltpu...  47.2 us
    all_to_all x6, waiting for transfers between devices, exchange(): return lax.all_to_all(pieces, 'z', 0, 0, tiled=True)  29.8 us
    all_to_all x6, starting transfers between devices, exchange(): return lax.all_to_all(pieces, 'z', 0, 0, tiled=True)  28.5 us
    unnamed x68, local copies, waits for them, and re-layouts  18.3 us
    pallas_call x6, Pallas kernels, split_weights(): pl.pallas_call(split_kernel, grid=(parts,), in_specs=[pl.BlockSpec((1, 1,...  11.8 us
    pallas_call x1, Pallas kernels, joined(): pl.pallas_call(functools.partial(joined_kernel, len(first)), grid_spec=pl...  10.6 us
  transfers between devices with their start and end apart: 66, of which 38 were waited for; matrix products, arithmetic and copies ran while one was open for 3% of the time, Pallas kernels for 17%

profile of v4, /device:TPU:0, one launch (start us, length us, event | category | flops | bytes accessed | tf_op | source)
XLA Modules:
  0.0 453.2 jit_solution(6500502903111731587)
XLA Ops:
  6.4 6.4 %all-to-all-start = ((bf16[4,512,256]{2,1,0:T(8,128)(2,1)}), bf16[4,512,256]{2,1,0:T(8,128)(2,1)S(1)}, u32[]{:S(2)}, u32[]{:S(2)}) async-start(bf16[4,512,256]{2,1,0:T(8,128)(2,1)} %shard_map.86), calls=%async_computation | async-start | bytes 2097152 | tf_op jit(solution)/shard_map/all_to_all | solution.py:72
  22.6 11.7 %collective-permute-done.1.refs_2_ = bf16[384,1024]{1,0:T(8,128)(2,1)S(1)} collective-permute-done((bf16[384,1024]{1,0:T(8,128)(2,1)S(1)}, bf16[384,1024]{1,0:T(8,128)(2,1)S(1)}, u32[]{:S(2)}, u32[]{:S(2)}) %collective-permute-start.1) | collective-permute-done | bytes 786464 | tf_op jit(solution)/shard_map/ppermute | solution.py:26
  34.3 16.5 %collective-permute-done.2.refs_4_ = bf16[384,1024]{1,0:T(8,128)(2,1)S(1)} collective-permute-done((bf16[384,1024]{1,0:T(8,128)(2,1)S(1)}, bf16[384,1024]{1,0:T(8,128)(2,1)S(1)}, u32[]{:S(2)}, u32[]{:S(2)}) %collective-permute-start.2) | collective-permute-done | bytes 786464 | tf_op jit(solution)/shard_map/ppermute | solution.py:26
  71.3 9.5 %collective-permute-done.6.refs_6_ = bf16[384,1024]{1,0:T(8,128)(2,1)} collective-permute-done((bf16[384,1024]{1,0:T(8,128)(2,1)}, bf16[384,1024]{1,0:T(8,128)(2,1)}, u32[]{:S(2)}, u32[]{:S(2)}) %collective-permute-start.6) | collective-permute-done | bytes 786464 | tf_op jit(solution)/shard_map/ppermute | solution.py:26
  80.8 15.7 %collective-permute-done.7.refs_8_ = bf16[384,1024]{1,0:T(8,128)(2,1)} collective-permute-done((bf16[384,1024]{1,0:T(8,128)(2,1)}, bf16[384,1024]{1,0:T(8,128)(2,1)}, u32[]{:S(2)}, u32[]{:S(2)}) %collective-permute-start.7) | collective-permute-done | bytes 786464 | tf_op jit(solution)/shard_map/ppermute | solution.py:26
  118.9 7.5 %collective-permute-done.11.refs_10_ = bf16[384,1024]{1,0:T(8,128)(2,1)} collective-permute-done((bf16[384,1024]{1,0:T(8,128)(2,1)}, bf16[384,1024]{1,0:T(8,128)(2,1)}, u32[]{:S(2)}, u32[]{:S(2)}) %collective-permute-start.11) | collective-permute-done | bytes 786464 | tf_op jit(solution)/shard_map/ppermute | solution.py:26
  126.4 15.7 %collective-permute-done.12.refs_12_ = bf16[384,1024]{1,0:T(8,128)(2,1)} collective-permute-done((bf16[384,1024]{1,0:T(8,128)(2,1)}, bf16[384,1024]{1,0:T(8,128)(2,1)}, u32[]{:S(2)}, u32[]{:S(2)}) %collective-permute-start.12) | collective-permute-done | bytes 786464 | tf_op jit(solution)/shard_map/ppermute | solution.py:26
  151.7 16.7 %collective-permute-done.16.refs_14_ = bf16[384,1024]{1,0:T(8,128)(2,1)} collective-permute-done((bf16[384,1024]{1,0:T(8,128)(2,1)}, bf16[384,1024]{1,0:T(8,128)(2,1)}, u32[]{:S(2)}, u32[]{:S(2)}) %collective-permute-start.16) | collective-permute-done | bytes 786464 | tf_op jit(solution)/shard_map/ppermute | solution.py:26
  177.1 19.1 %shard_map.93 = bf16[1536,768]{1,0:T(8,128)(2,1)} custom-call(s32[6]{0:T(128)} %stack.121.order_ref, bf16[384,1024]{1,0:T(8,128)(2,1)} %tokens_ref.1, bf16[384,1024]{1,0:T(8,128)(2,1)} %copy-done.21, bf16[384,1024]{1,0:T(8,128)(2,1)} %copy-done.22, bf16[384,1024]{1,0:T(8,128)(2,1)} %collective-permute-done.4.refs_3_, bf16[384,1024]{1,0:T(8,128)(2,1)} %copy-done.23, ...), custom_call_target="tpu_custom_call" | custom-call | tf_op jit(solution)/shard_map/pallas_call | solution.py:209
  211.5 14.7 %collective-permute-done.23.refs_10_ = bf16[512,1024]{1,0:T(8,128)(2,1)} collective-permute-done((bf16[512,1024]{1,0:T(8,128)(2,1)}, bf16[512,1024]{1,0:T(8,128)(2,1)}, u32[]{:S(2)}, u32[]{:S(2)}) %collective-permute-start.23) | collective-permute-done | bytes 1048608 | tf_op jit(solution)/shard_map/ppermute | solution.py:26
  236.4 6.2 %collective-permute-done.26 = bf16[384,256]{1,0:T(8,128)(2,1)S(1)} collective-permute-done((bf16[384,256]{1,0:T(8,128)(2,1)S(1)}, bf16[384,256]{1,0:T(8,128)(2,1)S(1)}, u32[]{:S(2)}, u32[]{:S(2)}) %collective-permute-start.26) | collective-permute-done | bytes 196640 | tf_op jit(solution)/shard_map/ppermute | solution.py:26
  245.4 6.1 %all-to-all-start.3 = ((bf16[4,512,256]{2,1,0:T(8,128)(2,1)}), bf16[4,512,256]{2,1,0:T(8,128)(2,1)S(1)}, u32[]{:S(2)}, u32[]{:S(2)}) async-start(bf16[4,512,256]{2,1,0:T(8,128)(2,1)} %shard_map.90), calls=%async_computation.3 | async-start | bytes 2097152 | tf_op jit(solution)/shard_map/all_to_all | solution.py:72
  254.3 9.1 %collective-permute-done.30.refs_2_ = bf16[384,1024]{1,0:T(8,128)(2,1)} collective-permute-done((bf16[384,1024]{1,0:T(8,128)(2,1)S(1)}, bf16[384,1024]{1,0:T(8,128)(2,1)}, u32[]{:S(2)}, u32[]{:S(2)}) %collective-permute-start.30) | collective-permute-done | bytes 786464 | tf_op jit(solution)/shard_map/ppermute | solution.py:26
  263.4 13.7 %all-to-all-done.3.refs_8_.refs_4_ = bf16[4,512,256]{2,1,0:T(8,128)(2,1)S(1)} async-done(((bf16[4,512,256]{2,1,0:T(8,128)(2,1)}), bf16[4,512,256]{2,1,0:T(8,128)(2,1)S(1)}, u32[]{:S(2)}, u32[]{:S(2)}) %all-to-all-start.3) | async-done | bytes 1048608 | tf_op jit(solution)/shard_map/all_to_all | solution.py:72
  282.5 10.6 %shard_map.95.refs_0_ = bf16[384,1024]{1,0:T(8,128)(2,1)} custom-call(s32[8]{0:T(128)} %stack.103.place_ref, bf16[384,1024]{1,0:T(8,128)(2,1)} %tokens_ref.1, bf16[384,1024]{1,0:T(8,128)(2,1)} %copy-done.16, bf16[384,1024]{1,0:T(8,128)(2,1)} %collective-permute-done.29.refs_1_, bf16[384,1024]{1,0:T(8,128)(2,1)} %collective-permute-done.30.refs_2_, ...), custom_call_target="tpu_custom_call" | custom-call | tf_op jit(solution)/shard_map/pallas_call | solution.py:126
  296.8 22.1 %collective-permute-done.34.refs_4_ = bf16[384,1024]{1,0:T(8,128)(2,1)S(1)} collective-permute-done((bf16[384,1024]{1,0:T(8,128)(2,1)}, bf16[384,1024]{1,0:T(8,128)(2,1)S(1)}, u32[]{:S(2)}, u32[]{:S(2)}) %collective-permute-start.34) | collective-permute-done | bytes 786464 | tf_op jit(solution)/shard_map/ppermute | solution.py:26
  323.5 4.5 all-to-all-start.4
  332.1 17.7 %collective-permute-done.38.refs_6_ = bf16[384,1024]{1,0:T(8,128)(2,1)S(1)} collective-permute-done((bf16[384,1024]{1,0:T(8,128)(2,1)}, bf16[384,1024]{1,0:T(8,128)(2,1)S(1)}, u32[]{:S(2)}, u32[]{:S(2)}) %collective-permute-start.38) | collective-permute-done | bytes 786464 | tf_op jit(solution)/shard_map/ppermute | solution.py:26
  354.7 18.1 %collective-permute-done.42.refs_0_ = bf16[384,1024]{1,0:T(8,128)(2,1)} collective-permute-done((bf16[384,1024]{1,0:T(8,128)(2,1)}, bf16[384,1024]{1,0:T(8,128)(2,1)}, u32[]{:S(2)}, u32[]{:S(2)}) %collective-permute-start.42) | collective-permute-done | bytes 786464 | tf_op jit(solution)/shard_map/ppermute | solution.py:26
  373.5 5.4 %collective-permute-done.41.refs_13_.refs_9_ = bf16[4,512,256]{2,1,0:T(8,128)(2,1)} collective-permute-done((bf16[4,512,256]{2,1,0:T(8,128)(2,1)S(1)}, bf16[4,512,256]{2,1,0:T(8,128)(2,1)}, u32[]{:S(2)}, u32[]{:S(2)}) %collective-permute-start.41) | collective-permute-done | bytes 1048608 | tf_op jit(solution)/shard_map/ppermute | solution.py:26
  378.9 11.4 %shard_map.96 = bf16[768,768]{1,0:T(8,128)(2,1)} custom-call(s32[6]{0:T(128)} %stack.121.order_ref, bf16[384,1024]{1,0:T(8,128)(2,1)} %shard_map.95.refs_0_, bf16[384,1024]{1,0:T(8,128)(2,1)} %copy-done.28, bf16[384,1024]{1,0:T(8,128)(2,1)} %copy-done.29, bf16[384,1024]{1,0:T(8,128)(2,1)} %collective-permute-done.36.refs_3_, bf16[384,1024]{1,0:T(8,128)(2,1)} %copy-done.27, ...), custom_call_target="tpu_custom_call" | custom-call | tf_op jit(solution)/shard_map/pallas_call | solution.py:209
  399.2 8.3 %shard_map.97 = bf16[384,768]{1,0:T(8,128)(2,1)} custom-call(s32[6]{0:T(128)} %stack.121.order_ref, bf16[384,1024]{1,0:T(8,128)(2,1)} %collective-permute-done.42.refs_0_, bf16[384,1024]{1,0:T(8,128)(2,1)} %collective-permute-done.43.refs_1_, bf16[384,1024]{1,0:T(8,128)(2,1)} %collective-permute-done.44.refs_2_, bf16[384,1024]{1,0:T(8,128)(2,1)} %copy-done.26, ...), custom_call_target="tpu_custom_call" | custom-call | tf_op jit(solution)/shard_map/pallas_call | solution.py:209
  412.3 8.4 %shard_map.98 = bf16[384,768]{1,0:T(8,128)(2,1)} custom-call(s32[6]{0:T(128)} %stack.121.order_ref, bf16[192,1024]{1,0:T(8,128)(2,1)} %get-tuple-element.79.refs_0_, bf16[192,1024]{1,0:T(8,128)(2,1)} %collective-permute-done.47.refs_1_, bf16[192,1024]{1,0:T(8,128)(2,1)} %collective-permute-done.48.refs_2_, ...), custom_call_target="tpu_custom_call" | custom-call | tf_op jit(solution)/shard_map/pallas_call | solution.py:209
  445.4 6.5 %collective-permute-done.58 = bf16[384,256]{1,0:T(8,128)(2,1)S(1)} collective-permute-done((bf16[384,256]{1,0:T(8,128)(2,1)S(1)}, bf16[384,256]{1,0:T(8,128)(2,1)S(1)}, u32[]{:S(2)}, u32[]{:S(2)}) %collective-permute-start.58) | collective-permute-done | bytes 196640 | tf_op jit(solution)/shard_map/ppermute | solution.py:26
  (239 shorter events, 170.2 us)
Async XLA Ops:
  6.4 49.0 %all-to-all-start = ((bf16[4,512,256]{2,1,0:T(8,128)(2,1)}), bf16[4,512,256]{2,1,0:T(8,128)(2,1)S(1)}, u32[]{:S(2)}, u32[]{:S(2)}) async-start(bf16[4,512,256]{2,1,0:T(8,128)(2,1)} %shard_map.86), calls=%async_computation | async-start | bytes 2097152 | tf_op jit(solution)/shard_map/all_to_all | solution.py:72
  12.8 38.9 %collective-permute-start.3 = (bf16[512,1024]{1,0:T(8,128)(2,1)}, bf16[512,1024]{1,0:T(8,128)(2,1)}, u32[]{:S(2)}, u32[]{:S(2)}) collective-permute-start(bf16[512,1024]{1,0:T(8,128)(2,1)} %refs_4_.1), channel_id=1, source_target_pairs={{0,4},{4,0},{1,5},{5,1},{2,6},{6,2},{3,7},{7,3},{8,12},{12,8},{9,1... | collective-permute-start | bytes 3145736 | tf_op jit(solution)/shard_map/ppermute | solution.py:26
  15.9 35.0 %collective-permute-start.2 = (bf16[384,1024]{1,0:T(8,128)(2,1)S(1)}, bf16[384,1024]{1,0:T(8,128)(2,1)S(1)}, u32[]{:S(2)}, u32[]{:S(2)}) collective-permute-start(bf16[384,1024]{1,0:T(8,128)(2,1)S(1)} %copy-done.15), channel_id=1, source_target_pairs={{0,8},{8,16},{16,24},{24,0},{1,9},{9,17},{17,25},{25,1},{2,10},{10... | collective-permute-start | bytes 2359304 | tf_op jit(solution)/shard_map/ppermute | solution.py:26
  55.4 45.6 %all-to-all-start.1 = ((bf16[4,512,256]{2,1,0:T(8,128)(2,1)}), bf16[4,512,256]{2,1,0:T(8,128)(2,1)S(1)}, u32[]{:S(2)}, u32[]{:S(2)}) async-start(bf16[4,512,256]{2,1,0:T(8,128)(2,1)} %shard_map.87), calls=%async_computation.1 | async-start | bytes 2097152 | tf_op jit(solution)/shard_map/all_to_all | solution.py:72
  58.9 37.6 %collective-permute-start.8 = (bf16[4,512,256]{2,1,0:T(8,128)(2,1)S(1)}, bf16[4,512,256]{2,1,0:T(8,128)(2,1)}, u32[]{:S(2)}, u32[]{:S(2)}) collective-permute-start(bf16[4,512,256]{2,1,0:T(8,128)(2,1)S(1)} %all-to-all-done.refs_16_), channel_id=1, source_target_pairs={{0,4},{4,0},{1,5},{5,1},{2,6},{6,2},{3,7},{7,3},{8,12},{12,8},{9,1... | collective-permute-start | bytes 3145736 | tf_op jit(solution)/shard_map/ppermute | solution.py:26
  62.5 34.0 %collective-permute-start.7 = (bf16[384,1024]{1,0:T(8,128)(2,1)}, bf16[384,1024]{1,0:T(8,128)(2,1)}, u32[]{:S(2)}, u32[]{:S(2)}) collective-permute-start(bf16[384,1024]{1,0:T(8,128)(2,1)} %copy-done.23), channel_id=1, source_target_pairs={{0,8},{8,16},{16,24},{24,0},{1,9},{9,17},{17,25},{25,1},{2,10},{10... | collective-permute-start | bytes 2359304 | tf_op jit(solution)/shard_map/ppermute | solution.py:26
  101.0 45.6 %all-to-all-start.2 = ((bf16[4,512,256]{2,1,0:T(8,128)(2,1)}), bf16[4,512,256]{2,1,0:T(8,128)(2,1)S(1)}, u32[]{:S(2)}, u32[]{:S(2)}) async-start(bf16[4,512,256]{2,1,0:T(8,128)(2,1)} %shard_map.89), calls=%async_computation.2 | async-start | bytes 2097152 | tf_op jit(solution)/shard_map/all_to_all | solution.py:72
  104.5 37.6 %collective-permute-start.13 = (bf16[4,512,256]{2,1,0:T(8,128)(2,1)S(1)}, bf16[4,512,256]{2,1,0:T(8,128)(2,1)}, u32[]{:S(2)}, u32[]{:S(2)}) collective-permute-start(bf16[4,512,256]{2,1,0:T(8,128)(2,1)S(1)} %all-to-all-done.1.refs_18_), channel_id=1, source_target_pairs={{0,4},{4,0},{1,5},{5,1},{2,6},{6,2},{3,7},{7,3},{8,12},{12,8},{9,1... | collective-permute-start | bytes 3145736 | tf_op jit(solution)/shard_map/ppermute | solution.py:26
  108.1 34.0 %collective-permute-start.12 = (bf16[384,1024]{1,0:T(8,128)(2,1)}, bf16[384,1024]{1,0:T(8,128)(2,1)}, u32[]{:S(2)}, u32[]{:S(2)}) collective-permute-start(bf16[384,1024]{1,0:T(8,128)(2,1)} %collective-permute-done.7.refs_8_), channel_id=1, source_target_pairs={{0,8},{8,16},{16,24},{24,0},{1,9},{9,17},{17,25},{25,1},{2,10},{10... | collective-permute-start | bytes 2359304 | tf_op jit(solution)/shard_map/ppermute | solution.py:26
  146.6 24.1 %collective-permute-start.18 = (bf16[4,512,256]{2,1,0:T(8,128)(2,1)S(1)}, bf16[4,512,256]{2,1,0:T(8,128)(2,1)S(1)}, u32[]{:S(2)}, u32[]{:S(2)}) collective-permute-start(bf16[4,512,256]{2,1,0:T(8,128)(2,1)S(1)} %all-to-all-done.2.refs_20_), channel_id=1, source_target_pairs={{0,4},{4,0},{1,5},{5,1},{2,6},{6,2},{3,7},{7,3},{8,12},{12,8},{9,1... | collective-permute-start | bytes 3145736 | tf_op jit(solution)/shard_map/ppermute | solution.py:26
  148.1 25.8 %collective-permute-start.19 = (bf16[512,1024]{1,0:T(8,128)(2,1)}, bf16[512,1024]{1,0:T(8,128)(2,1)S(1)}, u32[]{:S(2)}, u32[]{:S(2)}) collective-permute-start(bf16[512,1024]{1,0:T(8,128)(2,1)} %refs_4_.1), channel_id=1, source_target_pairs={{0,8},{8,16},{16,24},{24,0},{1,9},{9,17},{17,25},{25,1},{2,10},{10... | collective-permute-start | bytes 3145736 | tf_op jit(solution)/shard_map/ppermute | solution.py:26
  173.9 25.0 %collective-permute-start.21 = (bf16[512,1024]{1,0:T(8,128)(2,1)S(1)}, bf16[512,1024]{1,0:T(8,128)(2,1)}, u32[]{:S(2)}, u32[]{:S(2)}) collective-permute-start(bf16[512,1024]{1,0:T(8,128)(2,1)S(1)} %collective-permute-done.19.refs_6_), channel_id=1, source_target_pairs={{0,8},{8,16},{16,24},{24,0},{1,9},{9,17},{17,25},{25,1},{2,10},{10... | collective-permute-start | bytes 3145736 | tf_op jit(solution)/shard_map/ppermute | solution.py:26
  173.9 25.0 %collective-permute-start.22 = (bf16[512,1024]{1,0:T(8,128)(2,1)S(1)}, bf16[512,1024]{1,0:T(8,128)(2,1)}, u32[]{:S(2)}, u32[]{:S(2)}) collective-permute-start(bf16[512,1024]{1,0:T(8,128)(2,1)S(1)} %collective-permute-done.19.refs_6_), channel_id=1, source_target_pairs={{0,4},{4,0},{1,5},{5,1},{2,6},{6,2},{3,7},{7,3},{8,12},{12,8},{9,1... | collective-permute-start | bytes 3145736 | tf_op jit(solution)/shard_map/ppermute | solution.py:26
  198.9 27.2 %collective-permute-start.23 = (bf16[512,1024]{1,0:T(8,128)(2,1)}, bf16[512,1024]{1,0:T(8,128)(2,1)}, u32[]{:S(2)}, u32[]{:S(2)}) collective-permute-start(bf16[512,1024]{1,0:T(8,128)(2,1)} %collective-permute-done.21.refs_8_), channel_id=1, source_target_pairs={{0,8},{8,16},{16,24},{24,0},{1,9},{9,17},{17,25},{25,1},{2,10},{10... | collective-permute-start | bytes 3145736 | tf_op jit(solution)/shard_map/ppermute | solution.py:26
  202.0 24.6 %collective-permute-start.24 = (bf16[512,1024]{1,0:T(8,128)(2,1)}, bf16[512,1024]{1,0:T(8,128)(2,1)S(1)}, u32[]{:S(2)}, u32[]{:S(2)}) collective-permute-start(bf16[512,1024]{1,0:T(8,128)(2,1)} %collective-permute-done.21.refs_8_), channel_id=1, source_target_pairs={{0,4},{4,0},{1,5},{5,1},{2,6},{6,2},{3,7},{7,3},{8,12},{12,8},{9,1... | collective-permute-start | bytes 3145736 | tf_op jit(solution)/shard_map/ppermute | solution.py:26
  231.1 23.2 %collective-permute-start.28 = (bf16[512,1024]{1,0:T(8,128)(2,1)}, bf16[512,1024]{1,0:T(8,128)(2,1)}, u32[]{:S(2)}, u32[]{:S(2)}) collective-permute-start(bf16[512,1024]{1,0:T(8,128)(2,1)} %collective-permute-done.23.refs_10_), channel_id=1, source_target_pairs={{0,4},{4,0},{1,5},{5,1},{2,6},{6,2},{3,7},{7,3},{8,12},{12,8},{9,1... | collective-permute-start | bytes 3145736 | tf_op jit(solution)/shard_map/ppermute | solution.py:26
  245.4 31.7 %all-to-all-start.3 = ((bf16[4,512,256]{2,1,0:T(8,128)(2,1)}), bf16[4,512,256]{2,1,0:T(8,128)(2,1)S(1)}, u32[]{:S(2)}, u32[]{:S(2)}) async-start(bf16[4,512,256]{2,1,0:T(8,128)(2,1)} %shard_map.90), calls=%async_computation.3 | async-start | bytes 2097152 | tf_op jit(solution)/shard_map/all_to_all | solution.py:72
  277.1 46.4 %all-to-all-start.5 = ((bf16[4,512,256]{2,1,0:T(8,128)(2,1)}), bf16[4,512,256]{2,1,0:T(8,128)(2,1)}, u32[]{:S(2)}, u32[]{:S(2)}) async-start(bf16[4,512,256]{2,1,0:T(8,128)(2,1)} %shard_map.91), calls=%async_computation.5 | async-start | bytes 2097152 | tf_op jit(solution)/shard_map/all_to_all | solution.py:72
  293.1 28.4 %collective-permute-start.35 = (bf16[4,512,256]{2,1,0:T(8,128)(2,1)S(1)}, bf16[4,512,256]{2,1,0:T(8,128)(2,1)S(1)}, u32[]{:S(2)}, u32[]{:S(2)}) collective-permute-start(bf16[4,512,256]{2,1,0:T(8,128)(2,1)S(1)} %all-to-all-done.3.refs_8_.refs_4_), channel_id=1, source_target_pairs={{0,4},{4,0},{1,5},{5,1},{2,6},{6,2},{3,7},{7,3},{8,12},{12,8},{9,1... | collective-permute-start | bytes 3145736 | tf_op jit(solution)/shard_map/ppermute | solution.py:26
  294.7 24.1 %collective-permute-start.34 = (bf16[384,1024]{1,0:T(8,128)(2,1)}, bf16[384,1024]{1,0:T(8,128)(2,1)S(1)}, u32[]{:S(2)}, u32[]{:S(2)}) collective-permute-start(bf16[384,1024]{1,0:T(8,128)(2,1)} %shard_map.95.refs_0_), channel_id=1, source_target_pairs={{0,8},{8,16},{16,24},{24,0},{1,9},{9,17},{17,25},{25,1},{2,10},{10... | collective-permute-start | bytes 2359304 | tf_op jit(solution)/shard_map/ppermute | solution.py:26
  296.2 23.5 %collective-permute-start.33 = (bf16[384,1024]{1,0:T(8,128)(2,1)}, bf16[384,1024]{1,0:T(8,128)(2,1)S(1)}, u32[]{:S(2)}, u32[]{:S(2)}) collective-permute-start(bf16[384,1024]{1,0:T(8,128)(2,1)} %shard_map.95.refs_0_), channel_id=1, source_target_pairs={{0,2},{2,0},{1,3},{3,1},{4,6},{6,4},{5,7},{7,5},{8,10},{10,8},{9,1... | collective-permute-start | bytes 2359304 | tf_op jit(solution)/shard_map/ppermute | solution.py:26
  323.5 28.7 %all-to-all-start.4 = ((bf16[4,512,256]{2,1,0:T(8,128)(2,1)}), bf16[4,512,256]{2,1,0:T(8,128)(2,1)S(1)}, u32[]{:S(2)}, u32[]{:S(2)}) async-start(bf16[4,512,256]{2,1,0:T(8,128)(2,1)} %shard_map.92), calls=%async_computation.4 | async-start | bytes 2097152 | tf_op jit(solution)/shard_map/all_to_all | solution.py:72
  328.0 24.2 %collective-permute-start.39 = (bf16[4,512,256]{2,1,0:T(8,128)(2,1)}, bf16[4,512,256]{2,1,0:T(8,128)(2,1)}, u32[]{:S(2)}, u32[]{:S(2)}) collective-permute-start(bf16[4,512,256]{2,1,0:T(8,128)(2,1)} %all-to-all-done.5.refs_10_.refs_6_), channel_id=1, source_target_pairs={{0,4},{4,0},{1,5},{5,1},{2,6},{6,2},{3,7},{7,3},{8,12},{12,8},{9,1... | collective-permute-start | bytes 3145736 | tf_op jit(solution)/shard_map/ppermute | solution.py:26
  353.2 25.7 %collective-permute-start.41 = (bf16[4,512,256]{2,1,0:T(8,128)(2,1)S(1)}, bf16[4,512,256]{2,1,0:T(8,128)(2,1)}, u32[]{:S(2)}, u32[]{:S(2)}) collective-permute-start(bf16[4,512,256]{2,1,0:T(8,128)(2,1)S(1)} %all-to-all-done.4.refs_12_.refs_8_), channel_id=1, source_target_pairs={{0,4},{4,0},{1,5},{5,1},{2,6},{6,2},{3,7},{7,3},{8,12},{12,8},{9,1... | collective-permute-start | bytes 3145736 | tf_op jit(solution)/shard_map/ppermute | solution.py:26
  (75 other events, 1014.4 us)

commit v5 on v4

--- a/solution.py
+++ b/solution.py
@@ -150,7 +150,7 @@
     return rotate(value, "z", 1)
 
 
-def project_kernel(groups, order_ref, *refs):
+def project_kernel(groups, kept, order_ref, *refs):
     count = len(refs) - 5
     pieces = refs[: count - 3 * (order_ref.shape[0] - groups[1])]
     weights = refs[len(pieces) : count]
@@ -189,7 +189,7 @@
         for j in range(y_size):
             begin = pl.multiple_of(order_ref[groups[1] + j] * deep, deep)
             some = some + jnp.dot(
-                held[step, :, pl.ds(begin, deep)], weights[c * y_size + j][0], preferred_element_type=jnp.float32
+                held[step, :, pl.ds(begin, deep)], weights[c * y_size + j][order_ref[step] if kept else 0], preferred_element_type=jnp.float32
             )
         total[:, c * width : (c + 1) * width] += some
 
@@ -199,7 +199,7 @@
         out_ref[...] = (total[...] * scale).astype(out_ref.dtype)
 
 
-def project(found, weights, order):
+def project(found, weights, order, kept=False):
     groups = (len(found), len(found[0]))
     flat = [w for group in weights for w in group]
     pieces = [p for group in found for p in group]
@@ -207,12 +207,17 @@
     width = flat[0].shape[2]
     needed = groups[0] * rows * (groups[1] * features_here * 2 + 3 * width * 8 + 512) + 12 * flat[0][0].size * len(flat) // 3
     out = pl.pallas_call(
-        functools.partial(project_kernel, groups),
+        functools.partial(project_kernel, groups, kept),
         grid_spec=pltpu.PrefetchScalarGridSpec(
             num_scalar_prefetch=1,
             grid=(groups[1],),
             in_specs=[pl.BlockSpec(memory_space=pl.ANY)] * len(pieces)
-            + [pl.BlockSpec((1,) + w.shape[1:], lambda r, order: (order[r], 0, 0)) for w in flat],
+            + [
+                pl.BlockSpec(memory_space=pltpu.VMEM)
+                if kept
+                else pl.BlockSpec((1,) + w.shape[1:], lambda r, order: (order[r], 0, 0))
+                for w in flat
+            ],
             out_specs=pl.BlockSpec((groups[0] * rows, 3 * width), lambda r, order: (0, 0)),
             scratch_shapes=[
                 pltpu.VMEM((groups[1], groups[0] * rows, features_here), jnp.bfloat16),
@@ -222,7 +227,7 @@
             ],
         ),
         out_shape=jax.ShapeDtypeStruct((groups[0] * rows, 3 * width), jnp.bfloat16),
-        compiler_params=pltpu.CompilerParams(vmem_limit_bytes=60 * MIB),
+        compiler_params=pltpu.CompilerParams(vmem_limit_bytes=(30 * MIB) if kept else 60 * MIB),
     )(order, *pieces, *flat)
     return out.reshape(groups[0], rows, 3 * width)
 
@@ -354,20 +359,22 @@
     )(table, proj, before, feat)
 
 
-def medium_mix(early, last, feat, matrix, table, z_at):
+def medium_early(early, feat, table, span):
+    near = tails(early, 16)
+    query, kv = gate(early, near, feat, jnp.minimum(table[:, :-1], table.shape[1] - 2))
+    return near, query, kv, tails(kv, span)
+
+
+def medium_mix(early, made_early, last, feat, matrix, table, z_at):
     parts, span = table.shape[1], matrix.shape[1]
-    near_early, near_last = tails(early, 16), tails(last, 16)
-    inside = jnp.minimum(table[:, : parts - 1], parts - 2)
-    query, kv = gate(after(early, last), near_early, feat, inside)
-    far_early = tails(kv, span)
-    close = medium(query, kv, far_early, matrix, table[:, : parts - 2])
-    made = [close[k] for k in range(parts - 2)]
-    query, kv = gate(
-        jnp.concatenate([early[-1:], last]), jnp.concatenate([near_early, near_last]), feat, table[:, parts - 2 :]
-    )
+    near_early, query, kv, far_early = made_early
+    near = jnp.concatenate([near_early, tails(last, 16)])
+    close = medium(after(query, last), kv, far_early, matrix, table[:, : parts - 2])
+    both = after(jnp.concatenate([early[-1:], last]), close)
+    query, kv = gate(both, near, feat, table[:, parts - 2 :])
     far = jnp.concatenate([far_early, tails(kv[1:], span)])
     distant = medium(query, kv, far, matrix, table[:, parts - 2 :])
-    return home(made + [distant[0], distant[1]], z_at)
+    return home([close[k] for k in range(parts - 2)] + [distant[0], distant[1]], z_at)
 
 
 def medium(query, kv, before, matrix, table):
@@ -444,24 +451,25 @@
     step = Steps()
     ring, found, came, weights = [tokens], [], [], []
     rows_ring, held = [out_weight], []
-    splits = [split(1, c) for c in range(3)]
+    splits = [[split(block, c) for c in range(3)] for block in range(2)]
     for k in range(parts):
         if k < parts - 1:
-            ring.append(step(next_along_z, ring[k]))
-        else:
-            rows_ring.append(step(next_along_z, out_weight))
-        if k < 3:
-            came.append(step(exchange, split(0, k)))
+            ring.append(next_along_z(ring[k]))
         found.append([others("c", ring[k], step)])
         fresh = others("x", ring[k], step)[1:]
+        own = found[k][0][1:]
+        if k < 3:
+            came.append(exchange(after(splits[0][k], *own, *came[-1:])))
         if k:
             found[k - 1] += [others("c", piece, step) for piece in waiting]
         waiting = fresh
         if k == 0:
             held.append(others("y", out_weight, step))
         elif k <= 3:
-            weights.append(others("y", came[k - 1], step))
-        step.then(*([matrix] if k == 1 else splits if k == 2 else []))
+            weights.append(others("y", after(came[k - 1], *own), step))
+        if k == parts - 1:
+            rows_ring.append(step(next_along_z, after(out_weight, came[2])))
+        step.then(*([splits[0][1:], splits[1] + [matrix], []] + [[]] * parts)[k])
     found[-1] += [others("c", piece, at_once) for piece in waiting]
     proj = project([sum(group, []) for group in found], weights, order)
     near = tails(after(proj, *step.gate), 16)
@@ -475,8 +483,8 @@
     held.append(others("y", after(rows_ring[-1], *held[-1]), at_once))
     first = all_of_c([after(piece, *held[-1]) for piece in others("x", back, at_once)])
     step.then(*step.gate, back)
-    came, weights_next = [step(exchange, splits[0])], []
-    came.append(exchange(after(splits[1], came[0], *first)))
+    came, weights_next = [step(exchange, splits[1][0])], []
+    came.append(exchange(after(splits[1][1], came[0], *first)))
     stream = joined(tokens, first, held, places, where)
 
     step.then(stream)
@@ -493,7 +501,7 @@
     weights_next.append(others("y", came[0], step))
     swap(0)
     step.then()
-    came.append(step(exchange, splits[2]))
+    came.append(step(exchange, splits[1][2]))
     weights_next.append(others("y", came[1], step))
     swap(1)
     spread(0)
@@ -514,12 +522,14 @@
     near_half = others("x", ring[-1][:half], step)[1:]
     far_half = [step(next_along_z, piece[half:]) for piece in swapped[-1]]
     halves = [[others("c", ring[-1][:half], at_once)], [others("c", ring[-1][half:], at_once)]]
-    early = [early] + [project([sum(group, [])], weights_next, order) for group in found[2:]]
+    early = [early] + [project([sum(group, [])], weights_next, order, True) for group in found[2:]]
     early = jnp.concatenate(early)
     for group, more in zip(halves, (near_half, far_half)):
         group += [others("c", after(piece, early), at_once) for piece in more]
-    last = project([sum(group, []) for group in halves], weights_next, order).reshape(1, count, -1)
-    return stream, medium_mix(early, last, feat[1], matrix, table, z_at)
+    made_early = medium_early(early, feat[1], table, matrix.shape[1])
+    halves[0][0][0] = after(halves[0][0][0], made_early[2])
+    last = project([sum(group, []) for group in halves], weights_next, order, True).reshape(1, count, -1)
+    return stream, medium_mix(early, made_early, last, feat[1], matrix, table, z_at)
 
 
 def solution(mesh):

time: 456 us -> 443 us (0.971)
  starting transfers between devices: 82.3 us -> 75.9 us
    all_to_all x6, waiting for transfers between devices: 29.8 us -> 72.5 us  [exchange(): return lax.all_to_all(pieces, 'z', 0, 0, tiled=True)]
    ppermute x60, waiting for transfers between devices: 224 us -> 182 us  [rotate(): lax.ppermute(value, axis, [(i, (i + by) % size) for i in range(size)])]
    ppermute x60, starting transfers between devices: 53.8 us -> 48 us  [rotate(): lax.ppermute(value, axis, [(i, (i + by) % size) for i in range(size)])]
    unnamed x68 -> x74, local copies, waits for them, and re-layouts: 18.3 us -> 19 us
  transfers between devices with their start and end apart: 66 -> 66, of which waited for: 38 -> 36; matrix products, arithmetic and copies ran while one was open for 3% -> 2% of each run, Pallas kernels for 17% -> 18%
where the time goes in v5:
time: 443 us; the launch traced here: 442 us
  waiting for transfers between devices  254 us (57%)
  Pallas kernels  79.9 us (18%)
  starting transfers between devices  75.9 us (17%)
  local copies, waits for them, and re-layouts  26.8 us (6%)
    ppermute x60, waiting for transfers between devices, rotate(): lax.ppermute(value, axis, [(i, (i + by) % size) for i in range(size)])  182 us
    all_to_all x6, waiting for transfers between devices, exchange(): return lax.all_to_all(pieces, 'z', 0, 0, tiled=True)  72.5 us
    ppermute x60, starting transfers between devices, rotate(): lax.ppermute(value, axis, [(i, (i + by) % size) for i in range(size)])  48 us
    pallas_call x4, Pallas kernels, project(): pl.pallas_call(functools.partial(project_kernel, groups, kept), grid_spec...  45.7 us
    all_to_all x6, starting transfers between devices, exchange(): return lax.all_to_all(pieces, 'z', 0, 0, tiled=True)  27.9 us
    unnamed x74, local copies, waits for them, and re-layouts  19 us
    pallas_call x1, Pallas kernels, joined(): pl.pallas_call(functools.partial(joined_kernel, len(first)), grid_spec=pl...  10.6 us
    pallas_call x6, Pallas kernels, split_weights(): pl.pallas_call(split_kernel, grid=(parts,), in_specs=[pl.BlockSpec((1, 1,...  9.38 us
  transfers between devices with their start and end apart: 66, of which 36 were waited for; matrix products, arithmetic and copies ran while one was open for 2% of the time, Pallas kernels for 18%

profile of v5, /device:TPU:0, one launch (start us, length us, event | category | flops | bytes accessed | tf_op | source)
XLA Modules:
  0.0 441.6 jit_solution(12455518308640544457)
XLA Ops:
  30.4 18.7 %all-to-all-done.refs_16_ = bf16[4,512,256]{2,1,0:T(8,128)(2,1)S(1)} async-done(((bf16[4,512,256]{2,1,0:T(8,128)(2,1)}), bf16[4,512,256]{2,1,0:T(8,128)(2,1)S(1)}, u32[]{:S(2)}, u32[]{:S(2)}) %all-to-all-start) | async-done | bytes 1048608 | tf_op jit(solution)/shard_map/all_to_all | solution.py:72
  50.2 5.1 %all-to-all-start.1 = ((bf16[4,512,256]{2,1,0:T(8,128)(2,1)}), bf16[4,512,256]{2,1,0:T(8,128)(2,1)S(1)}, u32[]{:S(2)}, u32[]{:S(2)}) async-start(bf16[4,512,256]{2,1,0:T(8,128)(2,1)} %shard_map.86), calls=%async_computation.1 | async-start | bytes 2097152 | tf_op jit(solution)/shard_map/all_to_all | solution.py:72
  65.8 6.6 %collective-permute-done.9.refs_8_ = bf16[384,1024]{1,0:T(8,128)(2,1)} collective-permute-done((bf16[384,1024]{1,0:T(8,128)(2,1)}, bf16[384,1024]{1,0:T(8,128)(2,1)}, u32[]{:S(2)}, u32[]{:S(2)}) %collective-permute-start.9) | collective-permute-done | bytes 786464 | tf_op jit(solution)/shard_map/ppermute | solution.py:26
  74.3 19.0 %all-to-all-done.1.refs_18_ = bf16[4,512,256]{2,1,0:T(8,128)(2,1)S(1)} async-done(((bf16[4,512,256]{2,1,0:T(8,128)(2,1)}), bf16[4,512,256]{2,1,0:T(8,128)(2,1)S(1)}, u32[]{:S(2)}, u32[]{:S(2)}) %all-to-all-start.1) | async-done | bytes 1048608 | tf_op jit(solution)/shard_map/all_to_all | solution.py:72
  94.9 5.1 %all-to-all-start.2 = ((bf16[4,512,256]{2,1,0:T(8,128)(2,1)}), bf16[4,512,256]{2,1,0:T(8,128)(2,1)S(1)}, u32[]{:S(2)}, u32[]{:S(2)}) async-start(bf16[4,512,256]{2,1,0:T(8,128)(2,1)} %shard_map.87), calls=%async_computation.2 | async-start | bytes 2097152 | tf_op jit(solution)/shard_map/all_to_all | solution.py:72
  100.5 17.1 %collective-permute-done.14.refs_12_ = bf16[384,1024]{1,0:T(8,128)(2,1)} collective-permute-done((bf16[384,1024]{1,0:T(8,128)(2,1)}, bf16[384,1024]{1,0:T(8,128)(2,1)}, u32[]{:S(2)}, u32[]{:S(2)}) %collective-permute-start.14) | collective-permute-done | bytes 786464 | tf_op jit(solution)/shard_map/ppermute | solution.py:26
  121.1 17.5 %all-to-all-done.2.refs_20_ = bf16[4,512,256]{2,1,0:T(8,128)(2,1)S(1)} async-done(((bf16[4,512,256]{2,1,0:T(8,128)(2,1)}), bf16[4,512,256]{2,1,0:T(8,128)(2,1)S(1)}, u32[]{:S(2)}, u32[]{:S(2)}) %all-to-all-start.2) | async-done | bytes 1048608 | tf_op jit(solution)/shard_map/all_to_all | solution.py:72
  141.7 17.8 %collective-permute-done.16.refs_14_ = bf16[384,1024]{1,0:T(8,128)(2,1)} collective-permute-done((bf16[384,1024]{1,0:T(8,128)(2,1)}, bf16[384,1024]{1,0:T(8,128)(2,1)}, u32[]{:S(2)}, u32[]{:S(2)}) %collective-permute-start.16) | collective-permute-done | bytes 786464 | tf_op jit(solution)/shard_map/ppermute | solution.py:26
  159.4 6.3 %collective-permute-done.19.refs_6_ = bf16[512,1024]{1,0:T(8,128)(2,1)} collective-permute-done((bf16[512,1024]{1,0:T(8,128)(2,1)}, bf16[512,1024]{1,0:T(8,128)(2,1)}, u32[]{:S(2)}, u32[]{:S(2)}) %collective-permute-start.19) | collective-permute-done | bytes 1048608 | tf_op jit(solution)/shard_map/ppermute | solution.py:26
  169.9 19.5 %shard_map.93 = bf16[1536,768]{1,0:T(8,128)(2,1)} custom-call(s32[6]{0:T(128)} %stack.121.order_ref, bf16[384,1024]{1,0:T(8,128)(2,1)} %tokens_ref.1, bf16[384,1024]{1,0:T(8,128)(2,1)} %copy-done.24, bf16[384,1024]{1,0:T(8,128)(2,1)} %collective-permute-done.1.refs_2_, bf16[384,1024]{1,0:T(8,128)(2,1)} %collective-permute-done.3.refs_3_, ...), custom_call_target="tpu_custom_call" | custom-call | tf_op jit(solution)/shard_map/pallas_call | solution.py:209
  204.5 14.8 %collective-permute-done.23.refs_10_ = bf16[512,1024]{1,0:T(8,128)(2,1)} collective-permute-done((bf16[512,1024]{1,0:T(8,128)(2,1)}, bf16[512,1024]{1,0:T(8,128)(2,1)}, u32[]{:S(2)}, u32[]{:S(2)}) %collective-permute-start.23) | collective-permute-done | bytes 1048608 | tf_op jit(solution)/shard_map/ppermute | solution.py:26
  229.5 6.1 %collective-permute-done.26 = bf16[384,256]{1,0:T(8,128)(2,1)S(1)} collective-permute-done((bf16[384,256]{1,0:T(8,128)(2,1)S(1)}, bf16[384,256]{1,0:T(8,128)(2,1)S(1)}, u32[]{:S(2)}, u32[]{:S(2)}) %collective-permute-start.26) | collective-permute-done | bytes 196640 | tf_op jit(solution)/shard_map/ppermute | solution.py:26
  237.4 6.2 %all-to-all-start.3 = ((bf16[4,512,256]{2,1,0:T(8,128)(2,1)}), bf16[4,512,256]{2,1,0:T(8,128)(2,1)S(1)}, u32[]{:S(2)}, u32[]{:S(2)}) async-start(bf16[4,512,256]{2,1,0:T(8,128)(2,1)} %shard_map.89), calls=%async_computation.3 | async-start | bytes 2097152 | tf_op jit(solution)/shard_map/all_to_all | solution.py:72
  247.7 8.7 %collective-permute-done.30.refs_2_ = bf16[384,1024]{1,0:T(8,128)(2,1)} collective-permute-done((bf16[384,1024]{1,0:T(8,128)(2,1)S(1)}, bf16[384,1024]{1,0:T(8,128)(2,1)}, u32[]{:S(2)}, u32[]{:S(2)}) %collective-permute-start.30) | collective-permute-done | bytes 786464 | tf_op jit(solution)/shard_map/ppermute | solution.py:26
  256.4 12.7 %all-to-all-done.3.refs_8_.refs_4_ = bf16[4,512,256]{2,1,0:T(8,128)(2,1)S(1)} async-done(((bf16[4,512,256]{2,1,0:T(8,128)(2,1)}), bf16[4,512,256]{2,1,0:T(8,128)(2,1)S(1)}, u32[]{:S(2)}, u32[]{:S(2)}) %all-to-all-start.3) | async-done | bytes 1048608 | tf_op jit(solution)/shard_map/all_to_all | solution.py:72
  273.8 10.6 %shard_map.95.refs_0_ = bf16[384,1024]{1,0:T(8,128)(2,1)} custom-call(s32[8]{0:T(128)} %stack.103.place_ref, bf16[384,1024]{1,0:T(8,128)(2,1)} %tokens_ref.1, bf16[384,1024]{1,0:T(8,128)(2,1)} %copy-done.20, bf16[384,1024]{1,0:T(8,128)(2,1)} %collective-permute-done.29.refs_1_, bf16[384,1024]{1,0:T(8,128)(2,1)} %collective-permute-done.30.refs_2_, ...), custom_call_target="tpu_custom_call" | custom-call | tf_op jit(solution)/shard_map/pallas_call | solution.py:126
  289.2 21.0 %collective-permute-done.34.refs_4_ = bf16[384,1024]{1,0:T(8,128)(2,1)S(1)} collective-permute-done((bf16[384,1024]{1,0:T(8,128)(2,1)}, bf16[384,1024]{1,0:T(8,128)(2,1)S(1)}, u32[]{:S(2)}, u32[]{:S(2)}) %collective-permute-start.34) | collective-permute-done | bytes 786464 | tf_op jit(solution)/shard_map/ppermute | solution.py:26
  322.8 17.7 %collective-permute-done.38.refs_6_ = bf16[384,1024]{1,0:T(8,128)(2,1)S(1)} collective-permute-done((bf16[384,1024]{1,0:T(8,128)(2,1)}, bf16[384,1024]{1,0:T(8,128)(2,1)S(1)}, u32[]{:S(2)}, u32[]{:S(2)}) %collective-permute-start.38) | collective-permute-done | bytes 786464 | tf_op jit(solution)/shard_map/ppermute | solution.py:26
  345.8 18.3 %collective-permute-done.42.refs_0_ = bf16[384,1024]{1,0:T(8,128)(2,1)} collective-permute-done((bf16[384,1024]{1,0:T(8,128)(2,1)}, bf16[384,1024]{1,0:T(8,128)(2,1)}, u32[]{:S(2)}, u32[]{:S(2)}) %collective-permute-start.42) | collective-permute-done | bytes 786464 | tf_op jit(solution)/shard_map/ppermute | solution.py:26
  369.9 11.5 %shard_map.96 = bf16[768,768]{1,0:T(8,128)(2,1)} custom-call(s32[6]{0:T(128)} %stack.121.order_ref, bf16[384,1024]{1,0:T(8,128)(2,1)} %shard_map.95.refs_0_, bf16[384,1024]{1,0:T(8,128)(2,1)} %copy-done.31, bf16[384,1024]{1,0:T(8,128)(2,1)} %copy-done.32, bf16[384,1024]{1,0:T(8,128)(2,1)} %collective-permute-done.36.refs_3_, bf16[384,1024]{1,0:T(8,128)(2,1)} %copy-done.30, ...), custom_call_target="tpu_custom_call" | custom-call | tf_op jit(solution)/shard_map/pallas_call | solution.py:209
  390.4 7.1 %shard_map.97 = bf16[384,768]{1,0:T(8,128)(2,1)S(1)} custom-call(s32[6]{0:T(128)S(1)} %copy-done.15, bf16[384,1024]{1,0:T(8,128)(2,1)} %collective-permute-done.42.refs_0_, bf16[384,1024]{1,0:T(8,128)(2,1)} %collective-permute-done.43.refs_1_, bf16[384,1024]{1,0:T(8,128)(2,1)} %collective-permute-done.44.refs_2_, ...), custom_call_target="tpu_custom_call" | custom-call | tf_op jit(solution)/shard_map/pallas_call | solution.py:209
  405.2 7.7 %shard_map.99 = bf16[384,768]{1,0:T(8,128)(2,1)S(1)} custom-call(s32[6]{0:T(128)S(1)} %copy-done.15, bf16[192,1024]{1,0:T(8,128)(2,1)S(1)} %get-tuple-element.94.refs_0_, bf16[192,1024]{1,0:T(8,128)(2,1)S(1)} %collective-permute-done.48.refs_1_, bf16[192,1024]{1,0:T(8,128)(2,1)S(1)} %collective-permute-done.49.refs_2_, ...), custom_call_target="tpu_custom_call" | custom-call | tf_op jit(solution)/shard_map/pallas_call | solution.py:209
  429.7 5.4 %collective-permute-done.59 = bf16[384,256]{1,0:T(8,128)(2,1)S(1)} collective-permute-done((bf16[384,256]{1,0:T(8,128)(2,1)S(1)}, bf16[384,256]{1,0:T(8,128)(2,1)S(1)}, u32[]{:S(2)}, u32[]{:S(2)}) %collective-permute-start.59) | collective-permute-done | bytes 196640 | tf_op jit(solution)/shard_map/ppermute | solution.py:26
  435.1 5.3 %collective-permute-done.58 = bf16[384,256]{1,0:T(8,128)(2,1)S(1)} collective-permute-done((bf16[384,256]{1,0:T(8,128)(2,1)S(1)}, bf16[384,256]{1,0:T(8,128)(2,1)S(1)}, u32[]{:S(2)}, u32[]{:S(2)}) %collective-permute-start.58) | collective-permute-done | bytes 196640 | tf_op jit(solution)/shard_map/ppermute | solution.py:26
  (245 shorter events, 154.4 us)
Async XLA Ops:
  1.2 26.8 %collective-permute-start.2 = (bf16[512,1024]{1,0:T(8,128)(2,1)}, bf16[512,1024]{1,0:T(8,128)(2,1)S(1)}, u32[]{:S(2)}, u32[]{:S(2)}) collective-permute-start(bf16[512,1024]{1,0:T(8,128)(2,1)} %refs_4_.1), channel_id=1, source_target_pairs={{0,4},{4,0},{1,5},{5,1},{2,6},{6,2},{3,7},{7,3},{8,12},{12,8},{9,1... | collective-permute-start | bytes 3145736 | tf_op jit(solution)/shard_map/ppermute | solution.py:26
  13.5 35.7 %all-to-all-start = ((bf16[4,512,256]{2,1,0:T(8,128)(2,1)}), bf16[4,512,256]{2,1,0:T(8,128)(2,1)S(1)}, u32[]{:S(2)}, u32[]{:S(2)}) async-start(bf16[4,512,256]{2,1,0:T(8,128)(2,1)} %shard_map.88), calls=%async_computation | async-start | bytes 2097152 | tf_op jit(solution)/shard_map/all_to_all | solution.py:72
  49.2 25.2 %collective-permute-start.7 = (bf16[4,512,256]{2,1,0:T(8,128)(2,1)S(1)}, bf16[4,512,256]{2,1,0:T(8,128)(2,1)}, u32[]{:S(2)}, u32[]{:S(2)}) collective-permute-start(bf16[4,512,256]{2,1,0:T(8,128)(2,1)S(1)} %all-to-all-done.refs_16_), channel_id=1, source_target_pairs={{0,4},{4,0},{1,5},{5,1},{2,6},{6,2},{3,7},{7,3},{8,12},{12,8},{9,1... | collective-permute-start | bytes 3145736 | tf_op jit(solution)/shard_map/ppermute | solution.py:26
  49.7 22.7 %collective-permute-start.9 = (bf16[384,1024]{1,0:T(8,128)(2,1)}, bf16[384,1024]{1,0:T(8,128)(2,1)}, u32[]{:S(2)}, u32[]{:S(2)}) collective-permute-start(bf16[384,1024]{1,0:T(8,128)(2,1)} %collective-permute-done.4.refs_4_), channel_id=1, source_target_pairs={{0,8},{8,16},{16,24},{24,0},{1,9},{9,17},{17,25},{25,1},{2,10},{10... | collective-permute-start | bytes 2359304 | tf_op jit(solution)/shard_map/ppermute | solution.py:26
  49.7 22.7 %collective-permute-start.3 = (bf16[384,1024]{1,0:T(8,128)(2,1)}, bf16[384,1024]{1,0:T(8,128)(2,1)}, u32[]{:S(2)}, u32[]{:S(2)}) collective-permute-start(bf16[384,1024]{1,0:T(8,128)(2,1)} %collective-permute-done.1.refs_2_), channel_id=1, source_target_pairs={{0,1},{1,0},{2,3},{3,2},{4,5},{5,4},{6,7},{7,6},{8,9},{9,8},{10,11... | collective-permute-start | bytes 2359304 | tf_op jit(solution)/shard_map/ppermute | solution.py:26
  49.7 22.7 %collective-permute-start.6 = (bf16[384,1024]{1,0:T(8,128)(2,1)}, bf16[384,1024]{1,0:T(8,128)(2,1)}, u32[]{:S(2)}, u32[]{:S(2)}) collective-permute-start(bf16[384,1024]{1,0:T(8,128)(2,1)} %collective-permute-done.4.refs_4_), channel_id=1, source_target_pairs={{0,2},{2,0},{1,3},{3,1},{4,6},{6,4},{5,7},{7,5},{8,10},{10,8},{9,1... | collective-permute-start | bytes 2359304 | tf_op jit(solution)/shard_map/ppermute | solution.py:26
  50.2 43.1 %all-to-all-start.1 = ((bf16[4,512,256]{2,1,0:T(8,128)(2,1)}), bf16[4,512,256]{2,1,0:T(8,128)(2,1)S(1)}, u32[]{:S(2)}, u32[]{:S(2)}) async-start(bf16[4,512,256]{2,1,0:T(8,128)(2,1)} %shard_map.86), calls=%async_computation.1 | async-start | bytes 2097152 | tf_op jit(solution)/shard_map/all_to_all | solution.py:72
  93.3 26.9 %collective-permute-start.12 = (bf16[4,512,256]{2,1,0:T(8,128)(2,1)S(1)}, bf16[4,512,256]{2,1,0:T(8,128)(2,1)}, u32[]{:S(2)}, u32[]{:S(2)}) collective-permute-start(bf16[4,512,256]{2,1,0:T(8,128)(2,1)S(1)} %all-to-all-done.1.refs_18_), channel_id=1, source_target_pairs={{0,4},{4,0},{1,5},{5,1},{2,6},{6,2},{3,7},{7,3},{8,12},{12,8},{9,1... | collective-permute-start | bytes 3145736 | tf_op jit(solution)/shard_map/ppermute | solution.py:26
  94.9 22.7 %collective-permute-start.14 = (bf16[384,1024]{1,0:T(8,128)(2,1)}, bf16[384,1024]{1,0:T(8,128)(2,1)}, u32[]{:S(2)}, u32[]{:S(2)}) collective-permute-start(bf16[384,1024]{1,0:T(8,128)(2,1)} %collective-permute-done.9.refs_8_), channel_id=1, source_target_pairs={{0,8},{8,16},{16,24},{24,0},{1,9},{9,17},{17,25},{25,1},{2,10},{10... | collective-permute-start | bytes 2359304 | tf_op jit(solution)/shard_map/ppermute | solution.py:26
  94.9 43.7 %all-to-all-start.2 = ((bf16[4,512,256]{2,1,0:T(8,128)(2,1)}), bf16[4,512,256]{2,1,0:T(8,128)(2,1)S(1)}, u32[]{:S(2)}, u32[]{:S(2)}) async-start(bf16[4,512,256]{2,1,0:T(8,128)(2,1)} %shard_map.87), calls=%async_computation.2 | async-start | bytes 2097152 | tf_op jit(solution)/shard_map/all_to_all | solution.py:72
  138.6 27.2 %collective-permute-start.19 = (bf16[512,1024]{1,0:T(8,128)(2,1)}, bf16[512,1024]{1,0:T(8,128)(2,1)}, u32[]{:S(2)}, u32[]{:S(2)}) collective-permute-start(bf16[512,1024]{1,0:T(8,128)(2,1)} %refs_4_.1), channel_id=1, source_target_pairs={{0,8},{8,16},{16,24},{24,0},{1,9},{9,17},{17,25},{25,1},{2,10},{10... | collective-permute-start | bytes 3145736 | tf_op jit(solution)/shard_map/ppermute | solution.py:26
  138.6 27.2 %collective-permute-start.18 = (bf16[4,512,256]{2,1,0:T(8,128)(2,1)S(1)}, bf16[4,512,256]{2,1,0:T(8,128)(2,1)S(1)}, u32[]{:S(2)}, u32[]{:S(2)}) collective-permute-start(bf16[4,512,256]{2,1,0:T(8,128)(2,1)S(1)} %all-to-all-done.2.refs_20_), channel_id=1, source_target_pairs={{0,4},{4,0},{1,5},{5,1},{2,6},{6,2},{3,7},{7,3},{8,12},{12,8},{9,1... | collective-permute-start | bytes 3145736 | tf_op jit(solution)/shard_map/ppermute | solution.py:26
  166.7 26.3 %collective-permute-start.21 = (bf16[512,1024]{1,0:T(8,128)(2,1)}, bf16[512,1024]{1,0:T(8,128)(2,1)}, u32[]{:S(2)}, u32[]{:S(2)}) collective-permute-start(bf16[512,1024]{1,0:T(8,128)(2,1)} %collective-permute-done.19.refs_6_), channel_id=1, source_target_pairs={{0,8},{8,16},{16,24},{24,0},{1,9},{9,17},{17,25},{25,1},{2,10},{10... | collective-permute-start | bytes 3145736 | tf_op jit(solution)/shard_map/ppermute | solution.py:26
  166.8 26.3 %collective-permute-start.22 = (bf16[512,1024]{1,0:T(8,128)(2,1)}, bf16[512,1024]{1,0:T(8,128)(2,1)}, u32[]{:S(2)}, u32[]{:S(2)}) collective-permute-start(bf16[512,1024]{1,0:T(8,128)(2,1)} %collective-permute-done.19.refs_6_), channel_id=1, source_target_pairs={{0,4},{4,0},{1,5},{5,1},{2,6},{6,2},{3,7},{7,3},{8,12},{12,8},{9,1... | collective-permute-start | bytes 3145736 | tf_op jit(solution)/shard_map/ppermute | solution.py:26
  193.1 26.1 %collective-permute-start.23 = (bf16[512,1024]{1,0:T(8,128)(2,1)}, bf16[512,1024]{1,0:T(8,128)(2,1)}, u32[]{:S(2)}, u32[]{:S(2)}) collective-permute-start(bf16[512,1024]{1,0:T(8,128)(2,1)} %collective-permute-done.21.refs_8_), channel_id=1, source_target_pairs={{0,8},{8,16},{16,24},{24,0},{1,9},{9,17},{17,25},{25,1},{2,10},{10... | collective-permute-start | bytes 3145736 | tf_op jit(solution)/shard_map/ppermute | solution.py:26
  195.1 24.6 %collective-permute-start.24 = (bf16[512,1024]{1,0:T(8,128)(2,1)}, bf16[512,1024]{1,0:T(8,128)(2,1)S(1)}, u32[]{:S(2)}, u32[]{:S(2)}) collective-permute-start(bf16[512,1024]{1,0:T(8,128)(2,1)} %collective-permute-done.21.refs_8_), channel_id=1, source_target_pairs={{0,4},{4,0},{1,5},{5,1},{2,6},{6,2},{3,7},{7,3},{8,12},{12,8},{9,1... | collective-permute-start | bytes 3145736 | tf_op jit(solution)/shard_map/ppermute | solution.py:26
  224.8 22.9 %collective-permute-start.28 = (bf16[512,1024]{1,0:T(8,128)(2,1)}, bf16[512,1024]{1,0:T(8,128)(2,1)}, u32[]{:S(2)}, u32[]{:S(2)}) collective-permute-start(bf16[512,1024]{1,0:T(8,128)(2,1)} %collective-permute-done.23.refs_10_), channel_id=1, source_target_pairs={{0,4},{4,0},{1,5},{5,1},{2,6},{6,2},{3,7},{7,3},{8,12},{12,8},{9,1... | collective-permute-start | bytes 3145736 | tf_op jit(solution)/shard_map/ppermute | solution.py:26
  237.4 31.7 %all-to-all-start.3 = ((bf16[4,512,256]{2,1,0:T(8,128)(2,1)}), bf16[4,512,256]{2,1,0:T(8,128)(2,1)S(1)}, u32[]{:S(2)}, u32[]{:S(2)}) async-start(bf16[4,512,256]{2,1,0:T(8,128)(2,1)} %shard_map.89), calls=%async_computation.3 | async-start | bytes 2097152 | tf_op jit(solution)/shard_map/all_to_all | solution.py:72
  269.1 45.6 %all-to-all-start.5 = ((bf16[4,512,256]{2,1,0:T(8,128)(2,1)}), bf16[4,512,256]{2,1,0:T(8,128)(2,1)S(1)}, u32[]{:S(2)}, u32[]{:S(2)}) async-start(bf16[4,512,256]{2,1,0:T(8,128)(2,1)} %copy-done.14), calls=%async_computation.5 | async-start | bytes 2097152 | tf_op jit(solution)/shard_map/all_to_all | solution.py:72
  284.4 27.8 %collective-permute-start.35 = (bf16[4,512,256]{2,1,0:T(8,128)(2,1)S(1)}, bf16[4,512,256]{2,1,0:T(8,128)(2,1)}, u32[]{:S(2)}, u32[]{:S(2)}) collective-permute-start(bf16[4,512,256]{2,1,0:T(8,128)(2,1)S(1)} %all-to-all-done.3.refs_8_.refs_4_), channel_id=1, source_target_pairs={{0,4},{4,0},{1,5},{5,1},{2,6},{6,2},{3,7},{7,3},{8,12},{12,8},{9,1... | collective-permute-start | bytes 3145736 | tf_op jit(solution)/shard_map/ppermute | solution.py:26
  286.1 24.0 %collective-permute-start.34 = (bf16[384,1024]{1,0:T(8,128)(2,1)}, bf16[384,1024]{1,0:T(8,128)(2,1)S(1)}, u32[]{:S(2)}, u32[]{:S(2)}) collective-permute-start(bf16[384,1024]{1,0:T(8,128)(2,1)} %shard_map.95.refs_0_), channel_id=1, source_target_pairs={{0,8},{8,16},{16,24},{24,0},{1,9},{9,17},{17,25},{25,1},{2,10},{10... | collective-permute-start | bytes 2359304 | tf_op jit(solution)/shard_map/ppermute | solution.py:26
  314.7 28.7 %all-to-all-start.4 = ((bf16[4,512,256]{2,1,0:T(8,128)(2,1)}), bf16[4,512,256]{2,1,0:T(8,128)(2,1)S(1)}, u32[]{:S(2)}, u32[]{:S(2)}) async-start(bf16[4,512,256]{2,1,0:T(8,128)(2,1)} %copy-done.13), calls=%async_computation.4 | async-start | bytes 2097152 | tf_op jit(solution)/shard_map/all_to_all | solution.py:72
  318.7 24.7 %collective-permute-start.39 = (bf16[4,512,256]{2,1,0:T(8,128)(2,1)S(1)}, bf16[4,512,256]{2,1,0:T(8,128)(2,1)}, u32[]{:S(2)}, u32[]{:S(2)}) collective-permute-start(bf16[4,512,256]{2,1,0:T(8,128)(2,1)S(1)} %all-to-all-done.5.refs_10_.refs_6_), channel_id=1, source_target_pairs={{0,4},{4,0},{1,5},{5,1},{2,6},{6,2},{3,7},{7,3},{8,12},{12,8},{9,1... | collective-permute-start | bytes 3145736 | tf_op jit(solution)/shard_map/ppermute | solution.py:26
  344.2 25.7 %collective-permute-start.41 = (bf16[4,512,256]{2,1,0:T(8,128)(2,1)S(1)}, bf16[4,512,256]{2,1,0:T(8,128)(2,1)}, u32[]{:S(2)}, u32[]{:S(2)}) collective-permute-start(bf16[4,512,256]{2,1,0:T(8,128)(2,1)S(1)} %all-to-all-done.4.refs_12_.refs_8_), channel_id=1, source_target_pairs={{0,4},{4,0},{1,5},{5,1},{2,6},{6,2},{3,7},{7,3},{8,12},{12,8},{9,1... | collective-permute-start | bytes 3145736 | tf_op jit(solution)/shard_map/ppermute | solution.py:26
  (78 other events, 1073.4 us)

commit v6 on v5

--- a/solution.py
+++ b/solution.py
@@ -87,11 +87,11 @@
     return ((x_at - x_from) % x_size) * c_size + (c_at - c_from) % c_size
 
 
-def joined_kernel(blocks, place_ref, tokens_ref, *refs):
+def joined_kernel(blocks, cuts, place_ref, tokens_ref, *refs):
     firsts, rows = refs[:blocks], refs[blocks:-5]
     out_ref, first_held, rows_held, first_came, rows_came = refs[-5:]
     parts = place_ref.shape[0] // 2
-    y_size = len(rows) // parts
+    y_size = len(rows) // cuts // parts
     deep = rows[0].shape[0]
 
     def first_arrival(r):
@@ -109,22 +109,22 @@
     total = tokens_ref[...].astype(jnp.float32)
     for n in range(len(rows)):
         rows_arrival(n).wait()
-        begin = pl.multiple_of(place_ref[parts + n % y_size] * deep, deep)
+        begin = pl.multiple_of((place_ref[parts + n // cuts % y_size] * cuts + n % cuts) * deep, deep)
         total = total + jnp.dot(
-            first_held[place_ref[n // y_size], :, pl.ds(begin, deep)], rows_held[n], preferred_element_type=jnp.float32
+            first_held[place_ref[n // cuts // y_size], :, pl.ds(begin, deep)], rows_held[n], preferred_element_type=jnp.float32
         )
     out_ref[...] = total.astype(out_ref.dtype)
 
 
 def joined(tokens, first, held, places, where):
     _, y_at, x_at, c_at = where
-    parts, y_size = len(held), len(held[0])
+    parts, y_size = len(held), len(held[0][0])
     place = [slot_of(p, x_at, c_at) for p in places] + [(y_at - j) % y_size for j in range(y_size)]
     place += [y_at * 0] * (2 * parts - len(place))
-    rows = [w for group in held for w in group]
+    rows = [half[j] for group in held for j in range(y_size) for half in group]
     anywhere = pl.BlockSpec(memory_space=pl.ANY)
     return pl.pallas_call(
-        functools.partial(joined_kernel, len(first)),
+        functools.partial(joined_kernel, len(first), len(held[0])),
         grid_spec=pltpu.PrefetchScalarGridSpec(
             num_scalar_prefetch=1,
             grid=(1,),
@@ -450,7 +450,7 @@
 
     step = Steps()
     ring, found, came, weights = [tokens], [], [], []
-    rows_ring, held = [out_weight], []
+    rows_ring, held = [jnp.split(out_weight, 1 if out_weight.shape[0] % 256 else 2)], []
     splits = [[split(block, c) for c in range(3)] for block in range(2)]
     for k in range(parts):
         if k < parts - 1:
@@ -464,24 +464,28 @@
             found[k - 1] += [others("c", piece, step) for piece in waiting]
         waiting = fresh
         if k == 0:
-            held.append(others("y", out_weight, step))
+            held.append([others("y", half, step) for half in rows_ring[0]])
         elif k <= 3:
             weights.append(others("y", after(came[k - 1], *own), step))
         if k == parts - 1:
-            rows_ring.append(step(next_along_z, after(out_weight, came[2])))
+            rows_ring.append([step(next_along_z, after(half, came[2])) for half in rows_ring[0]])
         step.then(*([splits[0][1:], splits[1] + [matrix], []] + [[]] * parts)[k])
     found[-1] += [others("c", piece, at_once) for piece in waiting]
     proj = project([sum(group, []) for group in found], weights, order)
-    near = tails(after(proj, *step.gate), 16)
+    near = tails(proj, 16)
     for k in range(1, parts - 1):
-        rows_ring.append(step(next_along_z, rows_ring[k]))
-        held.append(others("y", after(rows_ring[k], near) if k == parts - 2 else rows_ring[k], step))
-        step.then(proj)
+        rows_ring.append([next_along_z(half) for half in rows_ring[k]])
+        held.append([])
+        for half in rows_ring[k]:
+            held[k].append(others("y", after(half, near) if k == parts - 2 else half, at_once))
+        if k == 1:
+            near = after(near, *rows_ring[-1], *sum(held[1], []))
     gated = short_mix(proj, near, feat[0], short_taps, table)
-    gated = after(gated, rows_ring[-1], *held[-1])
+    gated = after(gated, *rows_ring[-1], *sum(held[-1], []))
     back = home([gated[k] for k in range(parts)], z_at)
-    held.append(others("y", after(rows_ring[-1], *held[-1]), at_once))
-    first = all_of_c([after(piece, *held[-1]) for piece in others("x", back, at_once)])
+    held.append([others("y", after(half, *sum(held[-1], [])), at_once) for half in rows_ring[-1]])
+    first = all_of_c([after(piece, *sum(held[-1], [])) for piece in others("x", back, at_once)])
+    step.then(gated)
     step.then(*step.gate, back)
     came, weights_next = [step(exchange, splits[1][0])], []
     came.append(exchange(after(splits[1][1], came[0], *first)))

time: 443 us -> 442 us (level)
    all_to_all x6, waiting for transfers between devices: 72.5 us -> 30.6 us  [exchange(): return lax.all_to_all(pieces, 'z', 0, 0, tiled=True)]
    ppermute x60 -> x67, waiting for transfers between devices: 182 us -> 221 us  [rotate(): lax.ppermute(value, axis, [(i, (i + by) % size) for i in range(size)])]
    ppermute x60 -> x67, starting transfers between devices: 48 us -> 51.3 us  [rotate(): lax.ppermute(value, axis, [(i, (i + by) % size) for i in range(size)])]
    unnamed x74 -> x80, local copies, waits for them, and re-layouts: 19 us -> 18.1 us
  transfers between devices with their start and end apart: 66 -> 73, of which waited for: 36 -> 37; matrix products, arithmetic and copies ran while one was open for 2% -> 2% of each run, Pallas kernels for 18% -> 18%
where the time goes in v6:
time: 442 us; the launch traced here: 441 us
  waiting for transfers between devices  252 us (57%)
  Pallas kernels  80.7 us (18%)
  starting transfers between devices  79 us (18%)
  local copies, waits for them, and re-layouts  26 us (6%)
    ppermute x67, waiting for transfers between devices, rotate(): lax.ppermute(value, axis, [(i, (i + by) % size) for i in range(size)])  221 us
    ppermute x67, starting transfers between devices, rotate(): lax.ppermute(value, axis, [(i, (i + by) % size) for i in range(size)])  51.3 us
    pallas_call x4, Pallas kernels, project(): pl.pallas_call(functools.partial(project_kernel, groups, kept), grid_spec...  45.8 us
    all_to_all x6, waiting for transfers between devices, exchange(): return lax.all_to_all(pieces, 'z', 0, 0, tiled=True)  30.6 us
    all_to_all x6, starting transfers between devices, exchange(): return lax.all_to_all(pieces, 'z', 0, 0, tiled=True)  27.6 us
    unnamed x80, local copies, waits for them, and re-layouts  18.1 us
    pallas_call x1, Pallas kernels, joined(): pl.pallas_call(functools.partial(joined_kernel, len(first), len(held[0]))...  11.4 us
    pallas_call x6, Pallas kernels, split_weights(): pl.pallas_call(split_kernel, grid=(parts,), in_specs=[pl.BlockSpec((1, 1,...  9.34 us
  transfers between devices with their start and end apart: 73, of which 37 were waited for; matrix products, arithmetic and copies ran while one was open for 2% of the time, Pallas kernels for 18%

profile of v6, /device:TPU:0, one launch (start us, length us, event | category | flops | bytes accessed | tf_op | source)
XLA Modules:
  0.0 440.8 jit_solution(5628763425616137406)
XLA Ops:
  24.7 6.1 %collective-permute-done.2.refs_6_ = bf16[256,1024]{1,0:T(8,128)(2,1)S(1)} collective-permute-done((bf16[256,1024]{1,0:T(8,128)(2,1)S(1)}, bf16[256,1024]{1,0:T(8,128)(2,1)S(1)}, u32[]{:S(2)}, u32[]{:S(2)}) %collective-permute-start.2) | collective-permute-done | bytes 524320 | tf_op jit(solution)/shard_map/ppermute | solution.py:26
  30.8 9.8 %collective-permute-done.3.refs_7_ = bf16[256,1024]{1,0:T(8,128)(2,1)S(1)} collective-permute-done((bf16[256,1024]{1,0:T(8,128)(2,1)S(1)}, bf16[256,1024]{1,0:T(8,128)(2,1)S(1)}, u32[]{:S(2)}, u32[]{:S(2)}) %collective-permute-start.3) | collective-permute-done | bytes 524320 | tf_op jit(solution)/shard_map/ppermute | solution.py:26
  50.0 5.1 %all-to-all-start.1 = ((bf16[4,512,256]{2,1,0:T(8,128)(2,1)}), bf16[4,512,256]{2,1,0:T(8,128)(2,1)S(1)}, u32[]{:S(2)}, u32[]{:S(2)}) async-start(bf16[4,512,256]{2,1,0:T(8,128)(2,1)} %shard_map.86), calls=%async_computation.1 | async-start | bytes 2097152 | tf_op jit(solution)/shard_map/all_to_all | solution.py:72
  73.1 21.0 %all-to-all-done.1.refs_18_ = bf16[4,512,256]{2,1,0:T(8,128)(2,1)S(1)} async-done(((bf16[4,512,256]{2,1,0:T(8,128)(2,1)}), bf16[4,512,256]{2,1,0:T(8,128)(2,1)S(1)}, u32[]{:S(2)}, u32[]{:S(2)}) %all-to-all-start.1) | async-done | bytes 1048608 | tf_op jit(solution)/shard_map/all_to_all | solution.py:72
  96.2 5.1 %all-to-all-start.2 = ((bf16[4,512,256]{2,1,0:T(8,128)(2,1)}), bf16[4,512,256]{2,1,0:T(8,128)(2,1)S(1)}, u32[]{:S(2)}, u32[]{:S(2)}) async-start(bf16[4,512,256]{2,1,0:T(8,128)(2,1)} %shard_map.87), calls=%async_computation.2 | async-start | bytes 2097152 | tf_op jit(solution)/shard_map/all_to_all | solution.py:72
  101.3 16.1 %collective-permute-done.15.refs_12_ = bf16[384,1024]{1,0:T(8,128)(2,1)} collective-permute-done((bf16[384,1024]{1,0:T(8,128)(2,1)}, bf16[384,1024]{1,0:T(8,128)(2,1)}, u32[]{:S(2)}, u32[]{:S(2)}) %collective-permute-start.15) | collective-permute-done | bytes 786464 | tf_op jit(solution)/shard_map/ppermute | solution.py:26
  121.4 16.9 %collective-permute-done.17.refs_14_ = bf16[384,1024]{1,0:T(8,128)(2,1)} collective-permute-done((bf16[384,1024]{1,0:T(8,128)(2,1)}, bf16[384,1024]{1,0:T(8,128)(2,1)}, u32[]{:S(2)}, u32[]{:S(2)}) %collective-permute-start.17) | collective-permute-done | bytes 786464 | tf_op jit(solution)/shard_map/ppermute | solution.py:26
  140.1 16.7 %collective-permute-done.21.refs_8_ = bf16[256,1024]{1,0:T(8,128)(2,1)} collective-permute-done((bf16[256,1024]{1,0:T(8,128)(2,1)}, bf16[256,1024]{1,0:T(8,128)(2,1)}, u32[]{:S(2)}, u32[]{:S(2)}) %collective-permute-start.21) | collective-permute-done | bytes 524320 | tf_op jit(solution)/shard_map/ppermute | solution.py:26
  156.8 11.2 %collective-permute-done.23.refs_9_ = bf16[256,1024]{1,0:T(8,128)(2,1)} collective-permute-done((bf16[256,1024]{1,0:T(8,128)(2,1)}, bf16[256,1024]{1,0:T(8,128)(2,1)}, u32[]{:S(2)}, u32[]{:S(2)}) %collective-permute-start.23) | collective-permute-done | bytes 524320 | tf_op jit(solution)/shard_map/ppermute | solution.py:26
  172.1 19.5 %shard_map.93 = bf16[1536,768]{1,0:T(8,128)(2,1)} custom-call(s32[6]{0:T(128)} %stack.121.order_ref, bf16[384,1024]{1,0:T(8,128)(2,1)} %tokens_ref.1, bf16[384,1024]{1,0:T(8,128)(2,1)} %copy-done.24, bf16[384,1024]{1,0:T(8,128)(2,1)} %collective-permute-done.1.refs_2_, bf16[384,1024]{1,0:T(8,128)(2,1)} %collective-permute-done.4.refs_3_, ...), custom_call_target="tpu_custom_call" | custom-call | tf_op jit(solution)/shard_map/pallas_call | solution.py:209
  210.0 8.1 %collective-permute-done.28.refs_17_ = bf16[256,1024]{1,0:T(8,128)(2,1)S(1)} collective-permute-done((bf16[256,1024]{1,0:T(8,128)(2,1)}, bf16[256,1024]{1,0:T(8,128)(2,1)S(1)}, u32[]{:S(2)}, u32[]{:S(2)}) %collective-permute-start.28) | collective-permute-done | bytes 524320 | tf_op jit(solution)/shard_map/ppermute | solution.py:26
  228.2 5.4 %collective-permute-done.32 = bf16[384,256]{1,0:T(8,128)(2,1)S(1)} collective-permute-done((bf16[384,256]{1,0:T(8,128)(2,1)S(1)}, bf16[384,256]{1,0:T(8,128)(2,1)S(1)}, u32[]{:S(2)}, u32[]{:S(2)}) %collective-permute-start.32) | collective-permute-done | bytes 196640 | tf_op jit(solution)/shard_map/ppermute | solution.py:26
  242.3 13.0 %collective-permute-done.34.refs_18_ = bf16[256,1024]{1,0:T(8,128)(2,1)S(1)} collective-permute-done((bf16[256,1024]{1,0:T(8,128)(2,1)}, bf16[256,1024]{1,0:T(8,128)(2,1)S(1)}, u32[]{:S(2)}, u32[]{:S(2)}) %collective-permute-start.34) | collective-permute-done | bytes 524320 | tf_op jit(solution)/shard_map/ppermute | solution.py:26
  255.4 8.1 %collective-permute-done.35.refs_19_ = bf16[256,1024]{1,0:T(8,128)(2,1)S(1)} collective-permute-done((bf16[256,1024]{1,0:T(8,128)(2,1)}, bf16[256,1024]{1,0:T(8,128)(2,1)S(1)}, u32[]{:S(2)}, u32[]{:S(2)}) %collective-permute-start.35) | collective-permute-done | bytes 524320 | tf_op jit(solution)/shard_map/ppermute | solution.py:26
  272.7 11.4 %shard_map.95.refs_0_ = bf16[384,1024]{1,0:T(8,128)(2,1)} custom-call(s32[8]{0:T(128)} %stack.103.place_ref, bf16[384,1024]{1,0:T(8,128)(2,1)} %tokens_ref.1, bf16[384,1024]{1,0:T(8,128)(2,1)} %copy-done.20, bf16[384,1024]{1,0:T(8,128)(2,1)} %collective-permute-done.36.refs_1_, bf16[384,1024]{1,0:T(8,128)(2,1)} %collective-permute-done.37.refs_2_, ...), custom_call_target="tpu_custom_call" | custom-call | tf_op jit(solution)/shard_map/pallas_call | solution.py:126
  288.3 22.0 %collective-permute-done.41.refs_4_ = bf16[384,1024]{1,0:T(8,128)(2,1)S(1)} collective-permute-done((bf16[384,1024]{1,0:T(8,128)(2,1)}, bf16[384,1024]{1,0:T(8,128)(2,1)S(1)}, u32[]{:S(2)}, u32[]{:S(2)}) %collective-permute-start.41) | collective-permute-done | bytes 786464 | tf_op jit(solution)/shard_map/ppermute | solution.py:26
  322.9 17.7 %collective-permute-done.45.refs_6_ = bf16[384,1024]{1,0:T(8,128)(2,1)S(1)} collective-permute-done((bf16[384,1024]{1,0:T(8,128)(2,1)}, bf16[384,1024]{1,0:T(8,128)(2,1)S(1)}, u32[]{:S(2)}, u32[]{:S(2)}) %collective-permute-start.45) | collective-permute-done | bytes 786464 | tf_op jit(solution)/shard_map/ppermute | solution.py:26
  346.0 18.3 %collective-permute-done.49.refs_0_ = bf16[384,1024]{1,0:T(8,128)(2,1)} collective-permute-done((bf16[384,1024]{1,0:T(8,128)(2,1)}, bf16[384,1024]{1,0:T(8,128)(2,1)}, u32[]{:S(2)}, u32[]{:S(2)}) %collective-permute-start.49) | collective-permute-done | bytes 786464 | tf_op jit(solution)/shard_map/ppermute | solution.py:26
  364.9 5.2 %collective-permute-done.48.refs_13_.refs_9_ = bf16[4,512,256]{2,1,0:T(8,128)(2,1)} collective-permute-done((bf16[4,512,256]{2,1,0:T(8,128)(2,1)S(1)}, bf16[4,512,256]{2,1,0:T(8,128)(2,1)}, u32[]{:S(2)}, u32[]{:S(2)}) %collective-permute-start.48) | collective-permute-done | bytes 1048608 | tf_op jit(solution)/shard_map/ppermute | solution.py:26
  370.1 11.5 %shard_map.96 = bf16[768,768]{1,0:T(8,128)(2,1)} custom-call(s32[6]{0:T(128)} %stack.121.order_ref, bf16[384,1024]{1,0:T(8,128)(2,1)} %shard_map.95.refs_0_, bf16[384,1024]{1,0:T(8,128)(2,1)} %copy-done.28, bf16[384,1024]{1,0:T(8,128)(2,1)} %copy-done.29, bf16[384,1024]{1,0:T(8,128)(2,1)} %collective-permute-done.43.refs_3_, bf16[384,1024]{1,0:T(8,128)(2,1)} %copy-done.27, ...), custom_call_target="tpu_custom_call" | custom-call | tf_op jit(solution)/shard_map/pallas_call | solution.py:209
  389.5 7.1 %shard_map.97 = bf16[384,768]{1,0:T(8,128)(2,1)S(1)} custom-call(s32[6]{0:T(128)S(1)} %copy-done.15, bf16[384,1024]{1,0:T(8,128)(2,1)} %collective-permute-done.49.refs_0_, bf16[384,1024]{1,0:T(8,128)(2,1)} %collective-permute-done.50.refs_1_, bf16[384,1024]{1,0:T(8,128)(2,1)} %collective-permute-done.51.refs_2_, ...), custom_call_target="tpu_custom_call" | custom-call | tf_op jit(solution)/shard_map/pallas_call | solution.py:209
  404.5 7.7 %shard_map.99 = bf16[384,768]{1,0:T(8,128)(2,1)S(1)} custom-call(s32[6]{0:T(128)S(1)} %copy-done.15, bf16[192,1024]{1,0:T(8,128)(2,1)S(1)} %get-tuple-element.96.refs_0_, bf16[192,1024]{1,0:T(8,128)(2,1)S(1)} %collective-permute-done.55.refs_1_, bf16[192,1024]{1,0:T(8,128)(2,1)S(1)} %collective-permute-done.56.refs_2_, ...), custom_call_target="tpu_custom_call" | custom-call | tf_op jit(solution)/shard_map/pallas_call | solution.py:209
  429.0 5.4 %collective-permute-done.66 = bf16[384,256]{1,0:T(8,128)(2,1)S(1)} collective-permute-done((bf16[384,256]{1,0:T(8,128)(2,1)S(1)}, bf16[384,256]{1,0:T(8,128)(2,1)S(1)}, u32[]{:S(2)}, u32[]{:S(2)}) %collective-permute-start.66) | collective-permute-done | bytes 196640 | tf_op jit(solution)/shard_map/ppermute | solution.py:26
  434.4 5.3 %collective-permute-done.65 = bf16[384,256]{1,0:T(8,128)(2,1)S(1)} collective-permute-done((bf16[384,256]{1,0:T(8,128)(2,1)S(1)}, bf16[384,256]{1,0:T(8,128)(2,1)S(1)}, u32[]{:S(2)}, u32[]{:S(2)}) %collective-permute-start.65) | collective-permute-done | bytes 196640 | tf_op jit(solution)/shard_map/ppermute | solution.py:26
  (266 shorter events, 165.7 us)
Async XLA Ops:
  1.2 39.5 %collective-permute-start.1 = (bf16[384,1024]{1,0:T(8,128)(2,1)}, bf16[384,1024]{1,0:T(8,128)(2,1)}, u32[]{:S(2)}, u32[]{:S(2)}) collective-permute-start(bf16[384,1024]{1,0:T(8,128)(2,1)} %tokens_ref.1), channel_id=1, source_target_pairs={{0,2},{2,0},{1,3},{3,1},{4,6},{6,4},{5,7},{7,5},{8,10},{10,8},{9,1... | collective-permute-start | bytes 2359304 | tf_op jit(solution)/shard_map/ppermute | solution.py:26
  3.7 36.9 %collective-permute-start.5 = (bf16[384,1024]{1,0:T(8,128)(2,1)}, bf16[384,1024]{1,0:T(8,128)(2,1)}, u32[]{:S(2)}, u32[]{:S(2)}) collective-permute-start(bf16[384,1024]{1,0:T(8,128)(2,1)} %tokens_ref.1), channel_id=1, source_target_pairs={{0,8},{8,16},{16,24},{24,0},{1,9},{9,17},{17,25},{25,1},{2,10},{10... | collective-permute-start | bytes 2359304 | tf_op jit(solution)/shard_map/ppermute | solution.py:26
  11.9 36.0 %all-to-all-start = ((bf16[4,512,256]{2,1,0:T(8,128)(2,1)}), bf16[4,512,256]{2,1,0:T(8,128)(2,1)S(1)}, u32[]{:S(2)}, u32[]{:S(2)}) async-start(bf16[4,512,256]{2,1,0:T(8,128)(2,1)} %shard_map.88), calls=%async_computation | async-start | bytes 2097152 | tf_op jit(solution)/shard_map/all_to_all | solution.py:72
  47.9 25.2 %collective-permute-start.8 = (bf16[4,512,256]{2,1,0:T(8,128)(2,1)S(1)}, bf16[4,512,256]{2,1,0:T(8,128)(2,1)}, u32[]{:S(2)}, u32[]{:S(2)}) collective-permute-start(bf16[4,512,256]{2,1,0:T(8,128)(2,1)S(1)} %all-to-all-done.refs_16_), channel_id=1, source_target_pairs={{0,4},{4,0},{1,5},{5,1},{2,6},{6,2},{3,7},{7,3},{8,12},{12,8},{9,1... | collective-permute-start | bytes 3145736 | tf_op jit(solution)/shard_map/ppermute | solution.py:26
  50.0 44.1 %all-to-all-start.1 = ((bf16[4,512,256]{2,1,0:T(8,128)(2,1)}), bf16[4,512,256]{2,1,0:T(8,128)(2,1)S(1)}, u32[]{:S(2)}, u32[]{:S(2)}) async-start(bf16[4,512,256]{2,1,0:T(8,128)(2,1)} %shard_map.86), calls=%async_computation.1 | async-start | bytes 2097152 | tf_op jit(solution)/shard_map/all_to_all | solution.py:72
  94.1 25.2 %collective-permute-start.13 = (bf16[4,512,256]{2,1,0:T(8,128)(2,1)S(1)}, bf16[4,512,256]{2,1,0:T(8,128)(2,1)}, u32[]{:S(2)}, u32[]{:S(2)}) collective-permute-start(bf16[4,512,256]{2,1,0:T(8,128)(2,1)S(1)} %all-to-all-done.1.refs_18_), channel_id=1, source_target_pairs={{0,4},{4,0},{1,5},{5,1},{2,6},{6,2},{3,7},{7,3},{8,12},{12,8},{9,1... | collective-permute-start | bytes 3145736 | tf_op jit(solution)/shard_map/ppermute | solution.py:26
  96.2 42.2 %all-to-all-start.2 = ((bf16[4,512,256]{2,1,0:T(8,128)(2,1)}), bf16[4,512,256]{2,1,0:T(8,128)(2,1)S(1)}, u32[]{:S(2)}, u32[]{:S(2)}) async-start(bf16[4,512,256]{2,1,0:T(8,128)(2,1)} %shard_map.87), calls=%async_computation.2 | async-start | bytes 2097152 | tf_op jit(solution)/shard_map/all_to_all | solution.py:72
  120.9 47.2 %collective-permute-start.14 = (bf16[384,1024]{1,0:T(8,128)(2,1)}, bf16[384,1024]{1,0:T(8,128)(2,1)}, u32[]{:S(2)}, u32[]{:S(2)}) collective-permute-start(bf16[384,1024]{1,0:T(8,128)(2,1)} %collective-permute-done.12.refs_10_), channel_id=1, source_target_pairs={{0,1},{1,0},{2,3},{3,2},{4,5},{5,4},{6,7},{7,6},{8,9},{9,8},{10,11... | collective-permute-start | bytes 2359304 | tf_op jit(solution)/shard_map/ppermute | solution.py:26
  138.3 30.2 %collective-permute-start.18 = (bf16[384,1024]{1,0:T(8,128)(2,1)}, bf16[384,1024]{1,0:T(8,128)(2,1)}, u32[]{:S(2)}, u32[]{:S(2)}) collective-permute-start(bf16[384,1024]{1,0:T(8,128)(2,1)} %collective-permute-done.17.refs_14_), channel_id=1, source_target_pairs={{0,1},{1,0},{2,3},{3,2},{4,5},{5,4},{6,7},{7,6},{8,9},{9,8},{10,11... | collective-permute-start | bytes 2359304 | tf_op jit(solution)/shard_map/ppermute | solution.py:26
  138.4 33.7 %collective-permute-start.19 = (bf16[4,512,256]{2,1,0:T(8,128)(2,1)S(1)}, bf16[4,512,256]{2,1,0:T(8,128)(2,1)}, u32[]{:S(2)}, u32[]{:S(2)}) collective-permute-start(bf16[4,512,256]{2,1,0:T(8,128)(2,1)S(1)} %all-to-all-done.2.refs_20_), channel_id=1, source_target_pairs={{0,4},{4,0},{1,5},{5,1},{2,6},{6,2},{3,7},{7,3},{8,12},{12,8},{9,1... | collective-permute-start | bytes 3145736 | tf_op jit(solution)/shard_map/ppermute | solution.py:26
  139.9 28.2 %collective-permute-start.23 = (bf16[256,1024]{1,0:T(8,128)(2,1)}, bf16[256,1024]{1,0:T(8,128)(2,1)}, u32[]{:S(2)}, u32[]{:S(2)}) collective-permute-start(bf16[256,1024]{1,0:T(8,128)(2,1)} %copy-done.21), channel_id=1, source_target_pairs={{0,8},{8,16},{16,24},{24,0},{1,9},{9,17},{17,25},{25,1},{2,10},{10... | collective-permute-start | bytes 1572872 | tf_op jit(solution)/shard_map/ppermute | solution.py:26
  156.8 36.3 %collective-permute-start.22 = (bf16[256,1024]{1,0:T(8,128)(2,1)}, bf16[256,1024]{1,0:T(8,128)(2,1)}, u32[]{:S(2)}, u32[]{:S(2)}) collective-permute-start(bf16[256,1024]{1,0:T(8,128)(2,1)} %collective-permute-done.21.refs_8_), channel_id=1, source_target_pairs={{0,8},{8,16},{16,24},{24,0},{1,9},{9,17},{17,25},{25,1},{2,10},{10... | collective-permute-start | bytes 1572872 | tf_op jit(solution)/shard_map/ppermute | solution.py:26
  168.1 25.1 %collective-permute-start.24 = (bf16[256,1024]{1,0:T(8,128)(2,1)}, bf16[256,1024]{1,0:T(8,128)(2,1)}, u32[]{:S(2)}, u32[]{:S(2)}) collective-permute-start(bf16[256,1024]{1,0:T(8,128)(2,1)} %collective-permute-done.23.refs_9_), channel_id=1, source_target_pairs={{0,8},{8,16},{16,24},{24,0},{1,9},{9,17},{17,25},{25,1},{2,10},{10... | collective-permute-start | bytes 1572872 | tf_op jit(solution)/shard_map/ppermute | solution.py:26
  168.1 25.7 %collective-permute-start.25 = (bf16[256,1024]{1,0:T(8,128)(2,1)}, bf16[256,1024]{1,0:T(8,128)(2,1)}, u32[]{:S(2)}, u32[]{:S(2)}) collective-permute-start(bf16[256,1024]{1,0:T(8,128)(2,1)} %collective-permute-done.21.refs_8_), channel_id=1, source_target_pairs={{0,4},{4,0},{1,5},{5,1},{2,6},{6,2},{3,7},{7,3},{8,12},{12,8},{9,1... | collective-permute-start | bytes 1572872 | tf_op jit(solution)/shard_map/ppermute | solution.py:26
  168.5 25.3 %collective-permute-start.26 = (bf16[256,1024]{1,0:T(8,128)(2,1)}, bf16[256,1024]{1,0:T(8,128)(2,1)}, u32[]{:S(2)}, u32[]{:S(2)}) collective-permute-start(bf16[256,1024]{1,0:T(8,128)(2,1)} %collective-permute-done.23.refs_9_), channel_id=1, source_target_pairs={{0,4},{4,0},{1,5},{5,1},{2,6},{6,2},{3,7},{7,3},{8,12},{12,8},{9,1... | collective-permute-start | bytes 1572872 | tf_op jit(solution)/shard_map/ppermute | solution.py:26
  193.2 24.9 %collective-permute-start.28 = (bf16[256,1024]{1,0:T(8,128)(2,1)}, bf16[256,1024]{1,0:T(8,128)(2,1)S(1)}, u32[]{:S(2)}, u32[]{:S(2)}) collective-permute-start(bf16[256,1024]{1,0:T(8,128)(2,1)} %collective-permute-done.24.refs_13_), channel_id=1, source_target_pairs={{0,8},{8,16},{16,24},{24,0},{1,9},{9,17},{17,25},{25,1},{2,10},{10... | collective-permute-start | bytes 1572872 | tf_op jit(solution)/shard_map/ppermute | solution.py:26
  233.9 29.6 %collective-permute-start.37 = (bf16[384,1024]{1,0:T(8,128)(2,1)S(1)}, bf16[384,1024]{1,0:T(8,128)(2,1)}, u32[]{:S(2)}, u32[]{:S(2)}) collective-permute-start(bf16[384,1024]{1,0:T(8,128)(2,1)S(1)} %pad_maximum_fusion.3.refs_0_), channel_id=1, source_target_pairs={{0,2},{2,0},{1,3},{3,1},{4,6},{6,4},{5,7},{7,5},{8,10},{10,8},{9,1... | collective-permute-start | bytes 2359304 | tf_op jit(solution)/shard_map/ppermute | solution.py:26
  235.5 30.8 %all-to-all-start.3 = ((bf16[4,512,256]{2,1,0:T(8,128)(2,1)}), bf16[4,512,256]{2,1,0:T(8,128)(2,1)S(1)}, u32[]{:S(2)}, u32[]{:S(2)}) async-start(bf16[4,512,256]{2,1,0:T(8,128)(2,1)} %shard_map.89), calls=%async_computation.3 | async-start | bytes 2097152 | tf_op jit(solution)/shard_map/all_to_all | solution.py:72
  267.2 47.7 %all-to-all-start.5 = ((bf16[4,512,256]{2,1,0:T(8,128)(2,1)}), bf16[4,512,256]{2,1,0:T(8,128)(2,1)S(1)}, u32[]{:S(2)}, u32[]{:S(2)}) async-start(bf16[4,512,256]{2,1,0:T(8,128)(2,1)} %copy-done.14), calls=%async_computation.5 | async-start | bytes 2097152 | tf_op jit(solution)/shard_map/all_to_all | solution.py:72
  284.2 28.2 %collective-permute-start.42 = (bf16[4,512,256]{2,1,0:T(8,128)(2,1)S(1)}, bf16[4,512,256]{2,1,0:T(8,128)(2,1)}, u32[]{:S(2)}, u32[]{:S(2)}) collective-permute-start(bf16[4,512,256]{2,1,0:T(8,128)(2,1)S(1)} %all-to-all-done.3.refs_8_.refs_4_), channel_id=1, source_target_pairs={{0,4},{4,0},{1,5},{5,1},{2,6},{6,2},{3,7},{7,3},{8,12},{12,8},{9,1... | collective-permute-start | bytes 3145736 | tf_op jit(solution)/shard_map/ppermute | solution.py:26
  285.8 24.6 %collective-permute-start.41 = (bf16[384,1024]{1,0:T(8,128)(2,1)}, bf16[384,1024]{1,0:T(8,128)(2,1)S(1)}, u32[]{:S(2)}, u32[]{:S(2)}) collective-permute-start(bf16[384,1024]{1,0:T(8,128)(2,1)} %shard_map.95.refs_0_), channel_id=1, source_target_pairs={{0,8},{8,16},{16,24},{24,0},{1,9},{9,17},{17,25},{25,1},{2,10},{10... | collective-permute-start | bytes 2359304 | tf_op jit(solution)/shard_map/ppermute | solution.py:26
  314.9 28.8 %all-to-all-start.4 = ((bf16[4,512,256]{2,1,0:T(8,128)(2,1)}), bf16[4,512,256]{2,1,0:T(8,128)(2,1)S(1)}, u32[]{:S(2)}, u32[]{:S(2)}) async-start(bf16[4,512,256]{2,1,0:T(8,128)(2,1)} %copy-done.13), calls=%async_computation.4 | async-start | bytes 2097152 | tf_op jit(solution)/shard_map/all_to_all | solution.py:72
  318.8 24.9 %collective-permute-start.46 = (bf16[4,512,256]{2,1,0:T(8,128)(2,1)S(1)}, bf16[4,512,256]{2,1,0:T(8,128)(2,1)}, u32[]{:S(2)}, u32[]{:S(2)}) collective-permute-start(bf16[4,512,256]{2,1,0:T(8,128)(2,1)S(1)} %all-to-all-done.5.refs_10_.refs_6_), channel_id=1, source_target_pairs={{0,4},{4,0},{1,5},{5,1},{2,6},{6,2},{3,7},{7,3},{8,12},{12,8},{9,1... | collective-permute-start | bytes 3145736 | tf_op jit(solution)/shard_map/ppermute | solution.py:26
  344.5 25.7 %collective-permute-start.48 = (bf16[4,512,256]{2,1,0:T(8,128)(2,1)S(1)}, bf16[4,512,256]{2,1,0:T(8,128)(2,1)}, u32[]{:S(2)}, u32[]{:S(2)}) collective-permute-start(bf16[4,512,256]{2,1,0:T(8,128)(2,1)S(1)} %all-to-all-done.4.refs_12_.refs_8_), channel_id=1, source_target_pairs={{0,4},{4,0},{1,5},{5,1},{2,6},{6,2},{3,7},{7,3},{8,12},{12,8},{9,1... | collective-permute-start | bytes 3145736 | tf_op jit(solution)/shard_map/ppermute | solution.py:26
  (88 other events, 1275.0 us)
